TPU v7x, 32 devices: a whole 2x2x4 slice. The times are simulated.
32 devices in a mesh: seq: 8 (over z, y), head: 4 (over x, core).
Axes of the slice: x: 2, y: 2, z: 4, core: 2. Of those that a mesh axis runs over, the one named last changes fastest.
Arguments:
- inputs: bfloat16 [8192, 5120], P('seq', 'head'), may hold values from -0.59765625 to 0.59765625
- gates: bfloat16 [8192, 5120], P('seq', 'head'), may hold values from -6 to 6
- write_keys: bfloat16 [8192, 128], P('seq'), may hold values from -6 to 6
- read_keys: bfloat16 [8192, 128], P('seq'), may hold values from -0.125 to 0.125
- log_decay: float32 [80, 8192], P('head', 'seq'), may hold values from -3 to 0
- skip_gain: float32 [80], P('head'), may hold values from 0.5 to 4
- doc_ids: int32 [8192], P('seq'), may hold values from 0 to 3, never falling along the last dimension, each value on 1 to 4096 neighbouring positions
- out_weight: bfloat16 [5120, 2560], P('head'), may hold values from -0.078125 to 0.078125
- grad_out: bfloat16 [8192, 2560], P(('seq', 'head')), may hold values from -6 to 6
Outputs:
- mixed_out: bfloat16 [8192, 2560], P(('seq', 'head'))
- grad_inputs: bfloat16 [8192, 5120], P('seq', 'head')
Inputs may be any that keep to these rules, and one draw needn't show every extreme that they name: `doc_ids`: document ids never fall along the sequence; every document has 1 to 4096 tokens and one has exactly 4096.
All inputs are finite; a program needn't handle non-finite values.
Results may differ from a plain program's by a relative error of at most 0.02.
Values may be sent and summed in bfloat16 or wider, within the bound.
No kernel may reach another device: no remote copies, remote signals or barrier semaphores. Data moves between devices by JAX's collectives and lax.ppermute only.
A program may use at most 128 MiB of HBM per device.

v0:
```python
import jax
import jax.numpy as jnp
from jax import lax
from jax.sharding import PartitionSpec as P

GROUP = 256


def passed_along(block, axis, distance):
    devices = range(lax.axis_size(axis))
    route = [(i - distance, i) for i in devices if i - distance in devices]
    return lax.ppermute(block, axis, route)


def prefix(shard, axis, combine, identity, reverse):
    devices, place = (lax.axis_size(axis), lax.axis_index(axis))
    everything = jax.tree.map(
        lambda part, kind: lax.all_gather(part.astype(kind), axis),
        shard,
        (jnp.bfloat16, jnp.bfloat16),
    )
    start = jax.tree.map(
        lambda part, zero: jnp.broadcast_to(jnp.asarray(zero, part.dtype), part.shape),
        shard,
        identity,
    )

    def lap(k, before):
        at = devices - 1 - k if reverse else k
        reached = at > place if reverse else at < place
        new = combine(
            before, jax.tree.map(lambda part, own: part[at].astype(own.dtype), everything, shard)
        )
        return jax.tree.map(lambda a, b: jnp.where(reached, a, b), new, before)

    return lax.fori_loop(0, devices, lap, start)


def group_terms(write_blk, read_blk, decay_blk, doc_blk, before):
    block_len = doc_blk.shape[0]
    cumul = jnp.cumsum(decay_blk, axis=1)
    positions = jnp.arange(block_len)
    causal_same = (doc_blk[:, None] == doc_blk[None, :]) & (
        positions[:, None] >= positions[None, :]
    )
    spread = jnp.where(causal_same[None], cumul[:, :, None] - cumul[:, None, :], 0.0)
    decay_matrix = jnp.where(causal_same[None], jnp.exp(spread), 0.0)
    scores = jnp.dot(read_blk, write_blk.T, preferred_element_type=jnp.float32)
    weights = (decay_matrix * scores[None]).astype(jnp.bfloat16)
    entry_w = jnp.where((doc_blk == before)[None], jnp.exp(cumul), 0.0)
    exit_w = jnp.where(
        (doc_blk == doc_blk[block_len - 1])[None], jnp.exp(cumul[:, block_len - 1 :] - cumul), 0.0
    )
    return (weights, entry_w, exit_w, entry_w[:, block_len - 1])


def combine(earlier, later):
    return (earlier[0] * later[0], later[0][:, None, None] * earlier[1] + later[1])


def shards(
    inputs, gates, write_keys, read_keys, log_decay, skip_gain, doc_ids, out_weight, grad_out
):
    tok_rows, inner = inputs.shape
    head_count = log_decay.shape[0]
    head_width = inner // head_count
    state_width = write_keys.shape[1]
    group_count = tok_rows // GROUP
    before = passed_along(doc_ids[tok_rows - 1 :] + 1, "seq", 1) - 1
    doc_blocks = doc_ids.reshape(group_count, GROUP)
    befores = jnp.concatenate([before, doc_blocks[:-1, GROUP - 1]])
    blocks_b = write_keys.reshape(group_count, GROUP, state_width)
    blocks_c = read_keys.reshape(group_count, GROUP, state_width)
    blocks_d = log_decay.reshape(head_count, group_count, GROUP).transpose(1, 0, 2)
    blocks_x = inputs.reshape(group_count, GROUP, head_count, head_width)
    weights, entry_w, exit_w, decays = jax.vmap(group_terms)(
        blocks_b, blocks_c, blocks_d, doc_blocks, befores
    )
    entry_t = jnp.swapaxes(entry_w, 1, 2)[..., None]
    exit_t = jnp.swapaxes(exit_w, 1, 2)[..., None]
    skip_full = skip_gain[:, None]
    inner_mixed = jnp.einsum(
        "khts,kshp->kthp", weights, blocks_x, preferred_element_type=jnp.float32
    )
    write_scaled = (exit_t * blocks_x.astype(jnp.float32)).astype(jnp.bfloat16)
    own_states = jnp.einsum(
        "kshp,ksn->khpn", write_scaled, blocks_b, preferred_element_type=jnp.float32
    )
    empty_state = jnp.zeros((head_count, head_width, state_width), jnp.float32)
    unit_decay = jnp.ones((head_count,), jnp.float32)
    running = empty_state
    run_decay = unit_decay
    enter_states = []
    enter_decays = []
    for position in range(group_count):
        enter_states.append(running)
        enter_decays.append(run_decay)
        running = decays[position][:, None, None] * running + own_states[position]
        run_decay = decays[position] * run_decay
    silu_gate = jax.nn.silu(gates.astype(jnp.float32))
    grad_gated = lax.dot_general(
        lax.all_gather(grad_out, "head", axis=0, tiled=True),
        out_weight,
        (((1,), (1,)), ((), ())),
        preferred_element_type=jnp.float32,
    )
    grad_mix = (grad_gated * silu_gate).astype(jnp.bfloat16)
    blocks_dy = grad_mix.reshape(group_count, GROUP, head_count, head_width)
    inner_grad = jnp.einsum(
        "khts,kthp->kshp", weights, blocks_dy, preferred_element_type=jnp.float32
    )
    grad_scaled = (entry_t * blocks_dy.astype(jnp.float32)).astype(jnp.bfloat16)
    grad_states = jnp.einsum(
        "kthp,ktn->khpn", grad_scaled, blocks_c, preferred_element_type=jnp.float32
    )
    running_back = empty_state
    back_decay = unit_decay
    exit_states = []
    exit_decays = []
    for position in reversed(range(group_count)):
        exit_states.insert(0, running_back)
        exit_decays.insert(0, back_decay)
        running_back = grad_states[position] + decays[position][:, None, None] * running_back
        back_decay = decays[position] * back_decay
    state_in = prefix((run_decay, running), "seq", combine, (unit_decay, empty_state), False)[1]
    grad_in = prefix((run_decay, running_back), "seq", combine, (unit_decay, empty_state), True)[1]
    entering = jnp.stack(
        [
            enter_states[position] + enter_decays[position][:, None, None] * state_in
            for position in range(group_count)
        ]
    ).astype(jnp.bfloat16)
    carried = (
        jnp.einsum("ktn,khpn->kthp", blocks_c, entering, preferred_element_type=jnp.float32)
        * entry_t
    )
    mixed = inner_mixed + carried + skip_full * blocks_x.astype(jnp.float32)
    gated = (mixed.reshape(tok_rows, inner) * silu_gate).astype(jnp.bfloat16)
    mixed_out = lax.psum_scatter(
        jnp.dot(gated, out_weight, preferred_element_type=jnp.float32).astype(jnp.bfloat16),
        "head",
        scatter_dimension=0,
        tiled=True,
    )
    arriving = jnp.stack(
        [
            exit_states[position] + exit_decays[position][:, None, None] * grad_in
            for position in range(group_count)
        ]
    ).astype(jnp.bfloat16)
    carried_grad = (
        jnp.einsum("ksn,khpn->kshp", blocks_b, arriving, preferred_element_type=jnp.float32)
        * exit_t
    )
    grad_inputs = (inner_grad + carried_grad + skip_full * blocks_dy.astype(jnp.float32)).astype(
        jnp.bfloat16
    )
    return (mixed_out, grad_inputs.reshape(tok_rows, inner))


def solution(mesh):
    in_specs = (
        P("seq", "head"),
        P("seq", "head"),
        P("seq", None),
        P("seq", None),
        P("head", "seq"),
        P("head"),
        P("seq"),
        P("head", None),
        P(("seq", "head"), None),
    )
    out_specs = (P(("seq", "head"), None), P("seq", "head"))
    return jax.shard_map(shards, mesh=mesh, in_specs=in_specs, out_specs=out_specs, check_vma=False)
```

profile of v0, /device:TPU:0, one launch (start us, length us, event | category | flops | bytes accessed | tf_op | source)
XLA Modules:
  0.0 245.4 jit_solution(11866888225664961716)
XLA Ops:
  9.9 6.2 %collective-permute-start = (s32[1]{0:T(128)}, s32[1]{0:T(128)}, u32[]{:S(2)}, u32[]{:S(2)}) collective-permute-start(s32[1]{0:T(128)} %add.154), channel_id=1, source_target_pairs={{0,4},{4,8},{8,12},{12,16},{16,20},{20,24},{24,28},{1,5},{5,9},{9,... | collective-permute-start | bytes 20 | tf_op jit(solution)/shard_map/ppermute | solution.py:12
  17.8 2.3 reduce-window.6
  20.9 3.4 %copy.66 = bf16[1024,1280]{0,1:T(8,128)(2,1)S(1)} copy(bf16[1024,1280]{1,0:T(8,128)(2,1)} %param.13) | data formatting | bytes 5242880 | tf_op args[0]
  24.3 3.6 %reshape.243 = bf16[4,256,20,64]{1,0,3,2:T(4,128)(2,1)} reshape(bf16[1024,1280]{0,1:T(8,128)(2,1)S(1)} %copy.66) | data formatting | bytes 5242880 | tf_op jit(solution)/shard_map/reshape | solution.py:75
  31.1 4.2 %fusion.16 = f32[4,20,64,128]{3,2,1,0:T(8,128)} fusion(bf16[4,256,128,1]{2,1,3,0:T(8,128)(2,1)S(1)} %bitcast.160, f32[4,256,20]{1,2,0:T(8,128)S(1)} %copy.71, bf16[4,256,20,64]{1,0,3,2:T(4,128)(2,1)} %reshape.243), kind=kOutput, calls=%fused_computation.31 | convolution fusion | flops 339476480 | bytes 5586944 | tf_op jit(solution)/shard_map/kshp,ksn->khpn/dot_general | solution.py:86
  35.3 17.4 %all-gather.7.cloned.1.call-done = bf16[1024,2560]{1,0:T(8,128)(2,1)} async-done(((bf16[256,2560]{1,0:T(8,128)(2,1)}), bf16[1024,2560]{1,0:T(8,128)(2,1)}) %all-gather.7.cloned.1.call-update) | async-done | bytes 5242896 | tf_op jit(solution)/shard_map/all_gather | solution.py:102
  52.7 12.1 %multiply_convert_fusion.3 = bf16[1024,1280]{1,0:T(8,128)(2,1)} fusion(bf16[1024,2560]{1,0:T(8,128)(2,1)} %all-gather.7.cloned.1.call-done, bf16[1280,2560]{1,0:T(8,128)(2,1)} %param.20, bf16[1024,1280]{1,0:T(8,128)(2,1)S(1)} %copy-done.29), kind=kOutput, calls=%fused_computation.28 | convolution fusion | flops 6720061440 | bytes 17039360 | tf_op jit(solution)/shard_map/dot_general | solution.py:101
  64.9 3.0 %copy.76 = bf16[1024,1280]{0,1:T(8,128)(2,1)S(1)} copy(bf16[1024,1280]{1,0:T(8,128)(2,1)} %multiply_convert_fusion.3) | data formatting | bytes 5242880 | tf_op jit(solution)/shard_map/convert_element_type | solution.py:107
  67.9 3.5 %reshape.245 = bf16[4,256,20,64]{1,0,3,2:T(4,128)(2,1)} reshape(bf16[1024,1280]{0,1:T(8,128)(2,1)S(1)} %copy.76) | data formatting | bytes 5242880 | tf_op jit(solution)/shard_map/reshape | solution.py:108
  71.5 2.8 %fusion.14 = f32[4,20,64,128]{3,2,1,0:T(8,128)S(1)} fusion(bf16[4,256,128,1]{2,1,3,0:T(8,128)(2,1)S(1)} %bitcast.153, f32[4,256,20]{1,2,0:T(8,128)} %copy.73, bf16[4,256,20,64]{1,0,3,2:T(4,128)(2,1)} %reshape.245), kind=kOutput, calls=%fused_computation.30 | convolution fusion | flops 339476480 | bytes 5586944 | tf_op jit(solution)/shard_map/kthp,ktn->khpn/dot_general | solution.py:113
  81.4 20.6 %all-gather = bf16[8,20,1]{1,2,0:T(2,128)(2,1)S(1)} all-gather(bf16[1,20,1]{1,2,0:T(2,128)(2,1)} %copy.68), channel_id=2, replica_groups=mesh['seq'=8,'head'=4] {'seq'}, dimensions={0}, use_global_device_ids=true | all-gather | bytes 360 | tf_op jit(solution)/shard_map/all_gather | solution.py:18
  102.1 28.3 %all-gather.5.cloned.1.call-done = bf16[8,20,64,128]{3,2,1,0:T(8,128)(2,1)} async-done(((bf16[1,20,64,128]{3,2,1,0:T(8,128)(2,1)}), bf16[8,20,64,128]{3,2,1,0:T(8,128)(2,1)}) %all-gather.5.cloned.1.call-update) | async-done | bytes 2621456 | tf_op jit(solution)/shard_map/all_gather | solution.py:18
  130.5 9.6 %while.30 = (s32[]{:T(128)}, f32[20,64,128]{2,1,0:T(8,128)S(1)}, s32[]{:T(128)}, bf16[8,20]{1,0:T(8,128)(2,1)S(1)}, bf16[8,20,64,128]{3,2,1,0:T(8,128)(2,1)}, /*index=5*/s32[]{:T(128)}, s32[]{:T(128)}) while((s32[]{:T(128)}, f32[20,64,128]{2,1,0:T(8,128)S(1)}, s32[]{:T(128)}, bf16[8,20]{1,0:T(8,128)(2,1)S(1)}, ...), condition=%wide.region_3.4_spmd.clone, body=%wide.region_2.3_spmd.clone.sunk | while | flops 819224 | bytes 1638713 | solution.py:36
  143.2 6.3 %fusion.5 = f32[4,256,20,64]{1,3,2,0:T(8,128)S(1)} fusion(f32[4,20,64,256]{3,2,1,0:T(8,128)S(1)} %fusion.24, f32[20]{0:T(128)S(1)} %copy-done.30, f32[4,256,20]{1,2,0:T(8,128)S(1)} %copy-done.18, f32[4,256,256]{2,1,0:T(8,128)S(1)} %copy-done.5, f32[4,20,256]{2,1,0:T(8,128)S(1)} %copy-done.16, pred[4,256,256]{2,1,0:T(8,128)(4,1)S(1)} %copy-done.12, ...), kind=kOutput, calls=%fused_computation.17 | convolution fusion | flops 703856640 | bytes 14581840 | tf_op jit(solution)/shard_map/khts,kshp->kthp/dot_general | solution.py:82
  149.5 3.9 %copy.74 = f32[4,256,20,64]{1,0,3,2:T(4,128)S(1)} copy(f32[4,256,20,64]{1,3,2,0:T(8,128)S(1)} %fusion.5) | data formatting | bytes 10485760 | tf_op jit(solution)/shard_map/add | solution.py:137
  153.4 3.8 %copy.84 = f32[160,8,4,256]{3,1,2,0:T(8,128)} copy(f32[160,8,4,256]{3,2,1,0:T(4,128)S(1)} %bitcast.155) | data formatting | bytes 10485760
  157.2 6.0 %copy.75 = f32[1024,1280]{1,0:T(8,128)} copy(f32[1024,1280]{0,1:T(8,128)} %bitcast.156) | data formatting | bytes 10485760 | tf_op jit(solution)/shard_map/reshape | solution.py:138
  163.2 12.9 %convolution_convert_fusion = bf16[1024,2560]{1,0:T(8,128)(2,1)} fusion(bf16[1280,2560]{1,0:T(8,128)(2,1)} %param.20, f32[1024,1280]{1,0:T(8,128)} %copy.75, bf16[1024,1280]{1,0:T(8,128)(2,1)} %param.14), kind=kOutput, calls=%fused_computation.15 | convolution fusion | flops 6722682880 | bytes 19660800 | tf_op jit(solution)/shard_map/dot_general | solution.py:140
  176.2 9.7 %all-gather.9.cloned.1.call-done = bf16[8,20,64,128]{3,2,1,0:T(8,128)(2,1)} async-done(((bf16[1,20,64,128]{3,2,1,0:T(8,128)(2,1)}), bf16[8,20,64,128]{3,2,1,0:T(8,128)(2,1)}) %all-gather.9.cloned.1.call-update) | async-done | bytes 2621456 | tf_op jit(solution)/shard_map/all_gather | solution.py:18
  185.9 15.0 %while.31 = (s32[]{:T(128)}, f32[20,64,128]{2,1,0:T(8,128)S(1)}, s32[]{:T(128)}, bf16[8,20]{1,0:T(8,128)(2,1)}, bf16[8,20,64,128]{3,2,1,0:T(8,128)(2,1)}, /*index=5*/s32[]{:T(128)}, s32[]{:T(128)}, s32[]{:T(128)}, s32[]{:T(128)}) while((s32[]{:T(128)}, f32[20,64,128]{2,1,0:T(8,128)S(1)}, s32[]{:T(128)}, bf16[8,20]{1,0:T(8,128)(2,1)}, ...), condition=%wide.region_6.7_spmd.clone, body=%wide.region_5.6_spmd.clone.sunk | while | flops 819228 | bytes 1638775 | solution.py:36
  203.2 7.1 %fusion.11 = bf16[4,256,20,64]{1,3,2,0:T(8,128)(2,1)S(1)} fusion(f32[4,20,64,256]{3,2,1,0:T(8,128)S(1)} %fusion.32, f32[20]{0:T(128)S(1)} %copy-done.31, f32[4,256,20]{1,2,0:T(8,128)S(1)} %copy-done.15, f32[4,256,256]{2,1,0:T(8,128)S(1)} %copy-done.6, f32[4,20,256]{2,1,0:T(8,128)S(1)} %copy-done.17, pred[4,256,256]{2,1,0:T(8,128)(4,1)S(1)} %copy-done.13, ...), kind=kOutput, calls=%fused_computation.23 | convolution fusion | flops 705167360 | bytes 11960400 | tf_op jit(solution)/shard_map/khts,kthp->kshp/dot_general | solution.py:109
  210.3 2.3 copy.79
  213.2 2.7 %copy.80 = bf16[1024,1280]{1,0:T(8,128)(2,1)} copy(bf16[1024,1280]{0,1:T(8,128)(2,1)S(1)} %bitcast.158) | data formatting | bytes 5242880
  215.9 23.0 %reduce-scatter.2.cloned.1.call-done = bf16[256,2560]{1,0:T(8,128)(2,1)} async-done(((bf16[1024,2560]{1,0:T(8,128)(2,1)}), bf16[256,2560]{1,0:T(8,128)(2,1)}) %reduce-scatter.2.cloned.1.call-update) | async-done | bytes 1310736 | tf_op jit(solution)/shard_map/reduce_scatter | solution.py:139
  (145 shorter events, 43.8 us)
Async XLA Ops:
  7.2 64.3 %copy-start = (bf16[1024,128]{1,0:T(8,128)(2,1)S(1)}, bf16[1024,128]{1,0:T(8,128)(2,1)}, u32[]{:S(2)}) copy-start(bf16[1024,128]{1,0:T(8,128)(2,1)} %param.16) | copy-start | bytes 786436
  7.2 45.6 %all-gather.7.cloned.1.call-start = ((), (), s32[]{:S(2)}) async-start(), calls=%async_computation.3 | async-start | bytes 6553600 | tf_op jit(solution)/shard_map/all_gather | solution.py:102
  7.9 122.6 %all-gather.5.cloned.1.call-start = ((), (), s32[]{:S(2)}) async-start(), calls=%async_computation.1 | async-start | bytes 2949120 | tf_op jit(solution)/shard_map/all_gather | solution.py:18
  9.9 18.3 %collective-permute-start = (s32[1]{0:T(128)}, s32[1]{0:T(128)}, u32[]{:S(2)}, u32[]{:S(2)}) collective-permute-start(s32[1]{0:T(128)} %add.154), channel_id=1, source_target_pairs={{0,4},{4,8},{8,12},{12,16},{16,20},{20,24},{24,28},{1,5},{5,9},{9,... | collective-permute-start | bytes 20 | tf_op jit(solution)/shard_map/ppermute | solution.py:12
  20.6 8.5 %copy-start.9 = (f32[4,20,256]{2,0,1:T(4,128)}, f32[4,20,256]{2,0,1:T(4,128)S(1)}, u32[]{:S(2)}) copy-start(f32[4,20,256]{2,0,1:T(4,128)S(1)} %reduce_window_sum.24) | copy-start | bytes 245764
  20.9 10.2 %copy-start.7 = (bf16[1024,128]{1,0:T(8,128)(2,1)S(1)}, bf16[1024,128]{1,0:T(8,128)(2,1)}, u32[]{:S(2)}) copy-start(bf16[1024,128]{1,0:T(8,128)(2,1)} %param.15) | copy-start | bytes 786436
  27.8 24.9 %copy-start.29 = (bf16[1024,1280]{1,0:T(8,128)(2,1)S(1)}, bf16[1024,1280]{1,0:T(8,128)(2,1)}, u32[]{:S(2)}) copy-start(bf16[1024,1280]{1,0:T(8,128)(2,1)} %param.14) | copy-start | bytes 7864324
  29.3 35.6 %copy-start.14 = (f32[4,256,20]{1,2,0:T(8,128)}, f32[4,256,20]{1,2,0:T(8,128)S(1)}, u32[]{:S(2)}) copy-start(f32[4,256,20]{1,2,0:T(8,128)S(1)} %copy.71) | copy-start | bytes 245764
  30.5 34.4 %copy-start.23 = (f32[20]{0:T(128)}, f32[20]{0:T(128)S(1)}, u32[]{:S(2)}) copy-start(f32[20]{0:T(128)S(1)} %get-tuple-element.283) | copy-start | bytes 244
  30.5 43.7 %copy-start.19 = (f32[20]{0:T(128)}, f32[20]{0:T(128)S(1)}, u32[]{:S(2)}) copy-start(f32[20]{0:T(128)S(1)} %get-tuple-element.285) | copy-start | bytes 244
  30.5 43.7 %copy-start.21 = (f32[20]{0:T(128)}, f32[20]{0:T(128)S(1)}, u32[]{:S(2)}) copy-start(f32[20]{0:T(128)S(1)} %get-tuple-element.282) | copy-start | bytes 244
  75.6 110.3 %all-gather.9.cloned.1.call-start = ((), (), s32[]{:S(2)}) async-start(), calls=%async_computation.4 | async-start | bytes 2949120 | tf_op jit(solution)/shard_map/all_gather | solution.py:18
  102.1 136.8 %reduce-scatter.2.cloned.1.call-start = ((), (), s32[]{:S(2)}) async-start(), calls=%async_computation.2 | async-start | bytes 6553600 | tf_op jit(solution)/shard_map/reduce_scatter | solution.py:139
  140.0 3.1 %copy-start.28 = (bf16[8,20]{1,0:T(8,128)(2,1)}, bf16[8,20]{1,0:T(8,128)(2,1)S(1)}, u32[]{:S(2)}) copy-start(bf16[8,20]{1,0:T(8,128)(2,1)S(1)} %get-tuple-element.452) | copy-start | bytes 964
  140.1 3.1 %copy-start.4 = (bf16[4,256,20,64]{1,0,3,2:T(4,128)(2,1)S(1)}, bf16[4,256,20,64]{1,0,3,2:T(4,128)(2,1)}, u32[]{:S(2)}) copy-start(bf16[4,256,20,64]{1,0,3,2:T(4,128)(2,1)} %reshape.243) | copy-start | bytes 7864324
  140.1 3.1 %copy-start.5 = (f32[4,256,256]{2,1,0:T(8,128)S(1)}, f32[4,256,256]{2,1,0:T(8,128)}, u32[]{:S(2)}) copy-start(f32[4,256,256]{2,1,0:T(8,128)} %fusion.61) | copy-start | bytes 3145732
  140.1 3.1 %copy-start.12 = (pred[4,256,256]{2,1,0:T(8,128)(4,1)S(1)}, pred[4,256,256]{2,1,0:T(8,128)(4,1)}, u32[]{:S(2)}) copy-start(pred[4,256,256]{2,1,0:T(8,128)(4,1)} %compare_and_fusion) | copy-start | bytes 786436
  140.1 3.1 %copy-start.16 = (f32[4,20,256]{2,1,0:T(8,128)S(1)}, f32[4,20,256]{2,1,0:T(8,128)}, u32[]{:S(2)}) copy-start(f32[4,20,256]{2,1,0:T(8,128)} %copy.64) | copy-start | bytes 245764
  140.1 3.1 %copy-start.18 = (f32[4,256,20]{1,2,0:T(8,128)S(1)}, f32[4,256,20]{1,2,0:T(8,128)}, u32[]{:S(2)}) copy-start(f32[4,256,20]{1,2,0:T(8,128)} %copy.73) | copy-start | bytes 245764
  176.2 24.7 %copy-start.20 = (f32[20]{0:T(128)S(1)}, f32[20]{0:T(128)}, u32[]{:S(2)}) copy-start(f32[20]{0:T(128)} %copy-done.19) | copy-start | bytes 244
  176.2 24.7 %copy-start.22 = (f32[20]{0:T(128)S(1)}, f32[20]{0:T(128)}, u32[]{:S(2)}) copy-start(f32[20]{0:T(128)} %copy-done.21) | copy-start | bytes 244
  176.2 24.7 %copy-start.26 = (f32[20]{0:T(128)S(1)}, f32[20]{0:T(128)}, u32[]{:S(2)}) copy-start(f32[20]{0:T(128)} %get-tuple-element.327) | copy-start | bytes 244
  185.9 16.3 %copy-start.8 = (bf16[1024,128]{1,0:T(8,128)(2,1)S(1)}, bf16[1024,128]{1,0:T(8,128)(2,1)}, u32[]{:S(2)}) copy-start(bf16[1024,128]{1,0:T(8,128)(2,1)} %param.15) | copy-start | bytes 786436
  212.6 26.3 %copy-start.1 = (bf16[1024,128]{1,0:T(8,128)(2,1)S(1)}, bf16[1024,128]{1,0:T(8,128)(2,1)}, u32[]{:S(2)}) copy-start(bf16[1024,128]{1,0:T(8,128)(2,1)} %param.16) | copy-start | bytes 786436
  (13 other events, 29.7 us)
Sparse Core Ops, SparseCore 0:
  9.6 43.1 all-gather.6
  75.8 54.6 all-gather.4
  132.7 53.2 all-gather.8
  188.9 49.9 reduce-scatter.1
where the time goes:
time: 247 us; the launch traced here: 245 us
  waiting for transfers between devices  79.2 us (32%)
  matrix products  49.4 us (20%)
  local copies, waits for them, and re-layouts  39.5 us (16%)
  other arithmetic  34 us (14%)
  blocking collectives  20.6 us (8%)
  between operations  15.8 us (6%)
  starting transfers between devices  6.32 us (3%)
    all_gather x2, waiting for transfers between devices, prefix(): lax.all_gather(part.astype(kind), axis)  38 us
    reduce_scatter x1, waiting for transfers between devices, shards(): lax.psum_scatter(jnp.dot(gated, out_weight, preferred_element_type=jnp.fl...  23 us
    all_gather x1, blocking collectives, prefix(): lax.all_gather(part.astype(kind), axis)  20.6 us
    select_n x16, other arithmetic, lap(): return jax.tree.map(lambda a, b: jnp.where(reached, a, b), new, before)  18.3 us
    all_gather x1, waiting for transfers between devices, shards(): lax.all_gather(grad_out, 'head', axis=0, tiled=True)  17.4 us
    dot_general x1, matrix products, shards(): jnp.dot(gated, out_weight, preferred_element_type=jnp.float32)  12.9 us
    dot_general x1, matrix products, shards(): lax.dot_general(lax.all_gather(grad_out, 'head', axis=0, tiled=True), out...  12.1 us
    unnamed x69, local copies, waits for them, and re-layouts  10.7 us
  transfers between devices with their start and end apart: 5, of which 4 were waited for; matrix products, arithmetic and copies ran while one was open for 41% of the time, Pallas kernels for 0%

commit v1 on v0

v1 whole, which is shorter than its diff:
```python
import functools
import math

import jax
import jax.numpy as jnp
from jax import lax
from jax.experimental import pallas as pl
from jax.experimental.pallas import tpu as pltpu
from jax.sharding import PartitionSpec as P

GROUP = 256
LANES = 128
LOG2E = math.log2(math.e)
F32 = jnp.float32
BF16 = jnp.bfloat16
NT = (((1,), (1,)), ((), ()))
TN = (((0,), (0,)), ((), ()))
VMEM_LIMIT = 56 * 2**20


def dot(a, b, dims=(((1,), (0,)), ((), ()))):
    return lax.dot_general(a, b, dims, preferred_element_type=F32)


def params():
    return pltpu.CompilerParams(vmem_limit_bytes=VMEM_LIMIT)


def cost(flops, nbytes):
    return pl.CostEstimate(flops=int(flops), bytes_accessed=int(nbytes), transcendentals=0)


def lanes_exact(row, spread):
    high = row.astype(BF16)
    low = (row - high.astype(F32)).astype(BF16)
    return dot(high, spread) + dot(low, spread)


def silu(gates):
    v = gates.astype(F32)
    return v / (1.0 + jnp.exp(-v))


def state_kernel(
    heads, place, x_ref, b_ref, ld_ref, doc_ref, spread_ref,
    ccol_ref, crow_ref, local_ref, keep_ref, send_ref, pre_ref, blk_ref,
    padded, running, total, last_doc,
):
    k = pl.program_id(0)
    half = running.shape[0] // 2

    @pl.when(k == 0)
    def _():
        padded[...] = jnp.zeros_like(padded)
        running[...] = jnp.zeros_like(running)
        total[...] = jnp.zeros_like(total)
        last_doc[...] = jnp.zeros_like(last_doc)
        pre_ref[...] = jnp.zeros_like(pre_ref)
        blk_ref[...] = jnp.zeros_like(blk_ref)

    padded[0:heads, :] = ld_ref[...]
    upto = lax.broadcasted_iota(jnp.int32, (GROUP, GROUP), 1) <= lax.broadcasted_iota(
        jnp.int32, (GROUP, GROUP), 0
    )
    cum = lax.dot_general(
        padded[...], upto.astype(F32), NT, precision=lax.Precision.HIGHEST,
        preferred_element_type=F32,
    ) * LOG2E
    rows = lax.broadcasted_iota(jnp.int32, (LANES, GROUP), 0)
    cum = jnp.where(rows == LANES - 1, doc_ref[...].astype(F32), cum)
    crow_ref[...] = cum[0 : crow_ref.shape[0]]
    ccol = cum.T
    ccol_ref[...] = ccol
    docs = ccol[:, LANES - 1 :]
    end = ccol[GROUP - 1 :]
    end_doc = end[:, LANES - 1 :]
    exit_w = jnp.where(docs == end_doc, jnp.exp2(jnp.minimum(end - ccol, 0.0)), 0.0).astype(BF16)
    spread = spread_ref[...]
    scaled = (dot(exit_w, spread) * x_ref[...].astype(F32)).astype(BF16)
    own = dot(b_ref[...], scaled, TN)
    same = end_doc == last_doc[0:1, 0:1]
    block_decay = jnp.where(same, jnp.exp2(end), 0.0)
    prefix = jnp.exp2(total[0:1])
    stacked = jnp.concatenate(
        [block_decay, prefix, jnp.exp2(total[0:1] + end), jnp.zeros((5, LANES), F32)], axis=0
    )
    wide = lanes_exact(stacked, spread)
    sub = lax.broadcasted_iota(jnp.int32, blk_ref.shape, 0)
    blk_ref[...] = jnp.where(sub == k, wide[0:1], blk_ref[...])
    pre_ref[...] = jnp.where(
        sub == k, wide[1:2], jnp.where(sub == k + 1, wide[2:3], pre_ref[...])
    )
    local_ref[0] = running[...].astype(BF16)
    running[...] = wide[0:1] * running[...] + own
    total[...] = total[...] + end
    last_doc[...] = jnp.broadcast_to(end_doc, last_doc.shape)

    @pl.when(k == pl.num_programs(0) - 1)
    def _():
        at = place[0]
        keep_ref[...] = running[pl.ds(at * half, half), :].astype(BF16)
        send_ref[...] = running[pl.ds((1 - at) * half, half), :].astype(BF16)


def local_states(inputs, write_keys, log_decay, docs_row, spread, side):
    tokens, inner = inputs.shape
    heads = log_decay.shape[0]
    n = write_keys.shape[1]
    blocks = tokens // GROUP
    head_rows = -(-heads // 8) * 8
    pre_rows = -(-(blocks + 1) // 8) * 8
    return pl.pallas_call(
        lambda place, *refs: state_kernel(heads, place, *refs),
        grid_spec=pltpu.PrefetchScalarGridSpec(
            num_scalar_prefetch=1,
            grid=(blocks,),
            in_specs=[
                pl.BlockSpec((GROUP, inner), lambda k, s: (k, 0)),
                pl.BlockSpec((GROUP, n), lambda k, s: (k, 0)),
                pl.BlockSpec((heads, GROUP), lambda k, s: (0, k)),
                pl.BlockSpec((1, GROUP), lambda k, s: (0, k)),
                pl.BlockSpec((LANES, inner), lambda k, s: (0, 0)),
            ],
            out_specs=[
                pl.BlockSpec((GROUP, LANES), lambda k, s: (k, 0)),
                pl.BlockSpec((head_rows, GROUP), lambda k, s: (0, k)),
                pl.BlockSpec((1, n, inner), lambda k, s: (k, 0, 0)),
                pl.BlockSpec((n // 2, inner), lambda k, s: (0, 0)),
                pl.BlockSpec((n // 2, inner), lambda k, s: (0, 0)),
                pl.BlockSpec((pre_rows, inner), lambda k, s: (0, 0)),
                pl.BlockSpec((pre_rows, inner), lambda k, s: (0, 0)),
            ],
            scratch_shapes=[
                pltpu.VMEM((LANES, GROUP), F32),
                pltpu.VMEM((n, inner), F32),
                pltpu.VMEM((8, LANES), F32),
                pltpu.VMEM((8, LANES), F32),
            ],
        ),
        out_shape=[
            jax.ShapeDtypeStruct((tokens, LANES), F32),
            jax.ShapeDtypeStruct((head_rows, tokens), F32),
            jax.ShapeDtypeStruct((blocks, n, inner), BF16),
            jax.ShapeDtypeStruct((n // 2, inner), BF16),
            jax.ShapeDtypeStruct((n // 2, inner), BF16),
            jax.ShapeDtypeStruct((pre_rows, inner), F32),
            jax.ShapeDtypeStruct((pre_rows, inner), F32),
        ],
        compiler_params=params(),
        cost_estimate=cost(4 * tokens * inner * n, tokens * inner * 2 * 3),
        name="local_states",
    )(side, inputs, write_keys, log_decay, docs_row, spread)


def inside_kernel(
    heads, width, backward, x_ref, b_ref, c_ref, ccol_ref, crow_ref, doc_ref, skip_ref, out_ref
):
    half = GROUP // 2
    col = ccol_ref[...]
    docs_col = col[:, LANES - 1 :]
    docs_row = doc_ref[...].astype(F32)
    rows = lax.broadcasted_iota(jnp.int32, (GROUP, GROUP), 0)
    cols = lax.broadcasted_iota(jnp.int32, (GROUP, GROUP), 1)
    if backward:
        scores = dot(b_ref[...], c_ref[...], NT)
        allowed = (docs_col == docs_row) & (rows <= cols)
    else:
        scores = dot(c_ref[...], b_ref[...], NT)
        allowed = (docs_col == docs_row) & (cols <= rows)
    scores = jnp.where(allowed, scores, 0.0)
    lane = lax.broadcasted_iota(jnp.int32, (GROUP, LANES), 1)
    per = LANES // width
    for j in range(heads // per):
        cut = slice(j * LANES, (j + 1) * LANES)
        x = x_ref[:, cut]
        base = skip_ref[:, cut] * x.astype(F32)
        top, bottom = base[:half], base[half:]
        for i in range(per):
            h = j * per + i
            own = jnp.where(lane // width == i, x, jnp.zeros_like(x))
            at_row = crow_ref[h : h + 1, :]
            at_col = col[:, h : h + 1]

            def weights(r, c):
                if backward:
                    gap = at_row[:, c] - at_col[r]
                else:
                    gap = at_col[r] - at_row[:, c]
                return (jnp.exp2(jnp.minimum(gap, 0.0)) * scores[r, c]).astype(BF16)

            low, high, both = slice(0, half), slice(half, GROUP), slice(0, GROUP)
            if backward:
                top = top + dot(weights(low, both), own)
                bottom = bottom + dot(weights(high, high), own[half:])
            else:
                top = top + dot(weights(low, low), own[:half])
                bottom = bottom + dot(weights(high, both), own)
        out_ref[:half, cut] = top.astype(BF16)
        out_ref[half:, cut] = bottom.astype(BF16)


def inside(x, write_keys, read_keys, ccol, crow, docs_row, skip, heads, backward):
    tokens, inner = x.shape
    n = write_keys.shape[1]
    head_rows = crow.shape[0]
    return pl.pallas_call(
        functools.partial(inside_kernel, heads, inner // heads, backward),
        grid=(tokens // GROUP,),
        in_specs=[
            pl.BlockSpec((GROUP, inner), lambda k: (k, 0)),
            pl.BlockSpec((GROUP, n), lambda k: (k, 0)),
            pl.BlockSpec((GROUP, n), lambda k: (k, 0)),
            pl.BlockSpec((GROUP, LANES), lambda k: (k, 0)),
            pl.BlockSpec((head_rows, GROUP), lambda k: (0, k)),
            pl.BlockSpec((1, GROUP), lambda k: (0, k)),
            pl.BlockSpec((1, inner), lambda k: (0, 0)),
        ],
        out_specs=pl.BlockSpec((GROUP, inner), lambda k: (k, 0)),
        out_shape=jax.ShapeDtypeStruct((tokens, inner), BF16),
        compiler_params=params(),
        cost_estimate=cost(8 * tokens * inner * GROUP, tokens * inner * 4),
        name="inside_backward" if backward else "inside_forward",
    )(x, write_keys, read_keys, ccol, crow, docs_row, skip)


def entry_wide(ccol, prior, spread):
    docs = ccol[:, LANES - 1 :]
    entry = jnp.where(docs == prior, jnp.exp2(ccol), 0.0).astype(BF16)
    return dot(entry, spread)


def tail_kernel(count, chunk, blocks, scalars, *refs):
    (mixed_refs, gate_refs, read_refs, ccol_refs, local_refs), rest = (
        [refs[i * count : (i + 1) * count] for i in range(5)],
        refs[5 * count :],
    )
    keep_ref, other_ref, pre_ref, spread_ref, w_ref = rest[:5]
    outs, gated = rest[5 : 5 + count], rest[5 + count]
    half = keep_ref.shape[0]

    @pl.when(pl.program_id(0) == 0)
    def _():
        before, side = scalars[0], scalars[1]
        at_low = side == 0
        keep, other = keep_ref[...].astype(F32), other_ref[...].astype(F32)
        state = jnp.concatenate(
            [jnp.where(at_low, keep, other), jnp.where(at_low, other, keep)], axis=0
        )
        sub = lax.broadcasted_iota(jnp.int32, pre_ref.shape, 0)
        for i in range(count):
            k = scalars[2 + blocks + i] * chunk // GROUP
            prior = jnp.where(k == 0, before, scalars[1 + jnp.maximum(k, 1)])
            live = (prior == before).astype(F32)
            decay = jnp.sum(jnp.where(sub == k, pre_ref[...], 0.0), axis=0, keepdims=True) * live
            entering = (local_refs[i][0].astype(F32) + decay * state).astype(BF16)
            carried = dot(read_refs[i][...], entering) * entry_wide(
                ccol_refs[i][...], prior.astype(F32), spread_ref[...]
            )
            gated[i] = (
                (mixed_refs[i][...].astype(F32) + carried) * silu(gate_refs[i][...])
            ).astype(BF16)

    for i in range(count):
        outs[i][...] = dot(gated[i], w_ref[...]).astype(BF16)


def forward_tail(
    chunk, scalars, count, mixed, gates, read_keys, ccol, local, keep, other, pre, spread, out_weight
):
    inner, width = out_weight.shape
    n = read_keys.shape[1]
    blocks = local.shape[0]
    tile = 512 if width % 512 == 0 else width
    pick = lambda i: (lambda j, s: (s[2 + blocks + i], 0))
    fixed = lambda shape: pl.BlockSpec(shape, lambda j, s: (0, 0))
    each = lambda shape: [pl.BlockSpec(shape, pick(i)) for i in range(count)]
    in_specs = (
        each((chunk, inner)) + each((chunk, inner)) + each((chunk, n)) + each((chunk, LANES))
        + [
            pl.BlockSpec(
                (1, n, inner), lambda j, s, i=i: (s[2 + blocks + i] * chunk // GROUP, 0, 0)
            )
            for i in range(count)
        ]
        + [
            fixed(keep.shape), fixed(other.shape), fixed(pre.shape), fixed(spread.shape),
            pl.BlockSpec((inner, tile), lambda j, s: (0, j)),
        ]
    )
    return pl.pallas_call(
        functools.partial(tail_kernel, count, chunk, blocks),
        grid_spec=pltpu.PrefetchScalarGridSpec(
            num_scalar_prefetch=1,
            grid=(width // tile,),
            in_specs=in_specs,
            out_specs=[pl.BlockSpec((chunk, tile), lambda j, s: (0, j))] * count,
            scratch_shapes=[pltpu.VMEM((count, chunk, inner), BF16)],
        ),
        out_shape=[jax.ShapeDtypeStruct((chunk, width), BF16)] * count,
        compiler_params=params(),
        cost_estimate=cost(
            2 * count * chunk * inner * width, inner * width * 2 + count * chunk * (inner * 4 + width * 2)
        ),
        name="forward_tail",
    )(
        scalars, *[mixed] * count, *[gates] * count, *[read_keys] * count, *[ccol] * count,
        *[local] * count, keep, other, pre, spread, out_weight,
    )


def grad_kernel(count, chunk, blocks, first, final, scalars, *refs):
    go_refs, gate_refs, read_refs, ccol_refs = [refs[i * count : (i + 1) * count] for i in range(4)]
    rest = list(refs[4 * count :])
    pre_ref, spread_ref, w_ref = rest[:3]
    rest = rest[3:]
    if not first:
        sum_in, rest = rest[0], rest[1:]
    mix_refs, state_refs, rest = rest[:count], rest[count : 2 * count], rest[2 * count :]
    before, side = scalars[0], scalars[1]
    sub = lax.broadcasted_iota(jnp.int32, pre_ref.shape, 0)
    summed = None if first else sum_in[...]
    for i in range(count):
        k = scalars[2 + blocks + i] * chunk // GROUP
        prior = jnp.where(k == 0, before, scalars[1 + jnp.maximum(k, 1)])
        live = (prior == before).astype(F32)
        mix = (dot(go_refs[i][...], w_ref[...], NT) * silu(gate_refs[i][...])).astype(BF16)
        mix_refs[i][...] = mix
        scaled = (
            entry_wide(ccol_refs[i][...], prior.astype(F32), spread_ref[...]) * mix.astype(F32)
        ).astype(BF16)
        state = dot(read_refs[i][...], scaled, TN)
        state_refs[i][...] = state.astype(BF16)
        decay = jnp.sum(jnp.where(sub == k, pre_ref[...], 0.0), axis=0, keepdims=True) * live
        part = decay * state
        summed = part if summed is None else summed + part
    if final:
        half = summed.shape[0] // 2
        at_low = side == 0
        rest[0][...] = jnp.where(at_low, summed[:half], summed[half:]).astype(BF16)
        rest[1][...] = jnp.where(at_low, summed[half:], summed[:half]).astype(BF16)
    else:
        rest[0][...] = summed


def grad_chunks(
    chunk, scalars, blocks, arrived, gates, read_keys, ccol, pre, spread, out_weight, summed, final
):
    count = len(arrived)
    inner, width = out_weight.shape
    n = read_keys.shape[1]
    tile = 256 if inner % 256 == 0 else LANES
    first = summed is None
    tiled = lambda rows: pl.BlockSpec((rows, tile), lambda j, s: (0, j))
    in_specs = (
        [pl.BlockSpec((chunk, width), lambda j, s: (0, 0))] * count
        + [pl.BlockSpec((chunk, tile), lambda j, s, i=i: (s[2 + blocks + i], j)) for i in range(count)]
        + [pl.BlockSpec((chunk, n), lambda j, s, i=i: (s[2 + blocks + i], 0)) for i in range(count)]
        + [pl.BlockSpec((chunk, LANES), lambda j, s, i=i: (s[2 + blocks + i], 0)) for i in range(count)]
        + [tiled(pre.shape[0]), tiled(LANES), pl.BlockSpec((tile, width), lambda j, s: (j, 0))]
        + ([] if first else [tiled(n)])
    )
    out_shape = [jax.ShapeDtypeStruct((chunk, inner), BF16)] * count + [
        jax.ShapeDtypeStruct((n, inner), BF16)
    ] * count
    out_specs = [tiled(chunk)] * count + [tiled(n)] * count
    if final:
        out_shape += [jax.ShapeDtypeStruct((n // 2, inner), BF16)] * 2
        out_specs += [tiled(n // 2)] * 2
    else:
        out_shape += [jax.ShapeDtypeStruct((n, inner), F32)]
        out_specs += [tiled(n)]
    res = pl.pallas_call(
        functools.partial(grad_kernel, count, chunk, blocks, first, final),
        grid_spec=pltpu.PrefetchScalarGridSpec(
            num_scalar_prefetch=1, grid=(inner // tile,), in_specs=in_specs, out_specs=out_specs
        ),
        out_shape=out_shape,
        compiler_params=params(),
        cost_estimate=cost(
            2 * count * chunk * inner * width, inner * width * 2 + count * chunk * (inner * 4 + width * 2)
        ),
        name="grad_chunks",
    )(
        scalars, *arrived, *[gates] * count, *[read_keys] * count, *[ccol] * count,
        pre, spread, out_weight, *([] if first else [summed]),
    )
    return res[:count], res[count : 2 * count], res[2 * count :]


def back_kernel(per, place, part_ref, b_ref, ccol_ref, state_ref, blk_ref, keep_ref, other_ref,
                spread_ref, out_ref, running):
    step = pl.program_id(0)
    k = pl.num_programs(0) - 1 - step
    half = keep_ref.shape[0]

    @pl.when(step == 0)
    def _():
        at = place[0]
        running[pl.ds(at * half, half), :] = keep_ref[...].astype(F32)
        running[pl.ds((1 - at) * half, half), :] = other_ref[...].astype(F32)

    ccol = ccol_ref[...]
    end = ccol[GROUP - 1 :]
    docs = ccol[:, LANES - 1 :]
    exit_w = jnp.where(
        docs == end[:, LANES - 1 :], jnp.exp2(jnp.minimum(end - ccol, 0.0)), 0.0
    ).astype(BF16)
    carried = dot(b_ref[...], running[...].astype(BF16)) * dot(exit_w, spread_ref[...])
    out_ref[...] = (part_ref[...].astype(F32) + carried).astype(BF16)
    sub = lax.broadcasted_iota(jnp.int32, blk_ref.shape, 0)
    decay = jnp.sum(jnp.where(sub == k, blk_ref[...], 0.0), axis=0, keepdims=True)
    state = state_ref[0].astype(F32)
    for i in range(1, per):
        state = state + state_ref[i].astype(F32)
    running[...] = state + decay * running[...]


def back_tail(side, part, write_keys, ccol, states, blk, keep, other, spread):
    tokens, inner = part.shape
    n = write_keys.shape[1]
    blocks = tokens // GROUP
    per = states.shape[0] // blocks
    turn = lambda j, s: (blocks - 1 - j, 0)
    fixed = lambda shape: pl.BlockSpec(shape, lambda j, s: (0, 0))
    return pl.pallas_call(
        functools.partial(back_kernel, per),
        grid_spec=pltpu.PrefetchScalarGridSpec(
            num_scalar_prefetch=1,
            grid=(blocks,),
            in_specs=[
                pl.BlockSpec((GROUP, inner), turn),
                pl.BlockSpec((GROUP, n), turn),
                pl.BlockSpec((GROUP, LANES), turn),
                pl.BlockSpec((per, n, inner), lambda j, s: (blocks - 1 - j, 0, 0)),
                fixed(blk.shape), fixed(keep.shape), fixed(other.shape), fixed(spread.shape),
            ],
            out_specs=pl.BlockSpec((GROUP, inner), turn),
            scratch_shapes=[pltpu.VMEM((n, inner), F32)],
        ),
        out_shape=jax.ShapeDtypeStruct((tokens, inner), BF16),
        compiler_params=params(),
        cost_estimate=cost(2 * tokens * inner * n, tokens * inner * 4),
        name="back_tail",
    )(side, part, write_keys, ccol, states, blk, keep, other, spread)


def shifted(block, axis, distance):
    size = lax.axis_size(axis)
    route = [(i, i + distance) for i in range(size) if 0 <= i + distance < size]
    return lax.ppermute(block, axis, route)


def swapped(block, axis):
    return lax.ppermute(block, axis, [(i, i ^ 1) for i in range(lax.axis_size(axis))])


def rotated(block, axis, distance):
    size = lax.axis_size(axis)
    return lax.ppermute(block, axis, [(i, (i + distance) % size) for i in range(size)])


def scan_shards(keep, send, own_decay, mate_decay, first_in_pair, way):
    size = lax.axis_size("seq")
    window = max(size // 4, 1)
    keep_f = keep.astype(F32)
    got = swapped(send, "seq").astype(F32)
    near = jnp.where(first_in_pair, keep_f, got)
    far = jnp.where(first_in_pair, got, keep_f)
    near_decay = jnp.where(first_in_pair, own_decay, mate_decay)
    far_decay = jnp.where(first_in_pair, mate_decay, own_decay)
    total = (far + far_decay * near).astype(BF16)
    decay = own_decay * mate_decay
    reach = 1
    while reach < window:
        total = (total.astype(F32) + decay * shifted(total, "seq", 2 * way * reach).astype(F32)).astype(
            BF16
        )
        if 2 * reach < window:
            decay = decay * shifted(decay, "seq", 2 * way * reach)
        reach *= 2
    at_first = shifted(total, "seq", 2 * way).astype(F32)
    at_second = near + near_decay * at_first
    mine = jnp.where(first_in_pair, at_first, at_second).astype(BF16)
    hers = jnp.where(first_in_pair, at_second, at_first).astype(BF16)
    return mine, swapped(hers, "seq")


def shards(
    inputs, gates, write_keys, read_keys, log_decay, skip_gain, doc_ids, out_weight, grad_out
):
    tokens, inner = inputs.shape
    heads = log_decay.shape[0]
    width = inner // heads
    blocks = tokens // GROUP
    members = lax.axis_size("head")
    chips = members // 2
    chunk = tokens // members
    here = lax.axis_index("head")
    chip, core = here // 2, here % 2
    side = (lax.axis_index("seq") % 2).astype(jnp.int32)
    low = side == 0

    sibling = swapped(grad_out, "head")
    remote = [rotated(grad_out, "head", 2 * d) for d in range(1, chips)]
    relayed = [swapped(part, "head") for part in remote]

    ends = doc_ids[GROUP - 1 :: GROUP]
    last = doc_ids[tokens - 1 :] + 1
    before1 = shifted(last, "seq", 1)
    before2 = shifted(last, "seq", 2)
    mate_last = swapped(last, "seq")
    own_same = (last == before1).astype(F32)
    mate_same = jnp.where(low, mate_last == last, mate_last == before2).astype(F32)
    base = jnp.concatenate([before1 - 1, side[None], ends])

    spread = (
        jnp.arange(LANES)[:, None] == (jnp.arange(inner) // width)[None, :]
    ).astype(BF16)
    docs_row = doc_ids[None, :]
    skip = jnp.repeat(skip_gain, width)[None, :]

    ccol, crow, local, keep, send, pre, blk = local_states(
        inputs, write_keys, log_decay, docs_row, spread, side[None]
    )
    own_raw = pre[blocks : blocks + 1]
    own_decay = own_raw * own_same
    mate_decay = swapped(own_raw, "seq") * mate_same
    enter_keep, enter_other = scan_shards(keep, send, own_decay, mate_decay, low, 1)

    mixed = inside(inputs, write_keys, read_keys, ccol, crow, docs_row, skip, heads, False)

    numbers = lambda *qs: jnp.concatenate([base, jnp.stack(qs).astype(jnp.int32)])
    args = (gates, read_keys, ccol, pre, spread, out_weight)
    mate = here ^ 1
    q_remote = [(here - 2 * d) % members for d in range(1, chips)]
    q_relayed = [q ^ 1 for q in q_remote]
    groups = [([here, mate], [grad_out, sibling])]
    for d in range(chips - 1):
        groups.append(([q_remote[d]], [remote[d]]))
        groups.append(([q_relayed[d]], [relayed[d]]))
    summed, order, mixes, states = None, [], [], []
    for at, (qs, arrived) in enumerate(groups):
        final = at == len(groups) - 1
        mix, state, rest = grad_chunks(
            chunk, numbers(*qs), blocks, arrived, *args, summed, final
        )
        order += qs
        mixes += mix
        states += state
        summed = rest[0]
    back_keep, back_send = rest
    arrive_keep, arrive_other = scan_shards(
        back_keep, back_send, own_decay, mate_decay, jnp.logical_not(low), -1
    )

    tail = lambda *qs: forward_tail(
        chunk, numbers(*qs), len(qs), mixed, gates, read_keys, ccol, local,
        enter_keep, enter_other, pre, spread, out_weight,
    )
    landed = []
    for d in range(1, chips):
        target = ((chip + d) % chips) * 2
        give, stay = tail(target + 1 - core, target + core)
        both = (stay.astype(F32) + swapped(give, "head").astype(F32)).astype(BF16)
        landed.append(rotated(both, "head", 2 * d))
    give, stay = tail(mate, here)
    out = stay.astype(F32) + swapped(give, "head").astype(F32)
    for part in landed:
        out = out + part.astype(F32)
    mixed_out = out.astype(BF16)

    slot = jnp.zeros((members,), jnp.int32).at[jnp.stack(order)].set(jnp.arange(members, dtype=jnp.int32))
    mix_all = jnp.stack(mixes)[slot].reshape(tokens, inner)
    state_all = jnp.stack(states)[slot]
    part = inside(mix_all, write_keys, read_keys, ccol, crow, docs_row, skip, heads, True)
    grad_inputs = back_tail(
        side[None], part, write_keys, ccol, state_all, blk, arrive_keep, arrive_other, spread
    )
    return mixed_out, grad_inputs


def solution(mesh):
    in_specs = (
        P("seq", "head"),
        P("seq", "head"),
        P("seq", None),
        P("seq", None),
        P("head", "seq"),
        P("head"),
        P("seq"),
        P("head", None),
        P(("seq", "head"), None),
    )
    out_specs = (P(("seq", "head"), None), P("seq", "head"))
    return jax.shard_map(shards, mesh=mesh, in_specs=in_specs, out_specs=out_specs, check_vma=False)
```

time: 247 us -> 176 us (0.71)
  Pallas kernels: 0 us -> 82.3 us
  waiting for transfers between devices: 79.2 us -> 28.9 us
  matrix products: 49.4 us -> 0 us
  starting transfers between devices: 6.32 us -> 33.1 us
  local copies, waits for them, and re-layouts: 39.5 us -> 14 us
  other arithmetic: 34 us -> 11.9 us
  blocking collectives: 20.6 us -> 0 us
  between operations: 15.8 us -> 4.71 us
    pallas_call x0 -> x9, Pallas kernels: none -> 82.3 us  [the longest x3 31.6 us: grad_chunks(): pl.pallas_call(functools.partial(grad_kernel, count, chunk, blocks, first...]
    all_gather x3 -> x0, waiting for transfers between devices: 55.5 us -> none  [the longest x2 38 us: prefix(): lax.all_gather(part.astype(kind), axis)]
    dot_general x9 -> x0, matrix products: 49.4 us -> none  [the longest x1 12.9 us: shards(): jnp.dot(gated, out_weight, preferred_element_type=jnp.float32)]
    ppermute x1 -> x18, waiting for transfers between devices: 0.01 us -> 28.9 us  [the longest x2 19.5 us: rotated(): lax.ppermute(block, axis, [(i, (i + distance) % size) for i in range(size)])]
    ppermute x1 -> x18, starting transfers between devices: 6.16 us -> 33.1 us  [the longest x6 19.4 us: shifted(): return lax.ppermute(block, axis, route)]
    reduce_scatter x1 -> x0, waiting for transfers between devices: 23 us -> none  [shards(): lax.psum_scatter(jnp.dot(gated, out_weight, preferred_element_type=jnp.fl...]
    all_gather x1 -> x0, blocking collectives: 20.6 us -> none  [prefix(): lax.all_gather(part.astype(kind), axis)]
    select_n x16 -> x4, other arithmetic: 18.3 us -> 0.94 us  [the longest x1 0.85 us: scan_shards(): near_decay = jnp.where(first_in_pair, own_decay, mate_decay)]
  transfers between devices with their start and end apart: 5 -> 18, of which waited for: 4 -> 6; matrix products, arithmetic and copies ran while one was open for 41% -> 11% of each run, Pallas kernels for 0% -> 41%
where the time goes in v1:
time: 176 us; the launch traced here: 175 us
  Pallas kernels  82.3 us (47%)
  starting transfers between devices  33.1 us (19%)
  waiting for transfers between devices  28.9 us (16%)
  local copies, waits for them, and re-layouts  14 us (8%)
  other arithmetic  11.9 us (7%)
  between operations  4.71 us (3%)
    pallas_call x3, Pallas kernels, grad_chunks(): pl.pallas_call(functools.partial(grad_kernel, count, chunk, blocks, first...  31.6 us
    pallas_call x2, Pallas kernels, forward_tail(): pl.pallas_call(functools.partial(tail_kernel, count, chunk, blocks), grid...  22.2 us
    ppermute x2, waiting for transfers between devices, rotated(): lax.ppermute(block, axis, [(i, (i + distance) % size) for i in range(size)])  19.5 us
    ppermute x6, starting transfers between devices, shifted(): return lax.ppermute(block, axis, route)  19.4 us
    pallas_call x2, Pallas kernels, inside(): pl.pallas_call(functools.partial(inside_kernel, heads, inner // heads, ba...  14.7 us
    ppermute x10, starting transfers between devices, swapped(): lax.ppermute(block, axis, [(i, i ^ 1) for i in range(lax.axis_size(axis))])  9.21 us
    ppermute x6, waiting for transfers between devices, shifted(): return lax.ppermute(block, axis, route)  8.56 us
    pallas_call x1, Pallas kernels, local_states(): pl.pallas_call(lambda place, *refs: state_kernel(heads, place, *refs), gr...  8 us
  transfers between devices with their start and end apart: 18, of which 6 were waited for; matrix products, arithmetic and copies ran while one was open for 11% of the time, Pallas kernels for 41%

profile of v1, /device:TPU:0, one launch (start us, length us, event | category | flops | bytes accessed | tf_op | source)
XLA Modules:
  0.0 174.9 jit_solution(3350673349782104314)
XLA Ops:
  0.6 3.0 %collective-permute-start.12 = (bf16[256,2560]{1,0:T(8,128)(2,1)}, bf16[256,2560]{1,0:T(8,128)(2,1)S(1)}, u32[]{:S(2)}, u32[]{:S(2)}) collective-permute-start(bf16[256,2560]{1,0:T(8,128)(2,1)} %refs_0_.3), channel_id=1, source_target_pairs={{0,2},{1,3},{2,0},{3,1},{4,6},{5,7},{6,4},{7,5},{8,10},{9,11},{10,... | collective-permute-start | bytes 3932168 | tf_op jit(solution)/shard_map/ppermute | solution.py:459
  5.6 4.7 %collective-permute-start = (s32[1]{0:T(128)}, s32[1]{0:T(128)}, u32[]{:S(2)}, u32[]{:S(2)}) collective-permute-start(s32[1]{0:T(128)} %add.74), channel_id=1, source_target_pairs={{0,4},{4,8},{8,12},{12,16},{16,20},{20,24},{24,28},{1,5},{5,9},{9,... | collective-permute-start | bytes 20 | tf_op jit(solution)/shard_map/ppermute | solution.py:450
  10.3 2.8 %collective-permute-start.3 = (s32[1]{0:T(128)}, s32[1]{0:T(128)}, u32[]{:S(2)}, u32[]{:S(2)}) collective-permute-start(s32[1]{0:T(128)} %add.74), channel_id=1, source_target_pairs={{0,4},{4,0},{8,12},{12,8},{16,20},{20,16},{24,28},{28,24},{1,5},{5... | collective-permute-start | bytes 20 | tf_op jit(solution)/shard_map/ppermute | solution.py:454
  13.1 4.8 %collective-permute-start.4 = (s32[1]{0:T(128)}, s32[1]{0:T(128)}, u32[]{:S(2)}, u32[]{:S(2)}) collective-permute-start(s32[1]{0:T(128)} %add.74), channel_id=1, source_target_pairs={{0,8},{4,12},{8,16},{12,20},{16,24},{20,28},{1,9},{5,13},{9,17},{1... | collective-permute-start | bytes 20 | tf_op jit(solution)/shard_map/ppermute | solution.py:450
  18.6 14.0 %collective-permute-done.12.refs_0_ = bf16[256,2560]{1,0:T(8,128)(2,1)S(1)} collective-permute-done((bf16[256,2560]{1,0:T(8,128)(2,1)}, bf16[256,2560]{1,0:T(8,128)(2,1)S(1)}, u32[]{:S(2)}, u32[]{:S(2)}) %collective-permute-start.12) | collective-permute-done | bytes 1310752 | tf_op jit(solution)/shard_map/ppermute | solution.py:459
  33.5 8.0 %local_states.1 = (f32[1024,128]{1,0:T(8,128)}, f32[24,1024]{1,0:T(8,128)}, bf16[4,128,1280]{2,1,0:T(8,128)(2,1)}, bf16[64,1280]{1,0:T(8,128)(2,1)}, bf16[64,128...) custom-call(s32[1]{0:T(128)} %bitcast.place, bf16[1024,1280]{1,0:T(8,128)(2,1)} %x_ref.1, ...), custom_call_target="tpu_custom_call" | custom-call | flops 671088640 | bytes 7864320 | tf_op jit(solution)/shard_map/local_states/pallas_call | solution.py:112
  42.3 1.8 %collective-permute-start.2 = (f32[1,1280]{1,0:T(1,128)S(1)}, f32[1,1280]{1,0:T(1,128)S(1)}, u32[]{:S(2)}, u32[]{:S(2)}) collective-permute-start(f32[1,1280]{1,0:T(1,128)S(1)} %slice.11), channel_id=1, source_target_pairs={{0,4},{4,0},{8,12},{12,8},{16,20},{20,16},{24,28},{28,24},{1,5},{5... | collective-permute-start | bytes 15368 | tf_op jit(solution)/shard_map/ppermute | solution.py:454
  51.3 13.7 %grad_chunks.3 = (bf16[256,1280]{1,0:T(8,128)(2,1)}, bf16[256,1280]{1,0:T(8,128)(2,1)}, bf16[128,1280]{1,0:T(8,128)(2,1)}, bf16[128,1280]{1,0:T(8,128)(2,1)}, f32[128,1280]{1,0:T(8,128)}) custom-call(s32[8]{0:T(128)} %concatenate.42.scalars, bf16[256,2560]{1,0:T(8,128)(2,1)} %refs_0_.3, bf16[256,2560]{1,0:T(8,128)(2,1)} %copy-done, ...), custom_call_target="tpu_custom_call" | custom-call | flops 3355443200 | bytes 11796480 | tf_op jit(solution)/shard_map/grad_chunks/pallas_call | solution.py:372
  64.9 8.9 %grad_chunks.4 = (bf16[256,1280]{1,0:T(8,128)(2,1)}, bf16[128,1280]{1,0:T(8,128)(2,1)}, f32[128,1280]{1,0:T(8,128)}) custom-call(s32[7]{0:T(128)} %get-tuple-element.53.scalars, bf16[256,2560]{1,0:T(8,128)(2,1)} %copy-done.3, bf16[1024,1280]{1,0:T(8,128)(2,1)} %refs_1_.5, bf16[1024,128]{1,0:T(8,128)(2,1)} %c_ref.3, ...), custom_call_target="tpu_custom_call" | custom-call | flops 1677721600 | bytes 9175040 | tf_op jit(solution)/shard_map/grad_chunks/pallas_call | solution.py:372
  73.9 9.0 %grad_chunks.5 = (bf16[256,1280]{1,0:T(8,128)(2,1)}, bf16[128,1280]{1,0:T(8,128)(2,1)}, bf16[64,1280]{1,0:T(8,128)(2,1)}, bf16[64,1280]{1,0:T(8,128)(2,1)}) custom-call(s32[7]{0:T(128)} %pad_add_fusion.2.scalars, bf16[256,2560]{1,0:T(8,128)(2,1)} %collective-permute-done.13.refs_0_, bf16[1024,1280]{1,0:T(8,128)(2,1)} %refs_1_.5, bf16[1024,128]{1,0:T(8,128)(2,1)} %c_ref.3, ...), custom_call_target="tpu_custom_call" | custom-call | flops 1677721600 | bytes 9175040 | tf_op jit(solution)/shard_map/grad_chunks/pallas_call | solution.py:372
  82.9 1.8 %collective-permute-start.14 = (bf16[64,1280]{1,0:T(8,128)(2,1)}, bf16[64,1280]{1,0:T(8,128)(2,1)S(1)}, u32[]{:S(2)}, u32[]{:S(2)}) collective-permute-start(bf16[64,1280]{1,0:T(8,128)(2,1)} %get-tuple-element.46), channel_id=1, source_target_pairs={{0,4},{4,0},{8,12},{12,8},{16,20},{20,16},{24,28},{28,24},{1,5},{5... | collective-permute-start | bytes 491528 | tf_op jit(solution)/shard_map/ppermute | solution.py:454
  84.8 3.5 %collective-permute-start.5 = (bf16[64,1280]{1,0:T(8,128)(2,1)S(1)}, bf16[64,1280]{1,0:T(8,128)(2,1)S(1)}, u32[]{:S(2)}, u32[]{:S(2)}) collective-permute-start(bf16[64,1280]{1,0:T(8,128)(2,1)S(1)} %fusion.2), channel_id=1, source_target_pairs={{0,8},{4,12},{8,16},{12,20},{16,24},{20,28},{1,9},{5,13},{9,17},{1... | collective-permute-start | bytes 491528 | tf_op jit(solution)/shard_map/ppermute | solution.py:450
  91.5 5.9 %collective-permute-done.15 = bf16[64,1280]{1,0:T(8,128)(2,1)S(1)} collective-permute-done((bf16[64,1280]{1,0:T(8,128)(2,1)S(1)}, bf16[64,1280]{1,0:T(8,128)(2,1)S(1)}, u32[]{:S(2)}, u32[]{:S(2)}) %collective-permute-start.15) | collective-permute-done | bytes 163872 | tf_op jit(solution)/shard_map/ppermute | solution.py:450
  97.4 3.7 %collective-permute-start.6 = (bf16[64,1280]{1,0:T(8,128)(2,1)S(1)}, bf16[64,1280]{1,0:T(8,128)(2,1)S(1)}, u32[]{:S(2)}, u32[]{:S(2)}) collective-permute-start(bf16[64,1280]{1,0:T(8,128)(2,1)S(1)} %get-tuple-element.60), channel_id=1, source_target_pairs={{0,8},{4,12},{8,16},{12,20},{16,24},{20,28},{1,9},{5,13},{9,17},{1... | collective-permute-start | bytes 491528 | tf_op jit(solution)/shard_map/ppermute | solution.py:450
  101.9 2.0 %collective-permute-done.6 = bf16[64,1280]{1,0:T(8,128)(2,1)S(1)} collective-permute-done((bf16[64,1280]{1,0:T(8,128)(2,1)S(1)}, bf16[64,1280]{1,0:T(8,128)(2,1)S(1)}, u32[]{:S(2)}, u32[]{:S(2)}) %collective-permute-start.6) | collective-permute-done | bytes 163872 | tf_op jit(solution)/shard_map/ppermute | solution.py:450
  106.3 7.4 %inside_forward.1.refs_0_.refs_1_ = bf16[1024,1280]{1,0:T(8,128)(2,1)} custom-call(bf16[1024,1280]{1,0:T(8,128)(2,1)} %x_ref.1, bf16[1024,128]{1,0:T(8,128)(2,1)} %b_ref.5, bf16[1024,128]{1,0:T(8,128)(2,1)} %c_ref.3, f32[1024,128]{1,0:T(8,128)} %get-tuple-element.25.ccol_ref.refs_6_.refs_7_.refs_3_, f32[24,1024]{1,0:T(8,128)} %get-tuple-element.26.crow_ref, ...), custom_call_target="tpu_custom_call" | custom-call | flops 2684354560 | bytes 5242880 | tf_op jit(solution)/shard_map/inside_forward/pallas_call | solution.py:206
  115.0 11.1 %forward_tail.3 = (bf16[256,2560]{1,0:T(8,128)(2,1)}, bf16[256,2560]{1,0:T(8,128)(2,1)}) custom-call(s32[8]{0:T(128)} %concatenate.41.scalars, bf16[1024,1280]{1,0:T(8,128)(2,1)} %inside_forward.1.refs_0_.refs_1_, bf16[1024,1280]{1,0:T(8,128)(2,1)} %inside_forward.1.refs_0_.refs_1_, bf16[1024,1280]{1,0:T(8,128)(2,1)} %refs_1_.5, bf16[1024,1280]{1,0:T(8,128)(2,1)} %refs_1_.5, ...), custom_call_target="tpu_custom_call" | custom-call | flops 3355443200 | bytes 11796480 | tf_op jit(solution)/shard_map/forward_tail/pallas_call | solution.py:290
  127.5 11.2 %forward_tail.2 = (bf16[256,2560]{1,0:T(8,128)(2,1)}, bf16[256,2560]{1,0:T(8,128)(2,1)}) custom-call(s32[8]{0:T(128)} %concatenate.40.scalars, bf16[1024,1280]{1,0:T(8,128)(2,1)} %inside_forward.1.refs_0_.refs_1_, bf16[1024,1280]{1,0:T(8,128)(2,1)} %inside_forward.1.refs_0_.refs_1_, bf16[1024,1280]{1,0:T(8,128)(2,1)} %refs_1_.5, bf16[1024,1280]{1,0:T(8,128)(2,1)} %refs_1_.5, ...), custom_call_target="tpu_custom_call" | custom-call | flops 3355443200 | bytes 11796480 | tf_op jit(solution)/shard_map/forward_tail/pallas_call | solution.py:290
  145.2 3.1 %gather_fusion.1 = bf16[4,128,1280]{2,1,0:T(8,128)(2,1)} fusion(bf16[4,128,1280]{2,1,0:T(8,128)(2,1)} %pad_maximum_fusion.1, s32[1024]{0:T(1024)S(1)} %pad_clamp_fusion), kind=kCustom, calls=%fused_computation.1 | custom fusion | bytes 2621456 | tf_op jit(solution)/shard_map/gather | solution.py:574
  148.3 2.2 %gather_fusion = bf16[4,256,1280]{2,1,0:T(8,128)(2,1)} fusion(bf16[4,256,1280]{2,1,0:T(8,128)(2,1)S(1)} %pad_maximum_fusion, s32[1024]{0:T(1024)S(1)} %pad_clamp_fusion), kind=kCustom, calls=%fused_computation | custom fusion | bytes 5242896 | tf_op jit(solution)/shard_map/gather | solution.py:573
  152.4 7.4 %inside_backward.1.part_ref = bf16[1024,1280]{1,0:T(8,128)(2,1)} custom-call(bf16[1024,1280]{1,0:T(8,128)(2,1)} %bitcast.26, bf16[1024,128]{1,0:T(8,128)(2,1)} %b_ref.5, bf16[1024,128]{1,0:T(8,128)(2,1)} %c_ref.3, f32[1024,128]{1,0:T(8,128)} %get-tuple-element.25.ccol_ref.refs_6_.refs_7_.refs_3_, f32[24,1024]{1,0:T(8,128)} %get-tuple-element.26.crow_ref, ...), custom_call_target="tpu_custom_call" | custom-call | flops 2684354560 | bytes 5242880 | tf_op jit(solution)/shard_map/inside_backward/pallas_call | solution.py:206
  160.5 5.7 %back_tail.1 = bf16[1024,1280]{1,0:T(8,128)(2,1)} custom-call(s32[1]{0:T(128)} %bitcast.place, bf16[1024,1280]{1,0:T(8,128)(2,1)} %inside_backward.1.part_ref, bf16[1024,128]{1,0:T(8,128)(2,1)} %b_ref.5, f32[1024,128]{1,0:T(8,128)} %get-tuple-element.25.ccol_ref.refs_6_.refs_7_.refs_3_, bf16[4,128,1280]{2,1,0:T(8,128)(2,1)} %gather_fusion.1, ...), custom_call_target="tpu_custom_call" | custom-call | flops 335544320 | bytes 5242880 | tf_op jit(solution)/shard_map/back_tail/pallas_call | solution.py:425
  166.2 5.5 %collective-permute-done.10 = bf16[256,2560]{1,0:T(8,128)(2,1)} collective-permute-done((bf16[256,2560]{1,0:T(8,128)(2,1)}, bf16[256,2560]{1,0:T(8,128)(2,1)}, u32[]{:S(2)}, u32[]{:S(2)}) %collective-permute-start.10) | collective-permute-done | bytes 1310752 | tf_op jit(solution)/shard_map/ppermute | solution.py:459
  171.7 3.2 %add_convert_fusion = bf16[256,2560]{1,0:T(8,128)(2,1)} fusion(bf16[256,2560]{1,0:T(8,128)(2,1)} %collective-permute-done.10, bf16[256,2560]{1,0:T(8,128)(2,1)} %collective-permute-done.8, bf16[256,2560]{1,0:T(8,128)(2,1)S(1)} %copy-done.1), kind=kLoop, calls=%fused_computation.4 | loop fusion | flops 3932160 | bytes 5242880 | tf_op jit(solution)/shard_map/convert_element_type | solution.py:570
  (84 shorter events, 25.9 us)
Async XLA Ops:
  0.6 32.0 %collective-permute-start.12 = (bf16[256,2560]{1,0:T(8,128)(2,1)}, bf16[256,2560]{1,0:T(8,128)(2,1)S(1)}, u32[]{:S(2)}, u32[]{:S(2)}) collective-permute-start(bf16[256,2560]{1,0:T(8,128)(2,1)} %refs_0_.3), channel_id=1, source_target_pairs={{0,2},{1,3},{2,0},{3,1},{4,6},{5,7},{6,4},{7,5},{8,10},{9,11},{10,... | collective-permute-start | bytes 3932168 | tf_op jit(solution)/shard_map/ppermute | solution.py:459
  3.6 46.5 %collective-permute-start.11 = (bf16[256,2560]{1,0:T(8,128)(2,1)}, bf16[256,2560]{1,0:T(8,128)(2,1)S(1)}, u32[]{:S(2)}, u32[]{:S(2)}) collective-permute-start(bf16[256,2560]{1,0:T(8,128)(2,1)} %refs_0_.3), channel_id=1, source_target_pairs={{0,1},{1,0},{2,3},{3,2},{4,5},{5,4},{6,7},{7,6},{8,9},{9,8},{10,11... | collective-permute-start | bytes 3932168 | tf_op jit(solution)/shard_map/ppermute | solution.py:454
  5.6 36.7 %collective-permute-start = (s32[1]{0:T(128)}, s32[1]{0:T(128)}, u32[]{:S(2)}, u32[]{:S(2)}) collective-permute-start(s32[1]{0:T(128)} %add.74), channel_id=1, source_target_pairs={{0,4},{4,8},{8,12},{12,16},{16,20},{20,24},{24,28},{1,5},{5,9},{9,... | collective-permute-start | bytes 20 | tf_op jit(solution)/shard_map/ppermute | solution.py:450
  10.3 35.6 %collective-permute-start.3 = (s32[1]{0:T(128)}, s32[1]{0:T(128)}, u32[]{:S(2)}, u32[]{:S(2)}) collective-permute-start(s32[1]{0:T(128)} %add.74), channel_id=1, source_target_pairs={{0,4},{4,0},{8,12},{12,8},{16,20},{20,16},{24,28},{28,24},{1,5},{5... | collective-permute-start | bytes 20 | tf_op jit(solution)/shard_map/ppermute | solution.py:454
  13.1 33.8 %collective-permute-start.4 = (s32[1]{0:T(128)}, s32[1]{0:T(128)}, u32[]{:S(2)}, u32[]{:S(2)}) collective-permute-start(s32[1]{0:T(128)} %add.74), channel_id=1, source_target_pairs={{0,8},{4,12},{8,16},{12,20},{16,24},{20,28},{1,9},{5,13},{9,17},{1... | collective-permute-start | bytes 20 | tf_op jit(solution)/shard_map/ppermute | solution.py:450
  32.6 8.9 %copy-start.3 = (bf16[256,2560]{1,0:T(8,128)(2,1)}, bf16[256,2560]{1,0:T(8,128)(2,1)S(1)}, u32[]{:S(2)}) copy-start(bf16[256,2560]{1,0:T(8,128)(2,1)S(1)} %collective-permute-done.12.refs_0_) | copy-start | bytes 3932164
  32.6 41.2 %collective-permute-start.13 = (bf16[256,2560]{1,0:T(8,128)(2,1)S(1)}, bf16[256,2560]{1,0:T(8,128)(2,1)}, u32[]{:S(2)}, u32[]{:S(2)}) collective-permute-start(bf16[256,2560]{1,0:T(8,128)(2,1)S(1)} %collective-permute-done.12.refs_0_), channel_id=1, source_target_pairs={{0,1},{1,0},{2,3},{3,2},{4,5},{5,4},{6,7},{7,6},{8,9},{9,8},{10,11... | collective-permute-start | bytes 3932168 | tf_op jit(solution)/shard_map/ppermute | solution.py:454
  42.3 7.0 %collective-permute-start.2 = (f32[1,1280]{1,0:T(1,128)S(1)}, f32[1,1280]{1,0:T(1,128)S(1)}, u32[]{:S(2)}, u32[]{:S(2)}) collective-permute-start(f32[1,1280]{1,0:T(1,128)S(1)} %slice.11), channel_id=1, source_target_pairs={{0,4},{4,0},{8,12},{12,8},{16,20},{20,16},{24,28},{28,24},{1,5},{5... | collective-permute-start | bytes 15368 | tf_op jit(solution)/shard_map/ppermute | solution.py:454
  45.9 38.8 %collective-permute-start.1 = (bf16[64,1280]{1,0:T(8,128)(2,1)}, bf16[64,1280]{1,0:T(8,128)(2,1)S(1)}, u32[]{:S(2)}, u32[]{:S(2)}) collective-permute-start(bf16[64,1280]{1,0:T(8,128)(2,1)} %get-tuple-element.28), channel_id=1, source_target_pairs={{0,4},{4,0},{8,12},{12,8},{16,20},{20,16},{24,28},{28,24},{1,5},{5... | collective-permute-start | bytes 491528 | tf_op jit(solution)/shard_map/ppermute | solution.py:454
  73.9 10.8 %copy-start.10 = (bf16[64,1280]{1,0:T(8,128)(2,1)S(1)}, bf16[64,1280]{1,0:T(8,128)(2,1)}, u32[]{:S(2)}) copy-start(bf16[64,1280]{1,0:T(8,128)(2,1)} %get-tuple-element.29) | copy-start | bytes 491524
  82.9 18.3 %copy-start.16 = (f32[20]{0:T(128)S(1)}, f32[20]{0:T(128)}, u32[]{:S(2)}) copy-start(f32[20]{0:T(128)} %param.14) | copy-start | bytes 244
  82.9 6.3 %collective-permute-start.14 = (bf16[64,1280]{1,0:T(8,128)(2,1)}, bf16[64,1280]{1,0:T(8,128)(2,1)S(1)}, u32[]{:S(2)}, u32[]{:S(2)}) collective-permute-start(bf16[64,1280]{1,0:T(8,128)(2,1)} %get-tuple-element.46), channel_id=1, source_target_pairs={{0,4},{4,0},{8,12},{12,8},{16,20},{20,16},{24,28},{28,24},{1,5},{5... | collective-permute-start | bytes 491528 | tf_op jit(solution)/shard_map/ppermute | solution.py:454
  84.8 6.7 %collective-permute-start.5 = (bf16[64,1280]{1,0:T(8,128)(2,1)S(1)}, bf16[64,1280]{1,0:T(8,128)(2,1)S(1)}, u32[]{:S(2)}, u32[]{:S(2)}) collective-permute-start(bf16[64,1280]{1,0:T(8,128)(2,1)S(1)} %fusion.2), channel_id=1, source_target_pairs={{0,8},{4,12},{8,16},{12,20},{16,24},{20,28},{1,9},{5,13},{9,17},{1... | collective-permute-start | bytes 491528 | tf_op jit(solution)/shard_map/ppermute | solution.py:450
  90.1 7.2 %collective-permute-start.15 = (bf16[64,1280]{1,0:T(8,128)(2,1)S(1)}, bf16[64,1280]{1,0:T(8,128)(2,1)S(1)}, u32[]{:S(2)}, u32[]{:S(2)}) collective-permute-start(bf16[64,1280]{1,0:T(8,128)(2,1)S(1)} %fusion.4), channel_id=1, source_target_pairs={{8,0},{12,4},{16,8},{20,12},{24,16},{28,20},{9,1},{13,5},{17,9},{2... | collective-permute-start | bytes 491528 | tf_op jit(solution)/shard_map/ppermute | solution.py:450
  97.4 6.5 %collective-permute-start.6 = (bf16[64,1280]{1,0:T(8,128)(2,1)S(1)}, bf16[64,1280]{1,0:T(8,128)(2,1)S(1)}, u32[]{:S(2)}, u32[]{:S(2)}) collective-permute-start(bf16[64,1280]{1,0:T(8,128)(2,1)S(1)} %get-tuple-element.60), channel_id=1, source_target_pairs={{0,8},{4,12},{8,16},{12,20},{16,24},{20,28},{1,9},{5,13},{9,17},{1... | collective-permute-start | bytes 491528 | tf_op jit(solution)/shard_map/ppermute | solution.py:450
  104.7 9.6 %collective-permute-start.7 = (bf16[64,1280]{1,0:T(8,128)(2,1)S(1)}, bf16[64,1280]{1,0:T(8,128)(2,1)S(1)}, u32[]{:S(2)}, u32[]{:S(2)}) collective-permute-start(bf16[64,1280]{1,0:T(8,128)(2,1)S(1)} %get-tuple-element.57), channel_id=1, source_target_pairs={{0,4},{4,0},{8,12},{12,8},{16,20},{20,16},{24,28},{28,24},{1,5},{5... | collective-permute-start | bytes 491528 | tf_op jit(solution)/shard_map/ppermute | solution.py:454
  126.0 13.2 %collective-permute-start.9 = (bf16[256,2560]{1,0:T(8,128)(2,1)}, bf16[256,2560]{1,0:T(8,128)(2,1)S(1)}, u32[]{:S(2)}, u32[]{:S(2)}) collective-permute-start(bf16[256,2560]{1,0:T(8,128)(2,1)} %get-tuple-element.34), channel_id=1, source_target_pairs={{0,1},{1,0},{2,3},{3,2},{4,5},{5,4},{6,7},{7,6},{8,9},{9,8},{10,11... | collective-permute-start | bytes 3932168 | tf_op jit(solution)/shard_map/ppermute | solution.py:454
  127.5 11.7 %copy-start.2 = (bf16[256,2560]{1,0:T(8,128)(2,1)S(1)}, bf16[256,2560]{1,0:T(8,128)(2,1)}, u32[]{:S(2)}) copy-start(bf16[256,2560]{1,0:T(8,128)(2,1)} %get-tuple-element.33) | copy-start | bytes 3932164
  138.7 27.5 %collective-permute-start.8 = (bf16[256,2560]{1,0:T(8,128)(2,1)}, bf16[256,2560]{1,0:T(8,128)(2,1)}, u32[]{:S(2)}, u32[]{:S(2)}) collective-permute-start(bf16[256,2560]{1,0:T(8,128)(2,1)} %get-tuple-element.32), channel_id=1, source_target_pairs={{0,1},{1,0},{2,3},{3,2},{4,5},{5,4},{6,7},{7,6},{8,9},{9,8},{10,11... | collective-permute-start | bytes 3932168 | tf_op jit(solution)/shard_map/ppermute | solution.py:454
  139.2 2.9 %copy-start.6 = (bf16[256,1280]{1,0:T(8,128)(2,1)S(1)}, bf16[256,1280]{1,0:T(8,128)(2,1)}, u32[]{:S(2)}) copy-start(bf16[256,1280]{1,0:T(8,128)(2,1)} %get-tuple-element.36) | copy-start | bytes 1966084
  140.6 31.0 %collective-permute-start.10 = (bf16[256,2560]{1,0:T(8,128)(2,1)}, bf16[256,2560]{1,0:T(8,128)(2,1)}, u32[]{:S(2)}, u32[]{:S(2)}) collective-permute-start(bf16[256,2560]{1,0:T(8,128)(2,1)} %add_convert_fusion.1), channel_id=1, source_target_pairs={{0,2},{1,3},{2,0},{3,1},{4,6},{5,7},{6,4},{7,5},{8,10},{9,11},{10,... | collective-permute-start | bytes 3932168 | tf_op jit(solution)/shard_map/ppermute | solution.py:459
  142.5 8.6 %collective-permute-start.16 = (bf16[64,1280]{1,0:T(8,128)(2,1)S(1)}, bf16[64,1280]{1,0:T(8,128)(2,1)S(1)}, u32[]{:S(2)}, u32[]{:S(2)}) collective-permute-start(bf16[64,1280]{1,0:T(8,128)(2,1)S(1)} %get-tuple-element.59), channel_id=1, source_target_pairs={{8,0},{12,4},{16,8},{20,12},{24,16},{28,20},{9,1},{13,5},{17,9},{2... | collective-permute-start | bytes 491528 | tf_op jit(solution)/shard_map/ppermute | solution.py:450
  151.9 7.9 %collective-permute-start.17 = (bf16[64,1280]{1,0:T(8,128)(2,1)S(1)}, bf16[64,1280]{1,0:T(8,128)(2,1)S(1)}, u32[]{:S(2)}, u32[]{:S(2)}) collective-permute-start(bf16[64,1280]{1,0:T(8,128)(2,1)S(1)} %get-tuple-element.55), channel_id=1, source_target_pairs={{0,4},{4,0},{8,12},{12,8},{16,20},{20,16},{24,28},{28,24},{1,5},{5... | collective-permute-start | bytes 491528 | tf_op jit(solution)/shard_map/ppermute | solution.py:454
  160.5 11.2 %copy-start.1 = (bf16[256,2560]{1,0:T(8,128)(2,1)S(1)}, bf16[256,2560]{1,0:T(8,128)(2,1)}, u32[]{:S(2)}) copy-start(bf16[256,2560]{1,0:T(8,128)(2,1)} %get-tuple-element.31) | copy-start | bytes 3932164
  (11 other events, 21.1 us)

commit v2 on v0

v2 whole, which is shorter than its diff:
```python
import functools
import math

import jax
import jax.numpy as jnp
from jax import lax
from jax.experimental import pallas as pl
from jax.experimental.pallas import tpu as pltpu
from jax.sharding import PartitionSpec as P

GROUP = 256
LANES = 128
TILE = 16
LOG2E = math.log2(math.e)
F32 = jnp.float32
BF16 = jnp.bfloat16
NT = (((1,), (1,)), ((), ()))
TN = (((0,), (0,)), ((), ()))
VM = pl.BlockSpec(memory_space=pltpu.VMEM)
SM = pl.BlockSpec(memory_space=pltpu.SMEM)
HB = pl.BlockSpec(memory_space=pltpu.HBM)
DECAY, DECAY_REST, LAST, FIRST = range(4)


def dot(a, b, dims=(((1,), (0,)), ((), ()))):
    return lax.dot_general(a, b, dims, preferred_element_type=F32)


def call(kernel, name, out_shape, in_specs, args, limit_mib=16, scratch=(), aliases=None):
    space = {id(VM): pltpu.VMEM, id(HB): pltpu.HBM}
    args = [
        arg if spec is SM else pltpu.with_memory_space_constraint(arg, space[id(spec)])
        for spec, arg in zip(in_specs, args, strict=True)
    ]
    return pl.pallas_call(
        kernel,
        in_specs=in_specs,
        out_specs=[VM if o.memory_space == pltpu.VMEM else HB for o in out_shape],
        out_shape=out_shape,
        scratch_shapes=scratch,
        input_output_aliases=aliases or {},
        compiler_params=pltpu.CompilerParams(vmem_limit_bytes=limit_mib * 2**20),
        cost_estimate=pl.CostEstimate(flops=1, bytes_accessed=1, transcendentals=0),
        name=name,
    )(*args)


def start(sems, *pairs):
    copies = [
        pltpu.make_async_copy(source, target, sems.at[i]) for i, (source, target) in enumerate(pairs)
    ]
    for copy in copies:
        copy.start()
    return copies


def split(value):
    high = value.astype(BF16)
    return high, (value - high.astype(F32)).astype(BF16)


def silu(gates):
    v = gates.astype(F32)
    return 0.5 * v * (1.0 + jnp.tanh(0.5 * v))


def row_at(rows, k):
    return jnp.sum(jnp.where(iota(rows.shape, 0) == k, rows, 0.0), axis=0, keepdims=True)


def iota(shape, dim):
    return lax.broadcasted_iota(jnp.int32, shape, dim)


def state_kernel(
    heads, blocks, places, x_hbm, b_hbm, c_hbm, ld_hbm, doc_ref, spread_ref,
    crow_ref, entry_ref, exit_ref, local_ref, keep_ref, send_ref, pre_ref, blk_ref, info_ref,
    x_ref, b_ref, c_ref, padded, running, ld_ref, sems,
):
    n, inner = running.shape
    half = n // 2
    parts = [pl.ds(k * GROUP, GROUP) for k in range(blocks)]
    ld_copy, b_copy, c_copy, *x_copies = start(
        sems, (ld_hbm, ld_ref), (b_hbm, b_ref), (c_hbm, c_ref),
        *[(x_hbm.at[p], x_ref.at[p]) for p in parts],
    )
    head_rows = crow_ref.shape[1]
    spread = spread_ref[...]
    later = (iota((GROUP, GROUP), 0) <= iota((GROUP, GROUP), 1)).astype(BF16)
    padded[...] = jnp.zeros_like(padded)
    row = iota((head_rows, GROUP), 0)
    pre_ref[...] = jnp.zeros_like(pre_ref)
    blk_ref[...] = jnp.zeros_like(blk_ref)
    info_ref[...] = jnp.zeros_like(info_ref)
    first_doc = last_doc = total = None
    ld_copy.wait()
    for k in range(blocks):
        at = slice(k * GROUP, (k + 1) * GROUP)
        padded[0:heads, :] = ld_ref[:, at] * LOG2E
        steps = padded[0:head_rows, :]
        high, rest = split(steps)
        mid, low = split(steps - high.astype(F32))
        cum = dot(high, later) + (dot(mid, later) + dot(low, later))
        cum = jnp.where(row == head_rows - 1, doc_ref[:, at].astype(F32), cum)
        crow_ref[k] = cum
        padded[0:head_rows, :] = cum
        ccol = padded[...].T
        padded[0:head_rows, :] = jnp.zeros((head_rows, GROUP), F32)
        docs = ccol[:, head_rows - 1 : head_rows]
        end = ccol[GROUP - 1 :]
        end_doc = end[:, head_rows - 1 : head_rows]
        if k == 0:
            first_doc = ccol[0:1, head_rows - 1 : head_rows]
            last_doc = first_doc
            total = jnp.zeros_like(end)
        exit_w = jnp.where(docs == end_doc, jnp.exp2(jnp.minimum(end - ccol, 0.0)), 0.0).astype(BF16)
        exit_ref[at, :] = exit_w
        entry_ref[at, :] = jnp.where(docs == last_doc, jnp.exp2(jnp.minimum(ccol, 0.0)), 0.0).astype(BF16)
        if k == 0:
            b_copy.wait()
        x_copies[k].wait()
        scaled = (dot(exit_w, spread) * x_ref[at, :].astype(F32)).astype(BF16)
        own = dot(b_ref[at, :], scaled, TN)
        block_decay = jnp.where(end_doc == last_doc, jnp.exp2(end), 0.0)
        whole = jnp.exp2(total + end)
        stacked = jnp.concatenate(
            [block_decay, jnp.where(end_doc == first_doc, whole, 0.0), whole, jnp.zeros((5, LANES), F32)],
            axis=0,
        )
        high, rest = split(stacked)
        wide = dot(high, spread) + dot(rest, spread)
        blk_ref[k : k + 1, :] = wide[0:1]
        if k == 0:
            local_ref[k] = jnp.zeros((n, inner), BF16)
            pre_ref[0:1, :] = jnp.ones((1, inner), F32)
            running[...] = own
        else:
            local_ref[k] = running[...].astype(BF16)
            running[...] = wide[0:1] * running[...] + own
        if k < blocks - 1:
            pre_ref[k + 1 : k + 2, :] = wide[1:2]
        total = total + end
        last_doc = end_doc
    raw = wide[2:3]
    last_row = jnp.broadcast_to(last_doc + 1.0, (1, inner))
    first_row = jnp.broadcast_to(first_doc + 1.0, (1, inner))
    info_ref[0:1, :] = raw
    info_ref[1:2, :] = last_row
    info_ref[2:3, :] = first_row
    side = places[0]
    keep_ref[...] = running[pl.ds(pl.multiple_of(side * half, half), half), :].astype(BF16)
    send_ref[0:half, :] = running[pl.ds(pl.multiple_of((1 - side) * half, half), half), :].astype(BF16)
    send_ref[half:, :] = tags(raw, last_row, first_row)
    c_copy.wait()


def tags(decay, last, first):
    high, rest = split(decay)
    rows = [high.astype(F32), rest.astype(F32), last, first]
    rows.append(jnp.zeros((TILE - len(rows), decay.shape[1]), F32))
    return jnp.concatenate(rows, axis=0).astype(BF16)


def untagged(block):
    half = block.shape[0] - TILE
    state, rows = block[:half].astype(F32), block[half:].astype(F32)
    row = lambda i: rows[i : i + 1]
    return state, row(DECAY) + row(DECAY_REST), row(LAST), row(FIRST)


def local_states(places, inputs, write_keys, read_keys, log_decay, docs_row, spread):
    tokens, inner = inputs.shape
    heads = log_decay.shape[0]
    n = write_keys.shape[1]
    blocks = tokens // GROUP
    head_rows = -(-(heads + 1) // 8) * 8
    block_rows = -(-blocks // 8) * 8
    return call(
        functools.partial(state_kernel, heads, blocks),
        "local_states",
        [
            pltpu.VMEM((blocks, head_rows, GROUP), F32),
            pltpu.VMEM((tokens, LANES), BF16),
            pltpu.VMEM((tokens, LANES), BF16),
            pltpu.VMEM((blocks, n, inner), BF16),
            pltpu.VMEM((n // 2, inner), BF16),
            pltpu.VMEM((n // 2 + TILE, inner), BF16),
            pltpu.VMEM((block_rows, inner), F32),
            pltpu.VMEM((block_rows, inner), F32),
            pltpu.VMEM((8, inner), F32),
            pltpu.VMEM((tokens, inner), BF16),
            pltpu.VMEM((tokens, n), BF16),
            pltpu.VMEM((tokens, n), BF16),
        ],
        [SM] + [HB] * 4 + [VM] * 2,
        (places, inputs, write_keys, read_keys, log_decay, docs_row, spread),
        scratch=[
            pltpu.VMEM((LANES, GROUP), F32),
            pltpu.VMEM((n, inner), F32),
            pltpu.VMEM((heads, tokens), F32),
            pltpu.SemaphoreType.DMA((3 + blocks,)),
        ],
    )


def inside_kernel(heads, width, blocks, backward, fetched, x_ref, b_ref, c_ref, crow_ref, skip_ref, _, *rest):
    fetch_hbm, out_ref, fetch_vm, padded = (
        rest[:fetched], rest[fetched], rest[fetched + 1 : 2 * fetched + 1], rest[2 * fetched + 1]
    )
    copies = start(rest[2 * fetched + 2], *zip(fetch_hbm, fetch_vm)) if fetched else []
    half = GROUP // 2
    head_rows = crow_ref.shape[1]
    per = LANES // width
    part = lambda k: pl.ds(pl.multiple_of(k * GROUP, GROUP), GROUP)
    lane = iota((GROUP, LANES), 1)
    rows, cols = iota((GROUP, GROUP), 0), iota((GROUP, GROUP), 1)
    causal = (rows <= cols) if backward else (cols <= rows)
    padded[...] = jnp.zeros_like(padded)

    @pl.loop(0, blocks)
    def _(k):
        at = part(k)
        padded[0:head_rows, :] = crow_ref[k]
        col = padded[...].T
        docs_row = crow_ref[k, head_rows - 1 : head_rows, :]
        allowed = (col[:, head_rows - 1 : head_rows] == docs_row) & causal
        if backward:
            scores = dot(b_ref[at, :], c_ref[at, :], NT)
        else:
            scores = dot(c_ref[at, :], b_ref[at, :], NT)
        scores = jnp.where(allowed, scores, 0.0)
        for j in range(heads // per):
            cut = slice(j * LANES, (j + 1) * LANES)
            x = x_ref[at, cut]
            base = skip_ref[:, cut] * x.astype(F32)
            top, bottom = base[:half], base[half:]
            for i in range(per):
                h = j * per + i
                own = jnp.where(lane // width == i, x, jnp.zeros_like(x))
                at_row = crow_ref[k, h : h + 1, :]
                at_col = col[:, h : h + 1]

                def weights(r, c):
                    if backward:
                        gap = at_row[:, c] - at_col[r]
                    else:
                        gap = at_col[r] - at_row[:, c]
                    return (jnp.exp2(jnp.minimum(gap, 0.0)) * scores[r, c]).astype(BF16)

                low, high, both = slice(0, half), slice(half, GROUP), slice(0, GROUP)
                if backward:
                    top = top + dot(weights(low, both), own)
                    bottom = bottom + dot(weights(high, high), own[half:])
                else:
                    top = top + dot(weights(low, low), own[:half])
                    bottom = bottom + dot(weights(high, both), own)
            low_at = pl.ds(pl.multiple_of(k * GROUP, GROUP), half)
            high_at = pl.ds(pl.multiple_of(k * GROUP + half, half), half)
            out_ref[low_at, cut] = top.astype(BF16)
            out_ref[high_at, cut] = bottom.astype(BF16)

    for copy in copies:
        copy.wait()


def inside(x, write_keys, read_keys, crow, skip, heads, backward, after, fetch=()):
    tokens, inner = x.shape
    blocks = tokens // GROUP
    return call(
        functools.partial(inside_kernel, heads, inner // heads, blocks, backward, len(fetch)),
        "inside_backward" if backward else "inside_forward",
        [pltpu.VMEM((tokens, inner), BF16)] + [pltpu.VMEM(a.shape, a.dtype) for a in fetch],
        [VM] * 6 + [HB] * len(fetch),
        (x, write_keys, read_keys, crow, skip, after, *fetch),
        scratch=[pltpu.VMEM((LANES, GROUP), F32)]
        + ([pltpu.SemaphoreType.DMA((len(fetch),))] if fetch else []),
    )


def tiling(size):
    step = next(step for step in (512, 256, LANES, size) if size % step == 0)
    return [pl.ds(j * step, step) for j in range(size // step)]


def tail_kernel(
    items, chunk, places, mixed_ref, gates_ref, read_ref, entry_ref, local_ref,
    keep_ref, other_ref, pre_ref, spread_ref, w_ref, _, *rest
):
    outs, gated = rest[:-1], rest[-1]
    at_low = places[0] == 0
    keep, other = keep_ref[...].astype(F32), other_ref[...].astype(F32)
    state = jnp.concatenate(
        [jnp.where(at_low, keep, other), jnp.where(at_low, other, keep)], axis=0
    )
    for i, item in enumerate(items):
        at = pl.ds(pl.multiple_of(places[item] * chunk, chunk), chunk)
        k = places[item] * chunk // GROUP
        entering = (local_ref[k].astype(F32) + row_at(pre_ref[...], k) * state).astype(BF16)
        carried = dot(read_ref[at, :], entering) * dot(entry_ref[at, :], spread_ref[...])
        gated[i * chunk : (i + 1) * chunk, :] = (
            (mixed_ref[at, :].astype(F32) + carried) * silu(gates_ref[at, :])
        ).astype(BF16)
    for cut in tiling(w_ref.shape[1]):
        both = dot(gated[...], w_ref[:, cut]).astype(BF16)
        for i in range(len(items)):
            outs[i][:, cut] = both[i * chunk : (i + 1) * chunk]


def forward_tail(
    chunk, items, places, mixed, gates, read_keys, entry, local, keep, other, pre, spread, out_weight, after
):
    inner, width = out_weight.shape
    count = len(items)
    return call(
        functools.partial(tail_kernel, items, chunk),
        "forward_tail",
        [pltpu.VMEM((chunk, width), BF16)] * count,
        [SM] + [VM] * 11,
        (places, mixed, gates, read_keys, entry, local, keep, other, pre, spread, out_weight, after),
        scratch=[pltpu.VMEM((count * chunk, inner), BF16)],
    )


def grad_kernel(items, chunk, first, final, places, *refs):
    count = len(items)
    go_refs, refs = refs[:count], refs[count:]
    gates_ref, read_ref, entry_ref, pre_ref, spread_ref, w_ref, _ = refs[:7]
    refs = refs[7:]
    if not first:
        sum_in, refs = refs[0], refs[3:]
    mix_ref, states_ref = refs[:2]
    summed = None if first else sum_in[...]
    for i, item in enumerate(items):
        at = pl.ds(pl.multiple_of(places[item] * chunk, chunk), chunk)
        k = places[item] * chunk // GROUP
        for cut in tiling(w_ref.shape[0]):
            grad = dot(go_refs[i][...], w_ref[cut, :], NT)
            mix_ref[at, cut] = (grad * silu(gates_ref[at, cut])).astype(BF16)
        scaled = (dot(entry_ref[at, :], spread_ref[...]) * mix_ref[at, :].astype(F32)).astype(BF16)
        state = dot(read_ref[at, :], scaled, TN)
        states_ref[places[item]] = state.astype(BF16)
        part = row_at(pre_ref[...], k) * state
        summed = part if summed is None else summed + part
    if final:
        half = summed.shape[0] // 2
        at_low = places[0] == 0
        refs[2][...] = jnp.where(at_low, summed[:half], summed[half:]).astype(BF16)
        refs[3][...] = jnp.where(at_low, summed[half:], summed[:half]).astype(BF16)
    else:
        refs[2][...] = summed


def grad_chunks(
    chunk, items, places, arrived, gates, read_keys, entry, pre, spread, out_weight, earlier, final, after
):
    count = len(arrived)
    inner = out_weight.shape[0]
    tokens = gates.shape[0]
    n = read_keys.shape[1]
    first = earlier is None
    out_shape = [pltpu.VMEM((tokens, inner), BF16), pltpu.VMEM((tokens // chunk, n, inner), BF16)]
    out_shape += [pltpu.VMEM((n // 2, inner), BF16)] * 2 if final else [pltpu.VMEM((n, inner), F32)]
    at = 1 + count + 7
    return call(
        functools.partial(grad_kernel, items, chunk, first, final),
        "grad_chunks",
        out_shape,
        [SM] + [VM] * (count + 7 + (0 if first else 3)),
        (
            places, *arrived, gates, read_keys, entry, pre, spread, out_weight, after,
            *([] if first else (earlier[2], earlier[0], earlier[1])),
        ),
        aliases=None if first else {at + 1: 0, at + 2: 1},
    )


def back_kernel(
    blocks, places, part_ref, b_ref, exit_ref, states_ref, blk_ref, keep_ref, other_ref, spread_ref,
    out_hbm, running, out_ref, out_sems,
):
    half = keep_ref.shape[0]
    per = states_ref.shape[0] // blocks
    side = places[0]
    running[pl.ds(pl.multiple_of(side * half, half), half), :] = keep_ref[...].astype(F32)
    running[pl.ds(pl.multiple_of((1 - side) * half, half), half), :] = other_ref[...].astype(F32)
    outgoing = []
    for k in reversed(range(blocks)):
        at = pl.ds(k * GROUP, GROUP)
        carried = dot(b_ref[at, :], running[...].astype(BF16)) * dot(exit_ref[at, :], spread_ref[...])
        out_ref[at, :] = (part_ref[at, :].astype(F32) + carried).astype(BF16)
        outgoing += start(out_sems.at[k], (out_ref.at[at], out_hbm.at[at]))
        if k:
            state = states_ref[k * per].astype(F32)
            for i in range(1, per):
                state = state + states_ref[k * per + i].astype(F32)
            running[...] = state + blk_ref[k : k + 1, :] * running[...]
    for copy in outgoing:
        copy.wait()


def back_tail(places, part, write_keys, exit_w, states, blk, keep, other, spread):
    tokens, inner = part.shape
    n = write_keys.shape[1]
    blocks = tokens // GROUP
    return call(
        functools.partial(back_kernel, blocks),
        "back_tail",
        [pltpu.HBM((tokens, inner), BF16)],
        [SM] + [VM] * 8,
        (places, part, write_keys, exit_w, states, blk, keep, other, spread),
        scratch=[
            pltpu.VMEM((n, inner), F32),
            pltpu.VMEM((tokens, inner), BF16),
            pltpu.SemaphoreType.DMA((blocks, 1)),
        ],
    )[0]


def shifted(block, axis, distance):
    size = lax.axis_size(axis)
    route = [(i, i + distance) for i in range(size) if 0 <= i + distance < size]
    return lax.ppermute(block, axis, route)


def swapped(block, axis):
    return lax.ppermute(block, axis, [(i, i ^ 1) for i in range(lax.axis_size(axis))])


def rotated(block, axis, distance):
    size = lax.axis_size(axis)
    return lax.ppermute(block, axis, [(i, (i + distance) % size) for i in range(size)])


def pair_kernel(places, keep_ref, got_ref, info_ref, _, tagged_ref, near_ref, facts_ref):
    low = places[0] == 0
    pick = lambda own, mate: (jnp.where(low, own, mate), jnp.where(low, mate, own))
    got, mate_raw, mate_last, mate_first = untagged(got_ref[...])
    near, far = pick(keep_ref[...].astype(F32), got)
    near_raw, far_raw = pick(info_ref[0:1, :], mate_raw)
    near_last, far_last = pick(info_ref[1:2, :], mate_last)
    near_first, far_first = pick(info_ref[2:3, :], mate_first)
    far_live = (far_first == near_last).astype(F32)
    far_decay = jnp.where(far_last == far_first, far_raw, 0.0) * far_live
    near_decay = jnp.where(near_last == near_first, near_raw, 0.0)
    half = near.shape[0]
    tagged_ref[:half, :] = (far + far_decay * near).astype(BF16)
    tagged_ref[half:, :] = tags(far_decay * near_decay, far_last, near_first)
    near_ref[...] = near.astype(BF16)
    facts_ref[...] = jnp.concatenate(
        [near_decay, far_decay, far_live, near_first, jnp.zeros((4, near.shape[1]), F32)], axis=0
    )


def enter_kernel(places, near_ref, facts_ref, one_ref, two_ref, _, *rest):
    mine_ref, hers_ref, out_ref = rest[len(rest) // 2 - 1 :][:3]
    low = places[0] == 0
    one, one_decay, one_last, one_first = untagged(one_ref[...])
    two, _, two_last, _ = untagged(two_ref[...])
    facts = facts_ref[...]
    at_near = one + jnp.where(one_first == two_last, one_decay, 0.0) * two
    near_live = (facts[3:4] == one_last).astype(F32)
    near_decay, far_decay, far_live = facts[0:1] * near_live, facts[1:2], facts[2:3]
    at_far = (near_ref[...].astype(F32) + near_decay * at_near) * far_live
    at_near = at_near * near_live
    mine_ref[...] = jnp.where(low, at_near, at_far).astype(BF16)
    hers_ref[...] = jnp.where(low, at_far, at_near).astype(BF16)
    out_ref[...] = jnp.concatenate(
        [near_decay, far_decay, near_live, far_live, jnp.zeros((4, near_decay.shape[1]), F32)], axis=0
    )


def pair_back_kernel(places, keep_ref, got_ref, facts_ref, _, tagged_ref, near_ref):
    low = places[0] == 0
    facts = facts_ref[...]
    keep, got = keep_ref[...].astype(F32), got_ref[...].astype(F32)
    near = jnp.where(low, got, keep) * facts[3:4]
    far = jnp.where(low, keep, got) * facts[2:3]
    half = near.shape[0]
    one = jnp.ones_like(facts[0:1])
    tagged_ref[:half, :] = (far + facts[0:1] * near).astype(BF16)
    tagged_ref[half:, :] = tags(facts[0:1] * facts[1:2], one, one)
    near_ref[...] = near.astype(BF16)


def enter_back_kernel(places, near_ref, facts_ref, one_ref, two_ref, _, mine_ref, hers_ref):
    low = places[0] == 0
    one, one_decay, one_last, one_first = untagged(one_ref[...])
    two, _, two_last, _ = untagged(two_ref[...])
    at_near = one + jnp.where(one_first == two_last, one_decay, 0.0) * two
    at_far = near_ref[...].astype(F32) + facts_ref[1:2, :] * at_near
    mine_ref[...] = jnp.where(low, at_far, at_near).astype(BF16)
    hers_ref[...] = jnp.where(low, at_near, at_far).astype(BF16)


def small(kernel, name, shapes, args, after, through=()):
    out_shape = [pltpu.VMEM(dims, kind) for dims, kind in shapes]
    out_shape += [pltpu.VMEM(a.shape, a.dtype) for a in through]
    count = len(args) + 1
    return call(
        kernel, name, out_shape, [SM] + [VM] * (len(args) + len(through)), (*args, after, *through),
        aliases={count + i: len(shapes) + i for i in range(len(through))},
    )


def between_pairs(tagged, way):
    half = tagged.shape[0] - TILE
    window = max(lax.axis_size("seq") // 4, 1)
    if window <= 2:
        one = shifted(tagged, "seq", 2 * way)
        return one, shifted(tagged, "seq", 4 * way) if window == 2 else jnp.zeros_like(one)
    total, decay, _, first = untagged(tagged)
    came, _, came_last, _ = untagged(shifted(tagged, "seq", 2 * way))
    decay = jnp.where(first == came_last, decay, 0.0)
    total = (total + decay * came).astype(BF16)
    reach = 2
    while reach < window:
        decay = decay * shifted(decay, "seq", way * reach)
        total = (total.astype(F32) + decay * shifted(total, "seq", 2 * way * reach).astype(F32)).astype(BF16)
        reach *= 2
    one = shifted(jnp.concatenate([total, tagged[half:]], axis=0), "seq", 2 * way)
    return one, jnp.zeros_like(one)


def shards(
    inputs, gates, write_keys, read_keys, log_decay, skip_gain, doc_ids, out_weight, grad_out
):
    tokens, inner = inputs.shape
    heads = log_decay.shape[0]
    width = inner // heads
    members = lax.axis_size("head")
    chips = members // 2
    chunk = tokens // members
    here = lax.axis_index("head")
    chip, core = here // 2, here % 2
    mate = here ^ 1
    side = lax.axis_index("seq") % 2
    numbers = [here, mate]
    for d in range(1, chips):
        source = (here - 2 * d) % members
        target = ((chip + d) % chips) * 2
        numbers += [source, source ^ 1, target + 1 - core, target + core]
    places = jnp.stack([side] + numbers).astype(jnp.int32)

    remote = [rotated(grad_out, "head", 2 * d) for d in range(1, chips)]
    sibling = swapped(grad_out, "head")

    spread = (
        jnp.arange(LANES)[:, None] == (jnp.arange(inner) // width)[None, :]
    ).astype(BF16)
    skip = jnp.repeat(skip_gain, width)[None, :]
    crow, entry, exit_w, local, keep, send, pre, blk, info, x, b, c = local_states(
        places, inputs, write_keys, read_keys, log_decay, doc_ids[None, :], spread
    )
    half, tagged, facts_shape = keep.shape, send.shape, info.shape
    mixed, gates, weight, own_grad = inside(
        x, b, c, crow, skip, heads, False, send, (gates, out_weight, grad_out)
    )
    pair, near, facts = small(
        pair_kernel, "pair", [(tagged, BF16), (half, BF16), (facts_shape, F32)],
        (places, keep, swapped(send, "seq"), info), mixed,
    )
    one, two = between_pairs(pair, 1)

    def grads(items, arrived, earlier, final, after):
        return grad_chunks(
            chunk, items, places, arrived, gates, c, entry, pre, spread, weight, earlier, final, after
        )

    back = grads((1, 2), [own_grad, sibling], None, chips == 1, pair)
    enter_keep, hers, facts, *remote = small(
        enter_kernel, "enter", [(half, BF16), (half, BF16), (facts_shape, F32)],
        (places, near, facts, one, two), back[1], remote,
    )
    enter_other = swapped(hers, "seq")

    def tail(items, after):
        return forward_tail(
            chunk, items, places, mixed, gates, c, entry, local, enter_keep, enter_other, pre, spread,
            weight, after,
        )

    after = hers
    for d in range(chips - 1):
        relayed = swapped(remote[d], "head")
        back = grads((3 + 4 * d,), [remote[d]], back, False, after)
        back = grads((4 + 4 * d,), [relayed], back, d == chips - 2, back[1])
        after = back[1]
    mix, states, back_keep, back_send = back
    got = swapped(back_send, "seq")
    landed = []
    after = back_send
    for d in range(chips - 1):
        give, stay = tail((5 + 4 * d, 6 + 4 * d), after)
        both = (stay.astype(F32) + swapped(give, "head").astype(F32)).astype(BF16)
        landed.append(rotated(both, "head", 2 * (d + 1)))
        after = give
    pair, near = small(
        pair_back_kernel, "pair_back", [(tagged, BF16), (half, BF16)],
        (places, back_keep, got, facts), after,
    )
    one, two = between_pairs(pair, -1)
    give, stay = tail((2, 1), pair)
    arrive_keep, hers = small(
        enter_back_kernel, "enter_back", [(half, BF16), (half, BF16)],
        (places, near, facts, one, two), give,
    )
    arrive_other = swapped(hers, "seq")
    part = inside(mix, b, c, crow, skip, heads, True, hers)[0]
    out = stay.astype(F32) + swapped(give, "head").astype(F32)
    for block in landed:
        out = out + block.astype(F32)
    grad_inputs = back_tail(
        places, part, b, exit_w, states, blk, arrive_keep, arrive_other, spread
    )
    return out.astype(BF16), grad_inputs


def solution(mesh):
    in_specs = (
        P("seq", "head"),
        P("seq", "head"),
        P("seq", None),
        P("seq", None),
        P("head", "seq"),
        P("head"),
        P("seq"),
        P("head", None),
        P(("seq", "head"), None),
    )
    out_specs = (P(("seq", "head"), None), P("seq", "head"))
    return jax.shard_map(shards, mesh=mesh, in_specs=in_specs, out_specs=out_specs, check_vma=False)
```

time: 247 us -> 105 us (0.43)
  the two profiles are of different devices: /device:TPU:0 before, /device:TPU:16 now
where the time goes in v2:
time: 105 us
  Pallas kernels  47.1 us (45%)
  waiting for transfers between devices  28.7 us (27%)
  starting transfers between devices  15.9 us (15%)
  local copies, waits for them, and re-layouts  10 us (10%)
  other arithmetic  1.97 us (2%)
    pallas_call x13, Pallas kernels, call(): pl.pallas_call(kernel, in_specs=in_specs, out_specs=[VM if o.memory_space...  47.1 us
    ppermute x4, waiting for transfers between devices, shifted(): return lax.ppermute(block, axis, route)  19.2 us
    unnamed x37, local copies, waits for them, and re-layouts  9.81 us
    ppermute x4, starting transfers between devices, shifted(): return lax.ppermute(block, axis, route)  8.17 us
    ppermute x8, starting transfers between devices, swapped(): lax.ppermute(block, axis, [(i, i ^ 1) for i in range(lax.axis_size(axis))])  5.56 us
    ppermute x8, waiting for transfers between devices, swapped(): lax.ppermute(block, axis, [(i, i ^ 1) for i in range(lax.axis_size(axis))])  5.04 us
    ppermute x2, waiting for transfers between devices, rotated(): lax.ppermute(block, axis, [(i, (i + distance) % size) for i in range(size)])  4.48 us
    ppermute x2, starting transfers between devices, rotated(): lax.ppermute(block, axis, [(i, (i + distance) % size) for i in range(size)])  2.15 us
  transfers between devices with their start and end apart: 14, of which 6 were waited for; matrix products, arithmetic and copies ran while one was open for 1% of the time, Pallas kernels for 39%

profile of v2, /device:TPU:16, one launch (start us, length us, event | category | flops | bytes accessed | tf_op | source)
XLA Modules:
  0.0 104.7 jit_solution(4115720623241823051)
XLA Ops:
  0.7 1.6 %collective-permute-start.4 = (bf16[256,2560]{1,0:T(8,128)(2,1)}, bf16[256,2560]{1,0:T(8,128)(2,1)S(1)}, u32[]{:S(2)}, u32[]{:S(2)}) collective-permute-start(bf16[256,2560]{1,0:T(8,128)(2,1)} %rest_2_.1), channel_id=1, source_target_pairs={{0,2},{1,3},{2,0},{3,1},{4,6},{5,7},{6,4},{7,5},{8,10},{9,11},{10,... | collective-permute-start | bytes 3932168 | tf_op jit(solution)/shard_map/ppermute | solution.py:431
  3.1 5.8 %local_states.1 = (f32[4,24,256]{2,1,0:T(8,128)S(1)}, bf16[1024,128]{1,0:T(8,128)(2,1)S(1)}, bf16[1024,128]{1,0:T(8,128)(2,1)S(1)}, bf16[4,128,1280]{2,1,0:T(8,1...) custom-call(s32[7]{0:T(128)S(1)} %stack.31.places, ...), custom_call_target="tpu_custom_call" | custom-call | flops 1 | bytes 1 | tf_op jit(solution)/shard_map/local_states/pallas_call | solution.py:35
  8.9 1.5 %copy-done = bf16[1024,1280]{1,0:T(8,128)(2,1)} copy-done((bf16[1024,1280]{1,0:T(8,128)(2,1)}, bf16[1024,1280]{1,0:T(8,128)(2,1)S(1)}, u32[]{:S(2)}) %copy-start) | copy-done | bytes 2621464
  14.3 1.5 %collective-permute-start = (bf16[80,1280]{1,0:T(8,128)(2,1)}, bf16[80,1280]{1,0:T(8,128)(2,1)}, u32[]{:S(2)}, u32[]{:S(2)}) collective-permute-start(bf16[80,1280]{1,0:T(8,128)(2,1)} %get-tuple-element.47._), channel_id=1, source_target_pairs={{0,4},{4,0},{8,12},{12,8},{16,20},{20,16},{24,28},{28,24},{1,5},{5... | collective-permute-start | bytes 614408 | tf_op jit(solution)/shard_map/ppermute | solution.py:426
  16.0 1.7 %copy-done.1 = bf16[1024,1280]{1,0:T(8,128)(2,1)S(1)} copy-done((bf16[1024,1280]{1,0:T(8,128)(2,1)S(1)}, bf16[1024,1280]{1,0:T(8,128)(2,1)}, u32[]{:S(2)}) %copy-start.1) | copy-done | bytes 2621464
  19.6 6.7 %inside_forward.1 = (bf16[1024,1280]{1,0:T(8,128)(2,1)S(1)}, bf16[1024,1280]{1,0:T(8,128)(2,1)S(1)}, bf16[1280,2560]{1,0:T(8,128)(2,1)S(1)}, bf16[256,2560]{1,0:T(8,128)(2,1)S(1)}) custom-call(bf16[1024,1280]{1,0:T(8,128)(2,1)S(1)} %copy-done.1, bf16[1024,128]{1,0:T(8,128)(2,1)S(1)} %copy-done.3, ...), custom_call_target="tpu_custom_call" | custom-call | flops 1 | bytes 1 | tf_op jit(solution)/shard_map/inside_forward/pallas_call | solution.py:35
  27.4 1.3 %collective-permute-start.2 = (bf16[80,1280]{1,0:T(8,128)(2,1)S(1)}, bf16[80,1280]{1,0:T(8,128)(2,1)S(1)}, u32[]{:S(2)}, u32[]{:S(2)}) collective-permute-start(bf16[80,1280]{1,0:T(8,128)(2,1)S(1)} %get-tuple-element.56.refs_8_), channel_id=1, source_target_pairs={{0,16},{4,20},{8,24},{12,28},{1,17},{5,21},{9,25},{13,29},{2,18},{... | collective-permute-start | bytes 614408 | tf_op jit(solution)/shard_map/ppermute | solution.py:422
  28.7 3.7 %collective-permute-start.1 = (bf16[80,1280]{1,0:T(8,128)(2,1)S(1)}, bf16[80,1280]{1,0:T(8,128)(2,1)S(1)}, u32[]{:S(2)}, u32[]{:S(2)}) collective-permute-start(bf16[80,1280]{1,0:T(8,128)(2,1)S(1)} %get-tuple-element.56.refs_8_), channel_id=1, source_target_pairs={{0,8},{4,12},{8,16},{12,20},{16,24},{20,28},{1,9},{5,13},{9,17},{1... | collective-permute-start | bytes 614408 | tf_op jit(solution)/shard_map/ppermute | solution.py:422
  32.4 6.1 %grad_chunks.3 = (bf16[1024,1280]{1,0:T(8,128)(2,1)S(1)}, bf16[4,128,1280]{2,1,0:T(8,128)(2,1)S(1)}, f32[128,1280]{1,0:T(8,128)S(1)}) custom-call(s32[7]{0:T(128)S(1)} %stack.31.places, bf16[256,2560]{1,0:T(8,128)(2,1)S(1)} %get-tuple-element.57.refs_0_, bf16[256,2560]{1,0:T(8,128)(2,1)} %collective-permute-done.3.refs_1_, ...), custom_call_target="tpu_custom_call" | custom-call | flops 1 | bytes 1 | tf_op jit(solution)/shard_map/grad_chunks/pallas_call | solution.py:35
  38.5 7.4 %collective-permute-done.1.one_ref = bf16[80,1280]{1,0:T(8,128)(2,1)S(1)} collective-permute-done((bf16[80,1280]{1,0:T(8,128)(2,1)S(1)}, bf16[80,1280]{1,0:T(8,128)(2,1)S(1)}, u32[]{:S(2)}, u32[]{:S(2)}) %collective-permute-start.1) | collective-permute-done | bytes 204832 | tf_op jit(solution)/shard_map/ppermute | solution.py:422
  47.2 3.0 %grad_chunks.4 = (bf16[1024,1280]{1,0:T(8,128)(2,1)S(1)}, bf16[4,128,1280]{2,1,0:T(8,128)(2,1)S(1)}, f32[128,1280]{1,0:T(8,128)S(1)}) custom-call(s32[7]{0:T(128)S(1)} %stack.31.places, bf16[256,2560]{1,0:T(8,128)(2,1)S(1)} %get-tuple-element.63.refs_0_, ...), custom_call_target="tpu_custom_call", output_to_operand_aliasing={{0}: (10, {}), {1}: (11, {})} | custom-call | flops 1 | bytes 1 | tf_op jit(solution)/shard_map/grad_chunks/pallas_call | solution.py:35
  50.3 2.9 %grad_chunks.5 = (bf16[1024,1280]{1,0:T(8,128)(2,1)S(1)}, bf16[4,128,1280]{2,1,0:T(8,128)(2,1)S(1)}, bf16[64,1280]{1,0:T(8,128)(2,1)S(1)}, bf16[64,1280]{1,0:T(8,128)(2,1)S(1)}) custom-call(s32[7]{0:T(128)S(1)} %stack.31.places, bf16[256,2560]{1,0:T(8,128)(2,1)S(1)} %collective-permute-done.6.refs_0_, ...), custom_call_target="tpu_custom_call", output_to_operand_aliasing={{0}: (10, {}), {1}: (11, {})} | custom-call | flops 1 | bytes 1 | tf_op jit(solution)/shard_map/grad_chunks/pallas_call | solution.py:35
  53.3 5.3 %forward_tail.2 = (bf16[256,2560]{1,0:T(8,128)(2,1)S(1)}, bf16[256,2560]{1,0:T(8,128)(2,1)S(1)}) custom-call(s32[7]{0:T(128)S(1)} %stack.31.places, bf16[1024,1280]{1,0:T(8,128)(2,1)S(1)} %get-tuple-element.48._.mixed_ref, bf16[1024,1280]{1,0:T(8,128)(2,1)S(1)} %get-tuple-element.49.refs_2_.refs_1_.gates_ref, ...), custom_call_target="tpu_custom_call" | custom-call | flops 1 | bytes 1 | tf_op jit(solution)/shard_map/forward_tail/pallas_call | solution.py:35
  58.8 1.5 %collective-permute-start.7 = (bf16[64,1280]{1,0:T(8,128)(2,1)S(1)}, bf16[64,1280]{1,0:T(8,128)(2,1)S(1)}, u32[]{:S(2)}, u32[]{:S(2)}) collective-permute-start(bf16[64,1280]{1,0:T(8,128)(2,1)S(1)} %get-tuple-element.70._), channel_id=1, source_target_pairs={{0,4},{4,0},{8,12},{12,8},{16,20},{20,16},{24,28},{28,24},{1,5},{5... | collective-permute-start | bytes 491528 | tf_op jit(solution)/shard_map/ppermute | solution.py:426
  60.3 5.0 %collective-permute-done.7.got_ref = bf16[64,1280]{1,0:T(8,128)(2,1)S(1)} collective-permute-done((bf16[64,1280]{1,0:T(8,128)(2,1)S(1)}, bf16[64,1280]{1,0:T(8,128)(2,1)S(1)}, u32[]{:S(2)}, u32[]{:S(2)}) %collective-permute-start.7) | collective-permute-done | bytes 163872 | tf_op jit(solution)/shard_map/ppermute | solution.py:426
  65.9 5.5 %forward_tail.3 = (bf16[256,2560]{1,0:T(8,128)(2,1)S(1)}, bf16[256,2560]{1,0:T(8,128)(2,1)S(1)}) custom-call(s32[7]{0:T(128)S(1)} %stack.31.places, bf16[1024,1280]{1,0:T(8,128)(2,1)S(1)} %get-tuple-element.48._.mixed_ref, bf16[1024,1280]{1,0:T(8,128)(2,1)S(1)} %get-tuple-element.49.refs_2_.refs_1_.gates_ref, ...), custom_call_target="tpu_custom_call" | custom-call | flops 1 | bytes 1 | tf_op jit(solution)/shard_map/forward_tail/pallas_call | solution.py:35
  73.8 1.9 %collective-permute-start.11 = (bf16[80,1280]{1,0:T(8,128)(2,1)S(1)}, bf16[80,1280]{1,0:T(8,128)(2,1)S(1)}, u32[]{:S(2)}, u32[]{:S(2)}) collective-permute-start(bf16[80,1280]{1,0:T(8,128)(2,1)S(1)} %get-tuple-element.73._), channel_id=1, source_target_pairs={{8,0},{12,4},{16,8},{20,12},{24,16},{28,20},{9,1},{13,5},{17,9},{2... | collective-permute-start | bytes 614408 | tf_op jit(solution)/shard_map/ppermute | solution.py:422
  75.8 7.8 %collective-permute-done.12.two_ref = bf16[80,1280]{1,0:T(8,128)(2,1)S(1)} collective-permute-done((bf16[80,1280]{1,0:T(8,128)(2,1)S(1)}, bf16[80,1280]{1,0:T(8,128)(2,1)S(1)}, u32[]{:S(2)}, u32[]{:S(2)}) %collective-permute-start.12) | collective-permute-done | bytes 204832 | tf_op jit(solution)/shard_map/ppermute | solution.py:422
  83.6 4.0 %collective-permute-done.11.one_ref = bf16[80,1280]{1,0:T(8,128)(2,1)S(1)} collective-permute-done((bf16[80,1280]{1,0:T(8,128)(2,1)S(1)}, bf16[80,1280]{1,0:T(8,128)(2,1)S(1)}, u32[]{:S(2)}, u32[]{:S(2)}) %collective-permute-start.11) | collective-permute-done | bytes 204832 | tf_op jit(solution)/shard_map/ppermute | solution.py:422
  88.2 1.5 %collective-permute-start.13 = (bf16[64,1280]{1,0:T(8,128)(2,1)S(1)}, bf16[64,1280]{1,0:T(8,128)(2,1)S(1)}, u32[]{:S(2)}, u32[]{:S(2)}) collective-permute-start(bf16[64,1280]{1,0:T(8,128)(2,1)S(1)} %get-tuple-element.79._), channel_id=1, source_target_pairs={{0,4},{4,0},{8,12},{12,8},{16,20},{20,16},{24,28},{28,24},{1,5},{5... | collective-permute-start | bytes 491528 | tf_op jit(solution)/shard_map/ppermute | solution.py:426
  89.8 5.7 %inside_backward.1.part_ref = bf16[1024,1280]{1,0:T(8,128)(2,1)S(1)} custom-call(bf16[1024,1280]{1,0:T(8,128)(2,1)S(1)} %get-tuple-element.77.x_ref, bf16[1024,128]{1,0:T(8,128)(2,1)S(1)} %copy-done.4, bf16[1024,128]{1,0:T(8,128)(2,1)S(1)} %get-tuple-element.45.c_ref.refs_3_.refs_2_.read_ref, f32[4,24,256]{2,1,0:T(8,128)S(1)} %copy-done.7, ...), custom_call_target="tpu_custom_call" | custom-call | flops 1 | bytes 1 | tf_op jit(solution)/shard_map/inside_backward/pallas_call | solution.py:35
  95.5 3.2 %back_tail.1 = bf16[1024,1280]{1,0:T(8,128)(2,1)} custom-call(s32[7]{0:T(128)S(1)} %stack.31.places, bf16[1024,1280]{1,0:T(8,128)(2,1)S(1)} %inside_backward.1.part_ref, bf16[1024,128]{1,0:T(8,128)(2,1)S(1)} %copy-done.4, bf16[1024,128]{1,0:T(8,128)(2,1)S(1)} %copy-done.9, bf16[4,128,1280]{2,1,0:T(8,128)(2,1)S(1)} %get-tuple-element.81.states_ref, ...), custom_call_target="tpu_custom_call" | custom-call | flops 1 | bytes 1 | tf_op jit(solution)/shard_map/back_tail/pallas_call | solution.py:35
  98.7 4.5 %collective-permute-done.10 = bf16[256,2560]{1,0:T(8,128)(2,1)S(1)} collective-permute-done((bf16[256,2560]{1,0:T(8,128)(2,1)S(1)}, bf16[256,2560]{1,0:T(8,128)(2,1)S(1)}, u32[]{:S(2)}, u32[]{:S(2)}) %collective-permute-start.10) | collective-permute-done | bytes 1310752 | tf_op jit(solution)/shard_map/ppermute | solution.py:431
  103.2 1.5 %add_convert_fusion = bf16[256,2560]{1,0:T(8,128)(2,1)} fusion(bf16[256,2560]{1,0:T(8,128)(2,1)S(1)} %collective-permute-done.10, bf16[256,2560]{1,0:T(8,128)(2,1)S(1)} %collective-permute-done.8, bf16[256,2560]{1,0:T(8,128)(2,1)S(1)} %get-tuple-element.74), kind=kLoop, calls=%fused_computation | loop fusion | flops 3932160 | bytes 5242880 | tf_op jit(solution)/shard_map/convert_element_type | solution.py:615
  (61 shorter events, 13.3 us)
Async XLA Ops:
  0.6 31.7 %collective-permute-start.3 = (bf16[256,2560]{1,0:T(8,128)(2,1)}, bf16[256,2560]{1,0:T(8,128)(2,1)}, u32[]{:S(2)}, u32[]{:S(2)}) collective-permute-start(bf16[256,2560]{1,0:T(8,128)(2,1)} %rest_2_.1), channel_id=1, source_target_pairs={{0,1},{1,0},{2,3},{3,2},{4,5},{5,4},{6,7},{7,6},{8,9},{9,8},{10,11... | collective-permute-start | bytes 3932168 | tf_op jit(solution)/shard_map/ppermute | solution.py:426
  0.7 45.2 %collective-permute-start.4 = (bf16[256,2560]{1,0:T(8,128)(2,1)}, bf16[256,2560]{1,0:T(8,128)(2,1)S(1)}, u32[]{:S(2)}, u32[]{:S(2)}) collective-permute-start(bf16[256,2560]{1,0:T(8,128)(2,1)} %rest_2_.1), channel_id=1, source_target_pairs={{0,2},{1,3},{2,0},{3,1},{4,6},{5,7},{6,4},{7,5},{8,10},{9,11},{10,... | collective-permute-start | bytes 3932168 | tf_op jit(solution)/shard_map/ppermute | solution.py:431
  3.1 12.8 %copy-start.17 = (f32[20]{0:T(128)S(1)}, f32[20]{0:T(128)}, u32[]{:S(2)}) copy-start(f32[20]{0:T(128)} %param.14) | copy-start | bytes 244
  8.9 1.5 %copy-start = (bf16[1024,1280]{1,0:T(8,128)(2,1)}, bf16[1024,1280]{1,0:T(8,128)(2,1)S(1)}, u32[]{:S(2)}) copy-start(bf16[1024,1280]{1,0:T(8,128)(2,1)S(1)} %get-tuple-element.43.x_ref) | copy-start | bytes 7864324
  14.3 11.9 %collective-permute-start = (bf16[80,1280]{1,0:T(8,128)(2,1)}, bf16[80,1280]{1,0:T(8,128)(2,1)}, u32[]{:S(2)}, u32[]{:S(2)}) collective-permute-start(bf16[80,1280]{1,0:T(8,128)(2,1)} %get-tuple-element.47._), channel_id=1, source_target_pairs={{0,4},{4,0},{8,12},{12,8},{16,20},{20,16},{24,28},{28,24},{1,5},{5... | collective-permute-start | bytes 614408 | tf_op jit(solution)/shard_map/ppermute | solution.py:426
  16.0 1.7 %copy-start.1 = (bf16[1024,1280]{1,0:T(8,128)(2,1)S(1)}, bf16[1024,1280]{1,0:T(8,128)(2,1)}, u32[]{:S(2)}) copy-start(bf16[1024,1280]{1,0:T(8,128)(2,1)} %copy-done) | copy-start | bytes 7864324
  17.8 0.9 copy-start.3
  19.6 6.7 %copy-start.11 = (bf16[64,1280]{1,0:T(8,128)(2,1)S(1)}, bf16[64,1280]{1,0:T(8,128)(2,1)}, u32[]{:S(2)}) copy-start(bf16[64,1280]{1,0:T(8,128)(2,1)} %copy-done.10) | copy-start | bytes 491524
  19.6 6.7 %copy-start.15 = (f32[8,1280]{1,0:T(8,128)S(1)}, f32[8,1280]{1,0:T(8,128)}, u32[]{:S(2)}) copy-start(f32[8,1280]{1,0:T(8,128)} %copy-done.14) | copy-start | bytes 122884
  27.4 11.1 %collective-permute-start.2 = (bf16[80,1280]{1,0:T(8,128)(2,1)S(1)}, bf16[80,1280]{1,0:T(8,128)(2,1)S(1)}, u32[]{:S(2)}, u32[]{:S(2)}) collective-permute-start(bf16[80,1280]{1,0:T(8,128)(2,1)S(1)} %get-tuple-element.56.refs_8_), channel_id=1, source_target_pairs={{0,16},{4,20},{8,24},{12,28},{1,17},{5,21},{9,25},{13,29},{2,18},{... | collective-permute-start | bytes 614408 | tf_op jit(solution)/shard_map/ppermute | solution.py:422
  28.7 17.2 %collective-permute-start.1 = (bf16[80,1280]{1,0:T(8,128)(2,1)S(1)}, bf16[80,1280]{1,0:T(8,128)(2,1)S(1)}, u32[]{:S(2)}, u32[]{:S(2)}) collective-permute-start(bf16[80,1280]{1,0:T(8,128)(2,1)S(1)} %get-tuple-element.56.refs_8_), channel_id=1, source_target_pairs={{0,8},{4,12},{8,16},{12,20},{16,24},{20,28},{1,9},{5,13},{9,17},{1... | collective-permute-start | bytes 614408 | tf_op jit(solution)/shard_map/ppermute | solution.py:422
  46.6 3.7 %collective-permute-start.6 = (bf16[256,2560]{1,0:T(8,128)(2,1)S(1)}, bf16[256,2560]{1,0:T(8,128)(2,1)S(1)}, u32[]{:S(2)}, u32[]{:S(2)}) collective-permute-start(bf16[256,2560]{1,0:T(8,128)(2,1)S(1)} %get-tuple-element.63.refs_0_), channel_id=1, source_target_pairs={{0,1},{1,0},{2,3},{3,2},{4,5},{5,4},{6,7},{7,6},{8,9},{9,8},{10,11... | collective-permute-start | bytes 3932168 | tf_op jit(solution)/shard_map/ppermute | solution.py:426
  46.7 6.6 %collective-permute-start.5 = (bf16[64,1280]{1,0:T(8,128)(2,1)S(1)}, bf16[64,1280]{1,0:T(8,128)(2,1)S(1)}, u32[]{:S(2)}, u32[]{:S(2)}) collective-permute-start(bf16[64,1280]{1,0:T(8,128)(2,1)S(1)} %get-tuple-element.62.refs_7_), channel_id=1, source_target_pairs={{0,4},{4,0},{8,12},{12,8},{16,20},{20,16},{24,28},{28,24},{1,5},{5... | collective-permute-start | bytes 491528 | tf_op jit(solution)/shard_map/ppermute | solution.py:426
  58.6 13.0 %collective-permute-start.9 = (bf16[256,2560]{1,0:T(8,128)(2,1)S(1)}, bf16[256,2560]{1,0:T(8,128)(2,1)S(1)}, u32[]{:S(2)}, u32[]{:S(2)}) collective-permute-start(bf16[256,2560]{1,0:T(8,128)(2,1)S(1)} %get-tuple-element.72._), channel_id=1, source_target_pairs={{0,1},{1,0},{2,3},{3,2},{4,5},{5,4},{6,7},{7,6},{8,9},{9,8},{10,11... | collective-permute-start | bytes 3932168 | tf_op jit(solution)/shard_map/ppermute | solution.py:426
  58.8 6.5 %collective-permute-start.7 = (bf16[64,1280]{1,0:T(8,128)(2,1)S(1)}, bf16[64,1280]{1,0:T(8,128)(2,1)S(1)}, u32[]{:S(2)}, u32[]{:S(2)}) collective-permute-start(bf16[64,1280]{1,0:T(8,128)(2,1)S(1)} %get-tuple-element.70._), channel_id=1, source_target_pairs={{0,4},{4,0},{8,12},{12,8},{16,20},{20,16},{24,28},{28,24},{1,5},{5... | collective-permute-start | bytes 491528 | tf_op jit(solution)/shard_map/ppermute | solution.py:426
  71.5 27.2 %collective-permute-start.8 = (bf16[256,2560]{1,0:T(8,128)(2,1)S(1)}, bf16[256,2560]{1,0:T(8,128)(2,1)S(1)}, u32[]{:S(2)}, u32[]{:S(2)}) collective-permute-start(bf16[256,2560]{1,0:T(8,128)(2,1)S(1)} %get-tuple-element.75._), channel_id=1, source_target_pairs={{0,1},{1,0},{2,3},{3,2},{4,5},{5,4},{6,7},{7,6},{8,9},{9,8},{10,11... | collective-permute-start | bytes 3932168 | tf_op jit(solution)/shard_map/ppermute | solution.py:426
  71.9 17.9 %copy-start.4 = (bf16[1024,128]{1,0:T(8,128)(2,1)S(1)}, bf16[1024,128]{1,0:T(8,128)(2,1)}, u32[]{:S(2)}) copy-start(bf16[1024,128]{1,0:T(8,128)(2,1)} %copy-done.2) | copy-start | bytes 786436
  71.9 17.9 %copy-start.7 = (f32[4,24,256]{2,1,0:T(8,128)S(1)}, f32[4,24,256]{2,1,0:T(8,128)}, u32[]{:S(2)}) copy-start(f32[4,24,256]{2,1,0:T(8,128)} %copy-done.5) | copy-start | bytes 294916
  71.9 31.2 %collective-permute-start.10 = (bf16[256,2560]{1,0:T(8,128)(2,1)S(1)}, bf16[256,2560]{1,0:T(8,128)(2,1)S(1)}, u32[]{:S(2)}, u32[]{:S(2)}) collective-permute-start(bf16[256,2560]{1,0:T(8,128)(2,1)S(1)} %add_convert_fusion.1), channel_id=1, source_target_pairs={{0,2},{1,3},{2,0},{3,1},{4,6},{5,7},{6,4},{7,5},{8,10},{9,11},{10,... | collective-permute-start | bytes 3932168 | tf_op jit(solution)/shard_map/ppermute | solution.py:431
  72.5 11.0 %collective-permute-start.12 = (bf16[80,1280]{1,0:T(8,128)(2,1)S(1)}, bf16[80,1280]{1,0:T(8,128)(2,1)S(1)}, u32[]{:S(2)}, u32[]{:S(2)}) collective-permute-start(bf16[80,1280]{1,0:T(8,128)(2,1)S(1)} %get-tuple-element.73._), channel_id=1, source_target_pairs={{16,0},{20,4},{24,8},{28,12},{17,1},{21,5},{25,9},{29,13},{18,2},{... | collective-permute-start | bytes 614408 | tf_op jit(solution)/shard_map/ppermute | solution.py:422
  73.8 13.7 %collective-permute-start.11 = (bf16[80,1280]{1,0:T(8,128)(2,1)S(1)}, bf16[80,1280]{1,0:T(8,128)(2,1)S(1)}, u32[]{:S(2)}, u32[]{:S(2)}) collective-permute-start(bf16[80,1280]{1,0:T(8,128)(2,1)S(1)} %get-tuple-element.73._), channel_id=1, source_target_pairs={{8,0},{12,4},{16,8},{20,12},{24,16},{28,20},{9,1},{13,5},{17,9},{2... | collective-permute-start | bytes 614408 | tf_op jit(solution)/shard_map/ppermute | solution.py:422
  88.2 7.2 %collective-permute-start.13 = (bf16[64,1280]{1,0:T(8,128)(2,1)S(1)}, bf16[64,1280]{1,0:T(8,128)(2,1)S(1)}, u32[]{:S(2)}, u32[]{:S(2)}) collective-permute-start(bf16[64,1280]{1,0:T(8,128)(2,1)S(1)} %get-tuple-element.79._), channel_id=1, source_target_pairs={{0,4},{4,0},{8,12},{12,8},{16,20},{20,16},{24,28},{28,24},{1,5},{5... | collective-permute-start | bytes 491528 | tf_op jit(solution)/shard_map/ppermute | solution.py:426
  89.8 5.7 %copy-start.9 = (bf16[1024,128]{1,0:T(8,128)(2,1)S(1)}, bf16[1024,128]{1,0:T(8,128)(2,1)}, u32[]{:S(2)}) copy-start(bf16[1024,128]{1,0:T(8,128)(2,1)} %copy-done.8) | copy-start | bytes 786436
  89.8 5.7 %copy-start.13 = (f32[8,1280]{1,0:T(8,128)S(1)}, f32[8,1280]{1,0:T(8,128)}, u32[]{:S(2)}) copy-start(f32[8,1280]{1,0:T(8,128)} %copy-done.12) | copy-start | bytes 122884
  (8 other events, 5.5 us)

commit v3 on v2

--- a/solution.py
+++ b/solution.py
@@ -26,7 +26,7 @@
     return lax.dot_general(a, b, dims, preferred_element_type=F32)
 
 
-def call(kernel, name, out_shape, in_specs, args, limit_mib=16, scratch=(), aliases=None):
+def call(kernel, name, out_shape, in_specs, args, limit_mib=12, scratch=(), aliases=None, flops=1):
     space = {id(VM): pltpu.VMEM, id(HB): pltpu.HBM}
     args = [
         arg if spec is SM else pltpu.with_memory_space_constraint(arg, space[id(spec)])
@@ -40,7 +40,7 @@
         scratch_shapes=scratch,
         input_output_aliases=aliases or {},
         compiler_params=pltpu.CompilerParams(vmem_limit_bytes=limit_mib * 2**20),
-        cost_estimate=pl.CostEstimate(flops=1, bytes_accessed=1, transcendentals=0),
+        cost_estimate=pl.CostEstimate(flops=int(flops), bytes_accessed=1, transcendentals=0),
         name=name,
     )(*args)
 
@@ -75,7 +75,7 @@
 def state_kernel(
     heads, blocks, places, x_hbm, b_hbm, c_hbm, ld_hbm, doc_ref, spread_ref,
     crow_ref, entry_ref, exit_ref, local_ref, keep_ref, send_ref, pre_ref, blk_ref, info_ref,
-    x_ref, b_ref, c_ref, padded, running, ld_ref, sems,
+    b_ref, c_ref, padded, running, ld_ref, x_ref, sems,
 ):
     n, inner = running.shape
     half = n // 2
@@ -188,7 +188,6 @@
             pltpu.VMEM((block_rows, inner), F32),
             pltpu.VMEM((block_rows, inner), F32),
             pltpu.VMEM((8, inner), F32),
-            pltpu.VMEM((tokens, inner), BF16),
             pltpu.VMEM((tokens, n), BF16),
             pltpu.VMEM((tokens, n), BF16),
         ],
@@ -198,27 +197,44 @@
             pltpu.VMEM((LANES, GROUP), F32),
             pltpu.VMEM((n, inner), F32),
             pltpu.VMEM((heads, tokens), F32),
+            pltpu.VMEM((tokens, inner), BF16),
             pltpu.SemaphoreType.DMA((3 + blocks,)),
         ],
     )
 
 
-def inside_kernel(heads, width, blocks, backward, fetched, x_ref, b_ref, c_ref, crow_ref, skip_ref, _, *rest):
+def inside_kernel(
+    heads, width, blocks, backward, fetched, chips, which, places,
+    x_ref, b_ref, c_ref, crow_ref, skip_ref, _, *rest
+):
+    per_chip = blocks // chips
+    if backward and which[0]:
+        rest = rest[1:]
     fetch_hbm, out_ref, fetch_vm, padded = (
         rest[:fetched], rest[fetched], rest[fetched + 1 : 2 * fetched + 1], rest[2 * fetched + 1]
     )
-    copies = start(rest[2 * fetched + 2], *zip(fetch_hbm, fetch_vm)) if fetched else []
     half = GROUP // 2
     head_rows = crow_ref.shape[1]
     per = LANES // width
     part = lambda k: pl.ds(pl.multiple_of(k * GROUP, GROUP), GROUP)
+    copies = []
+    if not backward:
+        sems, x_sems, x_hbm, x_ref = *rest[2 * fetched + 2 : 2 * fetched + 4], x_ref, rest[-1]
+        incoming = lambda k: pltpu.make_async_copy(x_hbm.at[part(k)], x_ref.at[part(k)], x_sems.at[k])
+        for k in range(blocks):
+            incoming(k).start()
+        copies = start(sems, *zip(fetch_hbm, fetch_vm))
     lane = iota((GROUP, LANES), 1)
     rows, cols = iota((GROUP, GROUP), 0), iota((GROUP, GROUP), 1)
     causal = (rows <= cols) if backward else (cols <= rows)
     padded[...] = jnp.zeros_like(padded)
 
-    @pl.loop(0, blocks)
-    def _(k):
+    @pl.loop(which[0] * per_chip, which[1] * per_chip)
+    def _(step):
+        k = step
+        if backward:
+            turn = places[1] // 2 + step // per_chip
+            k = lax.rem(turn, chips) * per_chip + lax.rem(step, per_chip)
         at = part(k)
         padded[0:head_rows, :] = crow_ref[k]
         col = padded[...].T
@@ -229,6 +245,8 @@
         else:
             scores = dot(c_ref[at, :], b_ref[at, :], NT)
         scores = jnp.where(allowed, scores, 0.0)
+        if not backward:
+            incoming(k).wait()
         for j in range(heads // per):
             cut = slice(j * LANES, (j + 1) * LANES)
             x = x_ref[at, cut]
@@ -263,17 +281,27 @@
         copy.wait()
 
 
-def inside(x, write_keys, read_keys, crow, skip, heads, backward, after, fetch=()):
+def inside(places, x, write_keys, read_keys, crow, skip, heads, after, fetch=(), which=None, earlier=None):
     tokens, inner = x.shape
     blocks = tokens // GROUP
+    backward = which is not None
+    chips = lax.axis_size("head") // 2 if backward else 1
+    carried = [] if earlier is None else [earlier]
     return call(
-        functools.partial(inside_kernel, heads, inner // heads, blocks, backward, len(fetch)),
+        functools.partial(
+            inside_kernel, heads, inner // heads, blocks, backward, len(fetch), chips, which or (0, 1)
+        ),
         "inside_backward" if backward else "inside_forward",
         [pltpu.VMEM((tokens, inner), BF16)] + [pltpu.VMEM(a.shape, a.dtype) for a in fetch],
-        [VM] * 6 + [HB] * len(fetch),
-        (x, write_keys, read_keys, crow, skip, after, *fetch),
+        [SM] + [VM if backward else HB] + [VM] * (5 + len(carried)) + [HB] * len(fetch),
+        (places, x, write_keys, read_keys, crow, skip, after, *carried, *fetch),
         scratch=[pltpu.VMEM((LANES, GROUP), F32)]
-        + ([pltpu.SemaphoreType.DMA((len(fetch),))] if fetch else []),
+        + ([] if backward else [
+            pltpu.SemaphoreType.DMA((len(fetch),)),
+            pltpu.SemaphoreType.DMA((blocks,)),
+            pltpu.VMEM((tokens, inner), BF16),
+        ]),
+        aliases={7: 0} if carried else None,
     )
 
 
@@ -284,9 +312,10 @@
 
 def tail_kernel(
     items, chunk, places, mixed_ref, gates_ref, read_ref, entry_ref, local_ref,
-    keep_ref, other_ref, pre_ref, spread_ref, w_ref, _, *rest
+    keep_ref, other_ref, pre_ref, spread_ref, w_ref, *rest
 ):
-    outs, gated = rest[:-1], rest[-1]
+    cuts = tiling(w_ref.shape[1])
+    outs, gated = rest[len(rest) - 2 - len(cuts) : -1], rest[-1]
     at_low = places[0] == 0
     keep, other = keep_ref[...].astype(F32), other_ref[...].astype(F32)
     state = jnp.concatenate(
@@ -300,10 +329,10 @@
         gated[i * chunk : (i + 1) * chunk, :] = (
             (mixed_ref[at, :].astype(F32) + carried) * silu(gates_ref[at, :])
         ).astype(BF16)
-    for cut in tiling(w_ref.shape[1]):
+    for j, cut in enumerate(cuts):
         both = dot(gated[...], w_ref[:, cut]).astype(BF16)
-        for i in range(len(items)):
-            outs[i][:, cut] = both[i * chunk : (i + 1) * chunk]
+        outs[j][...] = both[:chunk]
+        outs[-1][:, cut] = both[chunk:]
 
 
 def forward_tail(
@@ -314,11 +343,40 @@
     return call(
         functools.partial(tail_kernel, items, chunk),
         "forward_tail",
-        [pltpu.VMEM((chunk, width), BF16)] * count,
-        [SM] + [VM] * 11,
-        (places, mixed, gates, read_keys, entry, local, keep, other, pre, spread, out_weight, after),
+        [pltpu.VMEM((chunk, cut.size), BF16) for cut in tiling(width)] + [pltpu.VMEM((chunk, width), BF16)],
+        [SM] + [VM] * (10 + len(after)),
+        (places, mixed, gates, read_keys, entry, local, keep, other, pre, spread, out_weight, *after),
         scratch=[pltpu.VMEM((count * chunk, inner), BF16)],
     )
+
+
+def sum_kernel(count, final, *refs):
+    stay_ref, piece_refs, landed_refs = refs[0], refs[1 : 1 + count], refs[1 + count : len(refs) - 1 - 2 * final]
+    out_ref = refs[-2] if final else refs[-1]
+    outgoing = []
+    for j, cut in enumerate(tiling(stay_ref.shape[1])):
+        total = stay_ref[:, cut].astype(F32) + piece_refs[j][...].astype(F32)
+        for ref in landed_refs:
+            total = total + ref[:, cut].astype(F32)
+        out_ref[:, cut] = total.astype(BF16)
+        if final:
+            outgoing += start(refs[-1].at[j], (out_ref.at[:, cut], refs[-3].at[:, cut]))
+    for copy in outgoing:
+        copy.wait()
+
+
+def chunk_sum(stay, pieces, landed=(), final=False):
+    make = pltpu.HBM if final else pltpu.VMEM
+    return call(
+        functools.partial(sum_kernel, len(pieces), final),
+        "chunk_sum",
+        [make(stay.shape, stay.dtype)],
+        [VM] * (1 + len(pieces) + len(landed)),
+        (stay, *pieces, *landed),
+        scratch=[
+            pltpu.VMEM(stay.shape, stay.dtype), pltpu.SemaphoreType.DMA((len(pieces), 1))
+        ] if final else (),
+    )[0]
 
 
 def grad_kernel(items, chunk, first, final, places, *refs):
@@ -451,8 +509,9 @@
     )
 
 
-def enter_kernel(places, near_ref, facts_ref, one_ref, two_ref, _, *rest):
-    mine_ref, hers_ref, out_ref = rest[len(rest) // 2 - 1 :][:3]
+def enter_kernel(through, places, near_ref, facts_ref, one_ref, two_ref, _, *rest):
+    copies = start(rest[-1], *zip(rest[:through], rest[through + 3 :])) if through else []
+    mine_ref, hers_ref, out_ref = rest[through : through + 3]
     low = places[0] == 0
     one, one_decay, one_last, one_first = untagged(one_ref[...])
     two, _, two_last, _ = untagged(two_ref[...])
@@ -467,9 +526,12 @@
     out_ref[...] = jnp.concatenate(
         [near_decay, far_decay, near_live, far_live, jnp.zeros((4, near_decay.shape[1]), F32)], axis=0
     )
-
-
-def pair_back_kernel(places, keep_ref, got_ref, facts_ref, _, tagged_ref, near_ref):
+    for copy in copies:
+        copy.wait()
+
+
+def pair_back_kernel(places, keep_ref, got_ref, facts_ref, _, *rest):
+    tagged_ref, near_ref = rest[len(rest) // 2 - 1 :][:2]
     low = places[0] == 0
     facts = facts_ref[...]
     keep, got = keep_ref[...].astype(F32), got_ref[...].astype(F32)
@@ -482,7 +544,8 @@
     near_ref[...] = near.astype(BF16)
 
 
-def enter_back_kernel(places, near_ref, facts_ref, one_ref, two_ref, _, mine_ref, hers_ref):
+def enter_back_kernel(places, near_ref, facts_ref, one_ref, two_ref, _, *rest):
+    mine_ref, hers_ref = rest[len(rest) // 2 - 1 :][:2]
     low = places[0] == 0
     one, one_decay, one_last, one_first = untagged(one_ref[...])
     two, _, two_last, _ = untagged(two_ref[...])
@@ -492,13 +555,15 @@
     hers_ref[...] = jnp.where(low, at_near, at_far).astype(BF16)
 
 
-def small(kernel, name, shapes, args, after, through=()):
+def small(kernel, name, shapes, args, after, through=(), kept=()):
     out_shape = [pltpu.VMEM(dims, kind) for dims, kind in shapes]
-    out_shape += [pltpu.VMEM(a.shape, a.dtype) for a in through]
-    count = len(args) + 1
+    out_shape += [pltpu.VMEM(a.shape, a.dtype) for a in (*through, *kept)]
+    count = 1 + len(args) + len(through)
     return call(
-        kernel, name, out_shape, [SM] + [VM] * (len(args) + len(through)), (*args, after, *through),
-        aliases={count + i: len(shapes) + i for i in range(len(through))},
+        kernel, name, out_shape, [SM] + [VM] * len(args) + [HB] * len(through) + [VM] * len(kept),
+        (*args, after, *through, *kept),
+        aliases={count + i: len(shapes) + i for i in range(len(kept))},
+        scratch=[pltpu.SemaphoreType.DMA((len(through),))] if through else (),
     )
 
 
@@ -548,12 +613,12 @@
         jnp.arange(LANES)[:, None] == (jnp.arange(inner) // width)[None, :]
     ).astype(BF16)
     skip = jnp.repeat(skip_gain, width)[None, :]
-    crow, entry, exit_w, local, keep, send, pre, blk, info, x, b, c = local_states(
+    crow, entry, exit_w, local, keep, send, pre, blk, info, b, c = local_states(
         places, inputs, write_keys, read_keys, log_decay, doc_ids[None, :], spread
     )
     half, tagged, facts_shape = keep.shape, send.shape, info.shape
     mixed, gates, weight, own_grad = inside(
-        x, b, c, crow, skip, heads, False, send, (gates, out_weight, grad_out)
+        places, inputs, b, c, crow, skip, heads, send, (gates, out_weight, grad_out)
     )
     pair, near, facts = small(
         pair_kernel, "pair", [(tagged, BF16), (half, BF16), (facts_shape, F32)],
@@ -567,52 +632,52 @@
         )
 
     back = grads((1, 2), [own_grad, sibling], None, chips == 1, pair)
+    part = inside(places, back[0], b, c, crow, skip, heads, back[1], which=(0, 1))[0]
     enter_keep, hers, facts, *remote = small(
-        enter_kernel, "enter", [(half, BF16), (half, BF16), (facts_shape, F32)],
-        (places, near, facts, one, two), back[1], remote,
+        functools.partial(enter_kernel, len(remote)), "enter", [(half, BF16), (half, BF16), (facts_shape, F32)],
+        (places, near, facts, one, two), part, remote,
     )
     enter_other = swapped(hers, "seq")
 
-    def tail(items, after):
+    def tail(items, *after):
         return forward_tail(
             chunk, items, places, mixed, gates, c, entry, local, enter_keep, enter_other, pre, spread,
             weight, after,
         )
 
-    after = hers
     for d in range(chips - 1):
         relayed = swapped(remote[d], "head")
-        back = grads((3 + 4 * d,), [remote[d]], back, False, after)
+        back = grads((3 + 4 * d,), [remote[d]], back, False, hers)
         back = grads((4 + 4 * d,), [relayed], back, d == chips - 2, back[1])
-        after = back[1]
     mix, states, back_keep, back_send = back
     got = swapped(back_send, "seq")
-    landed = []
-    after = back_send
+    after, given, stayed = back_send, [], []
     for d in range(chips - 1):
-        give, stay = tail((5 + 4 * d, 6 + 4 * d), after)
-        both = (stay.astype(F32) + swapped(give, "head").astype(F32)).astype(BF16)
-        landed.append(rotated(both, "head", 2 * (d + 1)))
-        after = give
-    pair, near = small(
+        *give, after = tail((5 + 4 * d, 6 + 4 * d), after)
+        given += give
+        stayed.append(after)
+    pair, near, *given = small(
         pair_back_kernel, "pair_back", [(tagged, BF16), (half, BF16)],
-        (places, back_keep, got, facts), after,
+        (places, back_keep, got, facts), after, kept=given,
     )
     one, two = between_pairs(pair, -1)
-    give, stay = tail((2, 1), pair)
-    arrive_keep, hers = small(
+    landed, pieces = [], len(given) // max(chips - 1, 1)
+    for d in range(chips - 1):
+        got = [swapped(piece, "head") for piece in given[d * pieces : (d + 1) * pieces]]
+        after = chunk_sum(stayed[d], got)
+        landed.append(rotated(after, "head", 2 * (d + 1)))
+    *give, stay = tail((2, 1), pair, after)
+    part = inside(places, mix, b, c, crow, skip, heads, stay, which=(1, chips), earlier=part)[0]
+    arrive_keep, hers, *give = small(
         enter_back_kernel, "enter_back", [(half, BF16), (half, BF16)],
-        (places, near, facts, one, two), give,
+        (places, near, facts, one, two), part, kept=give,
     )
     arrive_other = swapped(hers, "seq")
-    part = inside(mix, b, c, crow, skip, heads, True, hers)[0]
-    out = stay.astype(F32) + swapped(give, "head").astype(F32)
-    for block in landed:
-        out = out + block.astype(F32)
+    out = chunk_sum(stay, [swapped(piece, "head") for piece in give], landed, True)
     grad_inputs = back_tail(
         places, part, b, exit_w, states, blk, arrive_keep, arrive_other, spread
     )
-    return out.astype(BF16), grad_inputs
+    return out, grad_inputs
 
 
 def solution(mesh):

time: 105 us -> 88.8 us (0.85)
  the two profiles are of different devices: /device:TPU:16 before, /device:TPU:0 now
where the time goes in v3:
time: 88.8 us; the launch traced here: 88.5 us
  Pallas kernels  50.1 us (56%)
  starting transfers between devices  21.6 us (24%)
  waiting for transfers between devices  14.7 us (17%)
  between operations  1.1 us (1%)
  local copies, waits for them, and re-layouts  1.01 us (1%)
    pallas_call x16, Pallas kernels, call(): pl.pallas_call(kernel, in_specs=in_specs, out_specs=[VM if o.memory_space...  50.1 us
    ppermute x4, starting transfers between devices, shifted(): return lax.ppermute(block, axis, route)  10.8 us
    ppermute x16, starting transfers between devices, swapped(): lax.ppermute(block, axis, [(i, i ^ 1) for i in range(lax.axis_size(axis))])  7.59 us
    ppermute x16, waiting for transfers between devices, swapped(): lax.ppermute(block, axis, [(i, i ^ 1) for i in range(lax.axis_size(axis))])  7.05 us
    ppermute x2, waiting for transfers between devices, rotated(): lax.ppermute(block, axis, [(i, (i + distance) % size) for i in range(size)])  4.15 us
    ppermute x4, waiting for transfers between devices, shifted(): return lax.ppermute(block, axis, route)  3.54 us
    ppermute x2, starting transfers between devices, rotated(): lax.ppermute(block, axis, [(i, (i + distance) % size) for i in range(size)])  3.17 us
  transfers between devices with their start and end apart: 22, of which 8 were waited for; matrix products, arithmetic and copies ran while one was open for 0% of the time, Pallas kernels for 52%

profile of v3, /device:TPU:0, one launch (start us, length us, event | category | flops | bytes accessed | tf_op | source)
XLA Modules:
  0.0 88.5 jit_solution(16318508612611636874)
XLA Ops:
  1.1 2.6 %collective-permute-start.4 = (bf16[256,2560]{1,0:T(8,128)(2,1)}, bf16[256,2560]{1,0:T(8,128)(2,1)}, u32[]{:S(2)}, u32[]{:S(2)}) collective-permute-start(bf16[256,2560]{1,0:T(8,128)(2,1)} %rest_2_.1), channel_id=1, source_target_pairs={{0,2},{1,3},{2,0},{3,1},{4,6},{5,7},{6,4},{7,5},{8,10},{9,11},{10,... | collective-permute-start | bytes 3932168 | tf_op jit(solution)/shard_map/ppermute | solution.py:489
  4.6 5.1 %local_states.1 = (f32[4,24,256]{2,1,0:T(8,128)S(1)}, bf16[1024,128]{1,0:T(8,128)(2,1)S(1)}, bf16[1024,128]{1,0:T(8,128)(2,1)S(1)}, bf16[4,128,1280]{2,1,0:T(8,1...) custom-call(s32[7]{0:T(128)S(1)} %stack.31.places, ...), custom_call_target="tpu_custom_call" | custom-call | flops 1 | bytes 1 | tf_op jit(solution)/shard_map/local_states/pallas_call | solution.py:35
  9.6 1.6 %collective-permute-start = (bf16[80,1280]{1,0:T(8,128)(2,1)S(1)}, bf16[80,1280]{1,0:T(8,128)(2,1)S(1)}, u32[]{:S(2)}, u32[]{:S(2)}) collective-permute-start(bf16[80,1280]{1,0:T(8,128)(2,1)S(1)} %get-tuple-element.63._), channel_id=1, source_target_pairs={{0,4},{4,0},{8,12},{12,8},{16,20},{20,16},{24,28},{28,24},{1,5},{5... | collective-permute-start | bytes 614408 | tf_op jit(solution)/shard_map/ppermute | solution.py:484
  11.4 7.0 %inside_forward.1 = (bf16[1024,1280]{1,0:T(8,128)(2,1)S(1)}, bf16[1024,1280]{1,0:T(8,128)(2,1)S(1)}, bf16[1280,2560]{1,0:T(8,128)(2,1)S(1)}, bf16[256,2560]{1,0:T(8,128)(2,1)S(1)}) custom-call(s32[7]{0:T(128)S(1)} %stack.31.places, bf16[1024,1280]{1,0:T(8,128)(2,1)} %x_ref.1, bf16[1024,128]{1,0:T(8,128)(2,1)S(1)} %get-tuple-element.60.b_ref, ...), custom_call_target="tpu_custom_call" | custom-call | flops 1 | bytes 1 | tf_op jit(solution)/shard_map/inside_forward/pallas_call | solution.py:35
  18.5 0.7 pair.1
  19.1 4.5 %collective-permute-start.2 = (bf16[80,1280]{1,0:T(8,128)(2,1)S(1)}, bf16[80,1280]{1,0:T(8,128)(2,1)S(1)}, u32[]{:S(2)}, u32[]{:S(2)}) collective-permute-start(bf16[80,1280]{1,0:T(8,128)(2,1)S(1)} %get-tuple-element.72.refs_8_), channel_id=1, source_target_pairs={{0,16},{4,20},{8,24},{12,28},{1,17},{5,21},{9,25},{13,29},{2,18},{... | collective-permute-start | bytes 614408 | tf_op jit(solution)/shard_map/ppermute | solution.py:480
  23.7 3.5 %collective-permute-start.1 = (bf16[80,1280]{1,0:T(8,128)(2,1)S(1)}, bf16[80,1280]{1,0:T(8,128)(2,1)S(1)}, u32[]{:S(2)}, u32[]{:S(2)}) collective-permute-start(bf16[80,1280]{1,0:T(8,128)(2,1)S(1)} %get-tuple-element.72.refs_8_), channel_id=1, source_target_pairs={{0,8},{4,12},{8,16},{12,20},{16,24},{20,28},{1,9},{5,13},{9,17},{1... | collective-permute-start | bytes 614408 | tf_op jit(solution)/shard_map/ppermute | solution.py:480
  27.2 6.1 %grad_chunks.3 = (bf16[1024,1280]{1,0:T(8,128)(2,1)S(1)}, bf16[4,128,1280]{2,1,0:T(8,128)(2,1)S(1)}, f32[128,1280]{1,0:T(8,128)S(1)}) custom-call(s32[7]{0:T(128)S(1)} %stack.31.places, bf16[256,2560]{1,0:T(8,128)(2,1)S(1)} %get-tuple-element.73.refs_0_, bf16[256,2560]{1,0:T(8,128)(2,1)} %collective-permute-done.3.refs_1_, ...), custom_call_target="tpu_custom_call" | custom-call | flops 1 | bytes 1 | tf_op jit(solution)/shard_map/grad_chunks/pallas_call | solution.py:35
  33.2 3.5 %inside_backward.2._.rest_0_ = bf16[1024,1280]{1,0:T(8,128)(2,1)S(1)} custom-call(s32[7]{0:T(128)S(1)} %stack.31.places, bf16[1024,1280]{1,0:T(8,128)(2,1)S(1)} %get-tuple-element.76.x_ref.refs_9_, bf16[1024,128]{1,0:T(8,128)(2,1)S(1)} %get-tuple-element.60.b_ref, bf16[1024,128]{1,0:T(8,128)(2,1)S(1)} %get-tuple-element.61.c_ref.refs_3_.refs_2_.read_ref, ...), custom_call_target="tpu_custom_call" | custom-call | flops 1 | bytes 1 | tf_op jit(solution)/shard_map/inside_backward/pallas_call | solution.py:35
  36.8 1.9 %enter.1 = (bf16[64,1280]{1,0:T(8,128)(2,1)S(1)}, bf16[64,1280]{1,0:T(8,128)(2,1)S(1)}, f32[8,1280]{1,0:T(8,128)S(1)}, bf16[256,2560]{1,0:T(8,128)(2,1)S(1)}) custom-call(s32[7]{0:T(128)S(1)} %stack.31.places, bf16[64,1280]{1,0:T(8,128)(2,1)S(1)} %get-tuple-element.70.near_ref, f32[8,1280]{1,0:T(8,128)S(1)} %get-tuple-element.71.facts_ref, ...), custom_call_target="tpu_custom_call" | custom-call | flops 1 | bytes 1 | tf_op jit(solution)/shard_map/enter/pallas_call | solution.py:35
  39.4 2.9 %grad_chunks.4 = (bf16[1024,1280]{1,0:T(8,128)(2,1)S(1)}, bf16[4,128,1280]{2,1,0:T(8,128)(2,1)S(1)}, f32[128,1280]{1,0:T(8,128)S(1)}) custom-call(s32[7]{0:T(128)S(1)} %stack.31.places, bf16[256,2560]{1,0:T(8,128)(2,1)S(1)} %get-tuple-element.80.refs_0_, ...), custom_call_target="tpu_custom_call", output_to_operand_aliasing={{0}: (10, {}), {1}: (11, {})} | custom-call | flops 1 | bytes 1 | tf_op jit(solution)/shard_map/grad_chunks/pallas_call | solution.py:35
  42.4 2.9 %grad_chunks.5 = (bf16[1024,1280]{1,0:T(8,128)(2,1)S(1)}, bf16[4,128,1280]{2,1,0:T(8,128)(2,1)S(1)}, bf16[64,1280]{1,0:T(8,128)(2,1)S(1)}, bf16[64,1280]{1,0:T(8,128)(2,1)S(1)}) custom-call(s32[7]{0:T(128)S(1)} %stack.31.places, bf16[256,2560]{1,0:T(8,128)(2,1)S(1)} %collective-permute-done.6.refs_0_, ...), custom_call_target="tpu_custom_call", output_to_operand_aliasing={{0}: (10, {}), {1}: (11, {})} | custom-call | flops 1 | bytes 1 | tf_op jit(solution)/shard_map/grad_chunks/pallas_call | solution.py:35
  45.3 1.6 %collective-permute-start.7 = (bf16[64,1280]{1,0:T(8,128)(2,1)S(1)}, bf16[64,1280]{1,0:T(8,128)(2,1)S(1)}, u32[]{:S(2)}, u32[]{:S(2)}) collective-permute-start(bf16[64,1280]{1,0:T(8,128)(2,1)S(1)} %get-tuple-element.86.rest_0_), channel_id=1, source_target_pairs={{0,4},{4,0},{8,12},{12,8},{16,20},{20,16},{24,28},{28,24},{1,5},{5... | collective-permute-start | bytes 491528 | tf_op jit(solution)/shard_map/ppermute | solution.py:484
  46.9 5.3 %forward_tail.2 = (bf16[256,512]{1,0:T(8,128)(2,1)S(1)}, bf16[256,512]{1,0:T(8,128)(2,1)S(1)}, bf16[256,512]{1,0:T(8,128)(2,1)S(1)}, bf16[256,512]{1,0:T(8,128)(...) custom-call(s32[7]{0:T(128)S(1)} %stack.31.places, ...), custom_call_target="tpu_custom_call" | custom-call | flops 1 | bytes 1 | tf_op jit(solution)/shard_map/forward_tail/pallas_call | solution.py:35
  56.9 1.3 %collective-permute-start.14 = (bf16[80,1280]{1,0:T(8,128)(2,1)S(1)}, bf16[80,1280]{1,0:T(8,128)(2,1)S(1)}, u32[]{:S(2)}, u32[]{:S(2)}) collective-permute-start(bf16[80,1280]{1,0:T(8,128)(2,1)S(1)} %get-tuple-element.94.rest_0_), channel_id=1, source_target_pairs={{16,0},{20,4},{24,8},{28,12},{17,1},{21,5},{25,9},{29,13},{18,2},{... | collective-permute-start | bytes 614408 | tf_op jit(solution)/shard_map/ppermute | solution.py:480
  58.1 1.5 %collective-permute-start.13 = (bf16[80,1280]{1,0:T(8,128)(2,1)S(1)}, bf16[80,1280]{1,0:T(8,128)(2,1)S(1)}, u32[]{:S(2)}, u32[]{:S(2)}) collective-permute-start(bf16[80,1280]{1,0:T(8,128)(2,1)S(1)} %get-tuple-element.94.rest_0_), channel_id=1, source_target_pairs={{8,0},{12,4},{16,8},{20,12},{24,16},{28,20},{9,1},{13,5},{17,9},{2... | collective-permute-start | bytes 614408 | tf_op jit(solution)/shard_map/ppermute | solution.py:480
  59.7 5.3 %forward_tail.3 = (bf16[256,512]{1,0:T(8,128)(2,1)S(1)}, bf16[256,512]{1,0:T(8,128)(2,1)S(1)}, bf16[256,512]{1,0:T(8,128)(2,1)S(1)}, bf16[256,512]{1,0:T(8,128)(...) custom-call(s32[7]{0:T(128)S(1)} %stack.31.places, ...), custom_call_target="tpu_custom_call" | custom-call | flops 1 | bytes 1 | tf_op jit(solution)/shard_map/forward_tail/pallas_call | solution.py:35
  65.0 3.4 %inside_backward.3._.part_ref = bf16[1024,1280]{1,0:T(8,128)(2,1)S(1)} custom-call(s32[7]{0:T(128)S(1)} %stack.31.places, bf16[1024,1280]{1,0:T(8,128)(2,1)S(1)} %get-tuple-element.102.x_ref, bf16[1024,128]{1,0:T(8,128)(2,1)S(1)} %get-tuple-element.60.b_ref, ...), custom_call_target="tpu_custom_call", output_to_operand_aliasing={{}: (7, {})} | custom-call | flops 1 | bytes 1 | tf_op jit(solution)/shard_map/inside_backward/pallas_call | solution.py:35
  68.3 3.5 %collective-permute-done.14.two_ref = bf16[80,1280]{1,0:T(8,128)(2,1)S(1)} collective-permute-done((bf16[80,1280]{1,0:T(8,128)(2,1)S(1)}, bf16[80,1280]{1,0:T(8,128)(2,1)S(1)}, u32[]{:S(2)}, u32[]{:S(2)}) %collective-permute-start.14) | collective-permute-done | bytes 204832 | tf_op jit(solution)/shard_map/ppermute | solution.py:480
  72.6 1.0 %collective-permute-start.21 = (bf16[64,1280]{1,0:T(8,128)(2,1)S(1)}, bf16[64,1280]{1,0:T(8,128)(2,1)S(1)}, u32[]{:S(2)}, u32[]{:S(2)}) collective-permute-start(bf16[64,1280]{1,0:T(8,128)(2,1)S(1)} %get-tuple-element.117), channel_id=1, source_target_pairs={{0,4},{4,0},{8,12},{12,8},{16,20},{20,16},{24,28},{28,24},{1,5},{5... | collective-permute-start | bytes 491528 | tf_op jit(solution)/shard_map/ppermute | solution.py:484
  74.1 5.1 %collective-permute-done.21.other_ref = bf16[64,1280]{1,0:T(8,128)(2,1)S(1)} collective-permute-done((bf16[64,1280]{1,0:T(8,128)(2,1)S(1)}, bf16[64,1280]{1,0:T(8,128)(2,1)S(1)}, u32[]{:S(2)}, u32[]{:S(2)}) %collective-permute-start.21) | collective-permute-done | bytes 163872 | tf_op jit(solution)/shard_map/ppermute | solution.py:484
  79.8 3.2 %back_tail.1 = bf16[1024,1280]{1,0:T(8,128)(2,1)} custom-call(s32[7]{0:T(128)S(1)} %stack.31.places, bf16[1024,1280]{1,0:T(8,128)(2,1)S(1)} %inside_backward.3._.part_ref, bf16[1024,128]{1,0:T(8,128)(2,1)S(1)} %get-tuple-element.60.b_ref, bf16[1024,128]{1,0:T(8,128)(2,1)S(1)} %get-tuple-element.113.exit_ref, ...), custom_call_target="tpu_custom_call" | custom-call | flops 1 | bytes 1 | tf_op jit(solution)/shard_map/back_tail/pallas_call | solution.py:35
  83.0 4.1 %collective-permute-done.20.refs_6_ = bf16[256,2560]{1,0:T(8,128)(2,1)S(1)} collective-permute-done((bf16[256,2560]{1,0:T(8,128)(2,1)S(1)}, bf16[256,2560]{1,0:T(8,128)(2,1)S(1)}, u32[]{:S(2)}, u32[]{:S(2)}) %collective-permute-start.20) | collective-permute-done | bytes 1310752 | tf_op jit(solution)/shard_map/ppermute | solution.py:489
  87.1 1.2 %chunk_sum.3 = bf16[256,2560]{1,0:T(8,128)(2,1)} custom-call(bf16[256,2560]{1,0:T(8,128)(2,1)S(1)} %get-tuple-element.100._.refs_0_, bf16[256,512]{1,0:T(8,128)(2,1)S(1)} %collective-permute-done.15.refs_1_, bf16[256,512]{1,0:T(8,128)(2,1)S(1)} %collective-permute-done.16.refs_2_, bf16[256,512]{1,0:T(8,128)(2,1)S(1)} %collective-permute-done.17.refs_3_, ...), custom_call_target="tpu_custom_call" | custom-call | flops 1 | bytes 1 | tf_op jit(solution)/shard_map/chunk_sum/pallas_call | solution.py:35
  (46 shorter events, 8.7 us)
Async XLA Ops:
  0.6 26.5 %collective-permute-start.3 = (bf16[256,2560]{1,0:T(8,128)(2,1)}, bf16[256,2560]{1,0:T(8,128)(2,1)}, u32[]{:S(2)}, u32[]{:S(2)}) collective-permute-start(bf16[256,2560]{1,0:T(8,128)(2,1)} %rest_2_.1), channel_id=1, source_target_pairs={{0,1},{1,0},{2,3},{3,2},{4,5},{5,4},{6,7},{7,6},{8,9},{9,8},{10,11... | collective-permute-start | bytes 3932168 | tf_op jit(solution)/shard_map/ppermute | solution.py:484
  1.1 35.7 %collective-permute-start.4 = (bf16[256,2560]{1,0:T(8,128)(2,1)}, bf16[256,2560]{1,0:T(8,128)(2,1)}, u32[]{:S(2)}, u32[]{:S(2)}) collective-permute-start(bf16[256,2560]{1,0:T(8,128)(2,1)} %rest_2_.1), channel_id=1, source_target_pairs={{0,2},{1,3},{2,0},{3,1},{4,6},{5,7},{6,4},{7,5},{8,10},{9,11},{10,... | collective-permute-start | bytes 3932168 | tf_op jit(solution)/shard_map/ppermute | solution.py:489
  3.9 0.7 copy-start
  4.6 6.7 %copy-start.1 = (f32[20]{0:T(128)S(1)}, f32[20]{0:T(128)}, u32[]{:S(2)}) copy-start(f32[20]{0:T(128)} %param.14) | copy-start | bytes 244
  9.6 8.8 %collective-permute-start = (bf16[80,1280]{1,0:T(8,128)(2,1)S(1)}, bf16[80,1280]{1,0:T(8,128)(2,1)S(1)}, u32[]{:S(2)}, u32[]{:S(2)}) collective-permute-start(bf16[80,1280]{1,0:T(8,128)(2,1)S(1)} %get-tuple-element.63._), channel_id=1, source_target_pairs={{0,4},{4,0},{8,12},{12,8},{16,20},{20,16},{24,28},{28,24},{1,5},{5... | collective-permute-start | bytes 614408 | tf_op jit(solution)/shard_map/ppermute | solution.py:484
  19.1 17.7 %collective-permute-start.2 = (bf16[80,1280]{1,0:T(8,128)(2,1)S(1)}, bf16[80,1280]{1,0:T(8,128)(2,1)S(1)}, u32[]{:S(2)}, u32[]{:S(2)}) collective-permute-start(bf16[80,1280]{1,0:T(8,128)(2,1)S(1)} %get-tuple-element.72.refs_8_), channel_id=1, source_target_pairs={{0,16},{4,20},{8,24},{12,28},{1,17},{5,21},{9,25},{13,29},{2,18},{... | collective-permute-start | bytes 614408 | tf_op jit(solution)/shard_map/ppermute | solution.py:480
  23.7 13.1 %collective-permute-start.1 = (bf16[80,1280]{1,0:T(8,128)(2,1)S(1)}, bf16[80,1280]{1,0:T(8,128)(2,1)S(1)}, u32[]{:S(2)}, u32[]{:S(2)}) collective-permute-start(bf16[80,1280]{1,0:T(8,128)(2,1)S(1)} %get-tuple-element.72.refs_8_), channel_id=1, source_target_pairs={{0,8},{4,12},{8,16},{12,20},{16,24},{20,28},{1,9},{5,13},{9,17},{1... | collective-permute-start | bytes 614408 | tf_op jit(solution)/shard_map/ppermute | solution.py:480
  38.7 3.6 %collective-permute-start.6 = (bf16[256,2560]{1,0:T(8,128)(2,1)S(1)}, bf16[256,2560]{1,0:T(8,128)(2,1)S(1)}, u32[]{:S(2)}, u32[]{:S(2)}) collective-permute-start(bf16[256,2560]{1,0:T(8,128)(2,1)S(1)} %get-tuple-element.80.refs_0_), channel_id=1, source_target_pairs={{0,1},{1,0},{2,3},{3,2},{4,5},{5,4},{6,7},{7,6},{8,9},{9,8},{10,11... | collective-permute-start | bytes 3932168 | tf_op jit(solution)/shard_map/ppermute | solution.py:484
  38.8 8.1 %collective-permute-start.5 = (bf16[64,1280]{1,0:T(8,128)(2,1)S(1)}, bf16[64,1280]{1,0:T(8,128)(2,1)S(1)}, u32[]{:S(2)}, u32[]{:S(2)}) collective-permute-start(bf16[64,1280]{1,0:T(8,128)(2,1)S(1)} %get-tuple-element.79.refs_7_), channel_id=1, source_target_pairs={{0,4},{4,0},{8,12},{12,8},{16,20},{20,16},{24,28},{28,24},{1,5},{5... | collective-permute-start | bytes 491528 | tf_op jit(solution)/shard_map/ppermute | solution.py:484
  45.3 6.9 %collective-permute-start.7 = (bf16[64,1280]{1,0:T(8,128)(2,1)S(1)}, bf16[64,1280]{1,0:T(8,128)(2,1)S(1)}, u32[]{:S(2)}, u32[]{:S(2)}) collective-permute-start(bf16[64,1280]{1,0:T(8,128)(2,1)S(1)} %get-tuple-element.86.rest_0_), channel_id=1, source_target_pairs={{0,4},{4,0},{8,12},{12,8},{16,20},{20,16},{24,28},{28,24},{1,5},{5... | collective-permute-start | bytes 491528 | tf_op jit(solution)/shard_map/ppermute | solution.py:484
  52.8 1.6 %collective-permute-start.8 = (bf16[256,512]{1,0:T(8,128)(2,1)S(1)}, bf16[256,512]{1,0:T(8,128)(2,1)S(1)}, u32[]{:S(2)}, u32[]{:S(2)}) collective-permute-start(bf16[256,512]{1,0:T(8,128)(2,1)S(1)} %get-tuple-element.95), channel_id=1, source_target_pairs={{0,1},{1,0},{2,3},{3,2},{4,5},{5,4},{6,7},{7,6},{8,9},{9,8},{10,11... | collective-permute-start | bytes 786440 | tf_op jit(solution)/shard_map/ppermute | solution.py:484
  52.9 1.9 %collective-permute-start.9 = (bf16[256,512]{1,0:T(8,128)(2,1)S(1)}, bf16[256,512]{1,0:T(8,128)(2,1)S(1)}, u32[]{:S(2)}, u32[]{:S(2)}) collective-permute-start(bf16[256,512]{1,0:T(8,128)(2,1)S(1)} %get-tuple-element.96), channel_id=1, source_target_pairs={{0,1},{1,0},{2,3},{3,2},{4,5},{5,4},{6,7},{7,6},{8,9},{9,8},{10,11... | collective-permute-start | bytes 786440 | tf_op jit(solution)/shard_map/ppermute | solution.py:484
  53.4 1.8 %collective-permute-start.10 = (bf16[256,512]{1,0:T(8,128)(2,1)S(1)}, bf16[256,512]{1,0:T(8,128)(2,1)S(1)}, u32[]{:S(2)}, u32[]{:S(2)}) collective-permute-start(bf16[256,512]{1,0:T(8,128)(2,1)S(1)} %get-tuple-element.97), channel_id=1, source_target_pairs={{0,1},{1,0},{2,3},{3,2},{4,5},{5,4},{6,7},{7,6},{8,9},{9,8},{10,11... | collective-permute-start | bytes 786440 | tf_op jit(solution)/shard_map/ppermute | solution.py:484
  53.5 2.1 %collective-permute-start.11 = (bf16[256,512]{1,0:T(8,128)(2,1)S(1)}, bf16[256,512]{1,0:T(8,128)(2,1)S(1)}, u32[]{:S(2)}, u32[]{:S(2)}) collective-permute-start(bf16[256,512]{1,0:T(8,128)(2,1)S(1)} %get-tuple-element.98), channel_id=1, source_target_pairs={{0,1},{1,0},{2,3},{3,2},{4,5},{5,4},{6,7},{7,6},{8,9},{9,8},{10,11... | collective-permute-start | bytes 786440 | tf_op jit(solution)/shard_map/ppermute | solution.py:484
  53.9 2.0 %collective-permute-start.12 = (bf16[256,512]{1,0:T(8,128)(2,1)S(1)}, bf16[256,512]{1,0:T(8,128)(2,1)S(1)}, u32[]{:S(2)}, u32[]{:S(2)}) collective-permute-start(bf16[256,512]{1,0:T(8,128)(2,1)S(1)} %get-tuple-element.99), channel_id=1, source_target_pairs={{0,1},{1,0},{2,3},{3,2},{4,5},{5,4},{6,7},{7,6},{8,9},{9,8},{10,11... | collective-permute-start | bytes 786440 | tf_op jit(solution)/shard_map/ppermute | solution.py:484
  56.2 30.9 %collective-permute-start.20 = (bf16[256,2560]{1,0:T(8,128)(2,1)S(1)}, bf16[256,2560]{1,0:T(8,128)(2,1)S(1)}, u32[]{:S(2)}, u32[]{:S(2)}) collective-permute-start(bf16[256,2560]{1,0:T(8,128)(2,1)S(1)} %chunk_sum.2.rest_1_), channel_id=1, source_target_pairs={{0,2},{1,3},{2,0},{3,1},{4,6},{5,7},{6,4},{7,5},{8,10},{9,11},{10,... | collective-permute-start | bytes 3932168 | tf_op jit(solution)/shard_map/ppermute | solution.py:489
  56.9 15.0 %collective-permute-start.14 = (bf16[80,1280]{1,0:T(8,128)(2,1)S(1)}, bf16[80,1280]{1,0:T(8,128)(2,1)S(1)}, u32[]{:S(2)}, u32[]{:S(2)}) collective-permute-start(bf16[80,1280]{1,0:T(8,128)(2,1)S(1)} %get-tuple-element.94.rest_0_), channel_id=1, source_target_pairs={{16,0},{20,4},{24,8},{28,12},{17,1},{21,5},{25,9},{29,13},{18,2},{... | collective-permute-start | bytes 614408 | tf_op jit(solution)/shard_map/ppermute | solution.py:480
  58.1 13.7 %collective-permute-start.13 = (bf16[80,1280]{1,0:T(8,128)(2,1)S(1)}, bf16[80,1280]{1,0:T(8,128)(2,1)S(1)}, u32[]{:S(2)}, u32[]{:S(2)}) collective-permute-start(bf16[80,1280]{1,0:T(8,128)(2,1)S(1)} %get-tuple-element.94.rest_0_), channel_id=1, source_target_pairs={{8,0},{12,4},{16,8},{20,12},{24,16},{28,20},{9,1},{13,5},{17,9},{2... | collective-permute-start | bytes 614408 | tf_op jit(solution)/shard_map/ppermute | solution.py:480
  72.5 6.7 %collective-permute-start.15 = (bf16[256,512]{1,0:T(8,128)(2,1)S(1)}, bf16[256,512]{1,0:T(8,128)(2,1)S(1)}, u32[]{:S(2)}, u32[]{:S(2)}) collective-permute-start(bf16[256,512]{1,0:T(8,128)(2,1)S(1)} %get-tuple-element.108), channel_id=1, source_target_pairs={{0,1},{1,0},{2,3},{3,2},{4,5},{5,4},{6,7},{7,6},{8,9},{9,8},{10,11... | collective-permute-start | bytes 786440 | tf_op jit(solution)/shard_map/ppermute | solution.py:484
  72.6 6.6 %collective-permute-start.21 = (bf16[64,1280]{1,0:T(8,128)(2,1)S(1)}, bf16[64,1280]{1,0:T(8,128)(2,1)S(1)}, u32[]{:S(2)}, u32[]{:S(2)}) collective-permute-start(bf16[64,1280]{1,0:T(8,128)(2,1)S(1)} %get-tuple-element.117), channel_id=1, source_target_pairs={{0,4},{4,0},{8,12},{12,8},{16,20},{20,16},{24,28},{28,24},{1,5},{5... | collective-permute-start | bytes 491528 | tf_op jit(solution)/shard_map/ppermute | solution.py:484
  73.6 9.3 %collective-permute-start.16 = (bf16[256,512]{1,0:T(8,128)(2,1)S(1)}, bf16[256,512]{1,0:T(8,128)(2,1)S(1)}, u32[]{:S(2)}, u32[]{:S(2)}) collective-permute-start(bf16[256,512]{1,0:T(8,128)(2,1)S(1)} %get-tuple-element.109), channel_id=1, source_target_pairs={{0,1},{1,0},{2,3},{3,2},{4,5},{5,4},{6,7},{7,6},{8,9},{9,8},{10,11... | collective-permute-start | bytes 786440 | tf_op jit(solution)/shard_map/ppermute | solution.py:484
  73.8 9.2 %collective-permute-start.17 = (bf16[256,512]{1,0:T(8,128)(2,1)S(1)}, bf16[256,512]{1,0:T(8,128)(2,1)S(1)}, u32[]{:S(2)}, u32[]{:S(2)}) collective-permute-start(bf16[256,512]{1,0:T(8,128)(2,1)S(1)} %get-tuple-element.110), channel_id=1, source_target_pairs={{0,1},{1,0},{2,3},{3,2},{4,5},{5,4},{6,7},{7,6},{8,9},{9,8},{10,11... | collective-permute-start | bytes 786440 | tf_op jit(solution)/shard_map/ppermute | solution.py:484
  79.2 3.7 %collective-permute-start.18 = (bf16[256,512]{1,0:T(8,128)(2,1)S(1)}, bf16[256,512]{1,0:T(8,128)(2,1)S(1)}, u32[]{:S(2)}, u32[]{:S(2)}) collective-permute-start(bf16[256,512]{1,0:T(8,128)(2,1)S(1)} %get-tuple-element.111), channel_id=1, source_target_pairs={{0,1},{1,0},{2,3},{3,2},{4,5},{5,4},{6,7},{7,6},{8,9},{9,8},{10,11... | collective-permute-start | bytes 786440 | tf_op jit(solution)/shard_map/ppermute | solution.py:484
  79.2 3.7 %collective-permute-start.19 = (bf16[256,512]{1,0:T(8,128)(2,1)S(1)}, bf16[256,512]{1,0:T(8,128)(2,1)S(1)}, u32[]{:S(2)}, u32[]{:S(2)}) collective-permute-start(bf16[256,512]{1,0:T(8,128)(2,1)S(1)} %get-tuple-element.112), channel_id=1, source_target_pairs={{0,1},{1,0},{2,3},{3,2},{4,5},{5,4},{6,7},{7,6},{8,9},{9,8},{10,11... | collective-permute-start | bytes 786440 | tf_op jit(solution)/shard_map/ppermute | solution.py:484

commit v4 on v3

--- a/solution.py
+++ b/solution.py
@@ -11,6 +11,9 @@
 GROUP = 256
 LANES = 128
 TILE = 16
+PARTS = 4
+HALVES = 1
+TAIL_COST, FAR_COST, NEAR_COST = 1.73e9, 2.306e10, 9.224e9
 LOG2E = math.log2(math.e)
 F32 = jnp.float32
 BF16 = jnp.bfloat16
@@ -73,75 +76,79 @@
 
 
 def state_kernel(
-    heads, blocks, places, x_hbm, b_hbm, c_hbm, ld_hbm, doc_ref, spread_ref,
-    crow_ref, entry_ref, exit_ref, local_ref, keep_ref, send_ref, pre_ref, blk_ref, info_ref,
-    b_ref, c_ref, padded, running, ld_ref, x_ref, sems,
+    heads, blocks, places, x_hbm, b_hbm, c_hbm, ld_hbm, doc_hbm, spread_ref, *rest
 ):
+    crow_ref, entry_ref, exit_ref, local_ref, keep_ref, send_ref, pre_ref, blk_ref, info_ref = rest[:9]
+    b_ref, c_ref, padded, running, ld_ref, doc_ref, x_ref, sems = rest[9:]
     n, inner = running.shape
     half = n // 2
     parts = [pl.ds(k * GROUP, GROUP) for k in range(blocks)]
-    ld_copy, b_copy, c_copy, *x_copies = start(
-        sems, (ld_hbm, ld_ref), (b_hbm, b_ref), (c_hbm, c_ref),
-        *[(x_hbm.at[p], x_ref.at[p]) for p in parts],
+    ld_copy, doc_copy, b_copy, *x_copies, c_copy = start(
+        sems, (ld_hbm, ld_ref), (doc_hbm, doc_ref), (b_hbm, b_ref),
+        *[(x_hbm.at[p], x_ref.at[p]) for p in parts], (c_hbm, c_ref),
     )
     head_rows = crow_ref.shape[1]
     spread = spread_ref[...]
     later = (iota((GROUP, GROUP), 0) <= iota((GROUP, GROUP), 1)).astype(BF16)
     padded[...] = jnp.zeros_like(padded)
     row = iota((head_rows, GROUP), 0)
+    states, ends, cols = [], [], []
     pre_ref[...] = jnp.zeros_like(pre_ref)
     blk_ref[...] = jnp.zeros_like(blk_ref)
     info_ref[...] = jnp.zeros_like(info_ref)
-    first_doc = last_doc = total = None
     ld_copy.wait()
+    doc_copy.wait()
     for k in range(blocks):
         at = slice(k * GROUP, (k + 1) * GROUP)
-        padded[0:heads, :] = ld_ref[:, at] * LOG2E
-        steps = padded[0:head_rows, :]
-        high, rest = split(steps)
-        mid, low = split(steps - high.astype(F32))
-        cum = dot(high, later) + (dot(mid, later) + dot(low, later))
-        cum = jnp.where(row == head_rows - 1, doc_ref[:, at].astype(F32), cum)
-        crow_ref[k] = cum
-        padded[0:head_rows, :] = cum
-        ccol = padded[...].T
-        padded[0:head_rows, :] = jnp.zeros((head_rows, GROUP), F32)
+        padded[k, 0:heads, :] = ld_ref[:, at] * LOG2E
+    steps = jnp.concatenate([padded[k, 0:head_rows, :] for k in range(blocks)], axis=0)
+    high, rest = split(steps)
+    mid, low = split(steps - high.astype(F32))
+    cum = dot(high, later) + (dot(mid, later) + dot(low, later))
+    for k in range(blocks):
+        at = slice(k * GROUP, (k + 1) * GROUP)
+        own_cum = cum[k * head_rows : (k + 1) * head_rows]
+        own_cum = jnp.where(row == head_rows - 1, doc_ref[:, at].astype(F32), own_cum)
+        crow_ref[k] = own_cum
+        padded[k, 0:head_rows, :] = own_cum
+    b_copy.wait()
+    for k in range(blocks):
+        at = slice(k * GROUP, (k + 1) * GROUP)
+        ccol = padded[k].T
+        cols.append(ccol)
         docs = ccol[:, head_rows - 1 : head_rows]
         end = ccol[GROUP - 1 :]
+        ends.append(end)
         end_doc = end[:, head_rows - 1 : head_rows]
-        if k == 0:
-            first_doc = ccol[0:1, head_rows - 1 : head_rows]
-            last_doc = first_doc
-            total = jnp.zeros_like(end)
         exit_w = jnp.where(docs == end_doc, jnp.exp2(jnp.minimum(end - ccol, 0.0)), 0.0).astype(BF16)
         exit_ref[at, :] = exit_w
-        entry_ref[at, :] = jnp.where(docs == last_doc, jnp.exp2(jnp.minimum(ccol, 0.0)), 0.0).astype(BF16)
-        if k == 0:
-            b_copy.wait()
         x_copies[k].wait()
         scaled = (dot(exit_w, spread) * x_ref[at, :].astype(F32)).astype(BF16)
-        own = dot(b_ref[at, :], scaled, TN)
-        block_decay = jnp.where(end_doc == last_doc, jnp.exp2(end), 0.0)
-        whole = jnp.exp2(total + end)
-        stacked = jnp.concatenate(
-            [block_decay, jnp.where(end_doc == first_doc, whole, 0.0), whole, jnp.zeros((5, LANES), F32)],
-            axis=0,
-        )
-        high, rest = split(stacked)
-        wide = dot(high, spread) + dot(rest, spread)
-        blk_ref[k : k + 1, :] = wide[0:1]
-        if k == 0:
-            local_ref[k] = jnp.zeros((n, inner), BF16)
-            pre_ref[0:1, :] = jnp.ones((1, inner), F32)
-            running[...] = own
-        else:
-            local_ref[k] = running[...].astype(BF16)
-            running[...] = wide[0:1] * running[...] + own
-        if k < blocks - 1:
-            pre_ref[k + 1 : k + 2, :] = wide[1:2]
+        states.append(dot(b_ref[at, :], scaled, TN))
+    doc_of = lambda line: line[:, head_rows - 1 : head_rows]
+    first_doc = doc_of(cols[0][0:1])
+    priors = [first_doc] + [doc_of(end) for end in ends[:-1]]
+    last_doc = doc_of(ends[-1])
+    total = jnp.zeros_like(ends[0])
+    decays, prefixes = [], []
+    for end, prior in zip(ends, priors):
+        decays.append(jnp.where(doc_of(end) == prior, jnp.exp2(end), 0.0))
         total = total + end
-        last_doc = end_doc
-    raw = wide[2:3]
+        prefixes.append(jnp.where(doc_of(end) == first_doc, jnp.exp2(total), 0.0))
+    stacked = decays + prefixes + [jnp.exp2(total)]
+    stacked.append(jnp.zeros((-len(stacked) % 8, LANES), F32))
+    high, rest = split(jnp.concatenate(stacked, axis=0))
+    wide = dot(high, spread) + dot(rest, spread)
+    blk_ref[0:blocks, :] = wide[0:blocks]
+    pre_ref[0:1, :] = jnp.ones((1, inner), F32)
+    pre_ref[1:blocks, :] = wide[blocks : 2 * blocks - 1]
+    local_ref[0] = jnp.zeros((n, inner), BF16)
+    now = states[0]
+    for k in range(1, blocks):
+        local_ref[k] = now.astype(BF16)
+        now = wide[k : k + 1] * now + states[k]
+    running[...] = now
+    raw = wide[2 * blocks : 2 * blocks + 1]
     last_row = jnp.broadcast_to(last_doc + 1.0, (1, inner))
     first_row = jnp.broadcast_to(first_doc + 1.0, (1, inner))
     info_ref[0:1, :] = raw
@@ -151,6 +158,10 @@
     keep_ref[...] = running[pl.ds(pl.multiple_of(side * half, half), half), :].astype(BF16)
     send_ref[0:half, :] = running[pl.ds(pl.multiple_of((1 - side) * half, half), half), :].astype(BF16)
     send_ref[half:, :] = tags(raw, last_row, first_row)
+    for k, prior in enumerate(priors):
+        at = slice(k * GROUP, (k + 1) * GROUP)
+        same = doc_of(cols[k]) == prior
+        entry_ref[at, :] = jnp.where(same, jnp.exp2(jnp.minimum(cols[k], 0.0)), 0.0).astype(BF16)
     c_copy.wait()
 
 
@@ -191,14 +202,15 @@
             pltpu.VMEM((tokens, n), BF16),
             pltpu.VMEM((tokens, n), BF16),
         ],
-        [SM] + [HB] * 4 + [VM] * 2,
+        [SM] + [HB] * 5 + [VM],
         (places, inputs, write_keys, read_keys, log_decay, docs_row, spread),
         scratch=[
-            pltpu.VMEM((LANES, GROUP), F32),
+            pltpu.VMEM((blocks, LANES, GROUP), F32),
             pltpu.VMEM((n, inner), F32),
             pltpu.VMEM((heads, tokens), F32),
+            pltpu.VMEM((1, tokens), jnp.int32),
             pltpu.VMEM((tokens, inner), BF16),
-            pltpu.SemaphoreType.DMA((3 + blocks,)),
+            pltpu.SemaphoreType.DMA((4 + blocks,)),
         ],
     )
 
@@ -217,13 +229,12 @@
     head_rows = crow_ref.shape[1]
     per = LANES // width
     part = lambda k: pl.ds(pl.multiple_of(k * GROUP, GROUP), GROUP)
-    copies = []
     if not backward:
-        sems, x_sems, x_hbm, x_ref = *rest[2 * fetched + 2 : 2 * fetched + 4], x_ref, rest[-1]
+        x_sems, x_hbm, x_ref = rest[-2], x_ref, rest[-1]
         incoming = lambda k: pltpu.make_async_copy(x_hbm.at[part(k)], x_ref.at[part(k)], x_sems.at[k])
         for k in range(blocks):
             incoming(k).start()
-        copies = start(sems, *zip(fetch_hbm, fetch_vm))
+    copies = start(rest[2 * fetched + 2], *zip(fetch_hbm, fetch_vm)) if fetched else []
     lane = iota((GROUP, LANES), 1)
     rows, cols = iota((GROUP, GROUP), 0), iota((GROUP, GROUP), 1)
     causal = (rows <= cols) if backward else (cols <= rows)
@@ -296,8 +307,8 @@
         [SM] + [VM if backward else HB] + [VM] * (5 + len(carried)) + [HB] * len(fetch),
         (places, x, write_keys, read_keys, crow, skip, after, *carried, *fetch),
         scratch=[pltpu.VMEM((LANES, GROUP), F32)]
+        + ([pltpu.SemaphoreType.DMA((len(fetch),))] if fetch else [])
         + ([] if backward else [
-            pltpu.SemaphoreType.DMA((len(fetch),)),
             pltpu.SemaphoreType.DMA((blocks,)),
             pltpu.VMEM((tokens, inner), BF16),
         ]),
@@ -310,78 +321,101 @@
     return [pl.ds(j * step, step) for j in range(size // step)]
 
 
-def tail_kernel(
+def gate_kernel(
     items, chunk, places, mixed_ref, gates_ref, read_ref, entry_ref, local_ref,
-    keep_ref, other_ref, pre_ref, spread_ref, w_ref, *rest
+    keep_ref, other_ref, pre_ref, spread_ref, *rest
 ):
-    cuts = tiling(w_ref.shape[1])
-    outs, gated = rest[len(rest) - 2 - len(cuts) : -1], rest[-1]
+    outs = rest[-len(items) :]
     at_low = places[0] == 0
     keep, other = keep_ref[...].astype(F32), other_ref[...].astype(F32)
     state = jnp.concatenate(
         [jnp.where(at_low, keep, other), jnp.where(at_low, other, keep)], axis=0
     )
-    for i, item in enumerate(items):
+    for item, out_ref in zip(items, outs):
         at = pl.ds(pl.multiple_of(places[item] * chunk, chunk), chunk)
         k = places[item] * chunk // GROUP
         entering = (local_ref[k].astype(F32) + row_at(pre_ref[...], k) * state).astype(BF16)
         carried = dot(read_ref[at, :], entering) * dot(entry_ref[at, :], spread_ref[...])
-        gated[i * chunk : (i + 1) * chunk, :] = (
+        out_ref[...] = (
             (mixed_ref[at, :].astype(F32) + carried) * silu(gates_ref[at, :])
         ).astype(BF16)
-    for j, cut in enumerate(cuts):
-        both = dot(gated[...], w_ref[:, cut]).astype(BF16)
-        outs[j][...] = both[:chunk]
-        outs[-1][:, cut] = both[chunk:]
-
-
-def forward_tail(
-    chunk, items, places, mixed, gates, read_keys, entry, local, keep, other, pre, spread, out_weight, after
+
+
+def gated_chunks(
+    chunk, items, places, mixed, gates, read_keys, entry, local, keep, other, pre, spread, after
 ):
-    inner, width = out_weight.shape
-    count = len(items)
+    inner = mixed.shape[1]
     return call(
-        functools.partial(tail_kernel, items, chunk),
-        "forward_tail",
-        [pltpu.VMEM((chunk, cut.size), BF16) for cut in tiling(width)] + [pltpu.VMEM((chunk, width), BF16)],
-        [SM] + [VM] * (10 + len(after)),
-        (places, mixed, gates, read_keys, entry, local, keep, other, pre, spread, out_weight, *after),
-        scratch=[pltpu.VMEM((count * chunk, inner), BF16)],
-    )
-
-
-def sum_kernel(count, final, *refs):
-    stay_ref, piece_refs, landed_refs = refs[0], refs[1 : 1 + count], refs[1 + count : len(refs) - 1 - 2 * final]
-    out_ref = refs[-2] if final else refs[-1]
+        functools.partial(gate_kernel, items, chunk),
+        "gated_chunks",
+        [pltpu.VMEM((chunk, inner), BF16)] * len(items),
+        [SM] + [VM] * (9 + len(after)),
+        (places, mixed, gates, read_keys, entry, local, keep, other, pre, spread, *after),
+    )
+
+
+def project_kernel(has_part, count, gated_ref, w_ref, *rest):
+    outs = rest[-count:]
+    width = outs[0].shape[1]
+    for i, out_ref in enumerate(outs):
+        for cut in tiling(width):
+            at = pl.ds(i * width + cut.start, cut.size)
+            total = dot(gated_ref[...], w_ref[:, at])
+            if has_part:
+                total = rest[0][:, at] + total
+            out_ref[:, cut] = total.astype(out_ref.dtype)
+
+
+def project(gated, weight, part, kind, after=(), count=1, flops=1):
+    shape = (gated.shape[0], weight.shape[1] // count)
+    parts = [] if part is None else [part]
+    return call(
+        functools.partial(project_kernel, bool(parts), count),
+        "project",
+        [pltpu.VMEM(shape, kind)] * count,
+        [VM] * (2 + len(parts) + len(after)),
+        (gated, weight, *parts, *after),
+        flops=flops,
+    )
+
+
+def sum_kernel(own_ref, *rest):
+    landed_refs, (out_hbm, out_ref, sems) = rest[:-3], rest[-3:]
     outgoing = []
-    for j, cut in enumerate(tiling(stay_ref.shape[1])):
-        total = stay_ref[:, cut].astype(F32) + piece_refs[j][...].astype(F32)
-        for ref in landed_refs:
-            total = total + ref[:, cut].astype(F32)
-        out_ref[:, cut] = total.astype(BF16)
-        if final:
-            outgoing += start(refs[-1].at[j], (out_ref.at[:, cut], refs[-3].at[:, cut]))
+    width = landed_refs[0].shape[1] if landed_refs else own_ref.shape[1]
+    for i in range(own_ref.shape[1] // width):
+        at = pl.ds(i * width, width)
+        total = own_ref[:, at]
+        for ref in landed_refs[i :: own_ref.shape[1] // width]:
+            total = total + ref[...].astype(F32)
+        out_ref[:, at] = total.astype(BF16)
+        outgoing += start(sems.at[i], (out_ref.at[:, at], out_hbm.at[:, at]))
     for copy in outgoing:
         copy.wait()
 
 
-def chunk_sum(stay, pieces, landed=(), final=False):
-    make = pltpu.HBM if final else pltpu.VMEM
+def chunk_sum(own, landed):
     return call(
-        functools.partial(sum_kernel, len(pieces), final),
+        sum_kernel,
         "chunk_sum",
-        [make(stay.shape, stay.dtype)],
-        [VM] * (1 + len(pieces) + len(landed)),
-        (stay, *pieces, *landed),
+        [pltpu.HBM(own.shape, BF16)],
+        [VM] * (1 + len(landed)),
+        (own, *landed),
         scratch=[
-            pltpu.VMEM(stay.shape, stay.dtype), pltpu.SemaphoreType.DMA((len(pieces), 1))
-        ] if final else (),
+            pltpu.VMEM(own.shape, BF16),
+            pltpu.SemaphoreType.DMA((HALVES, 1)),
+        ],
     )[0]
 
 
-def grad_kernel(items, chunk, first, final, places, *refs):
+def grad_kernel(items, chunk, first, final, distant, places, *refs):
     count = len(items)
     go_refs, refs = refs[:count], refs[count:]
+    if distant:
+        go_ref, sems, refs = refs[-2], refs[-1], refs[:-2]
+        for copy in start(sems, (go_refs[0], go_ref)):
+            copy.wait()
+        go_refs = [go_ref]
     gates_ref, read_ref, entry_ref, pre_ref, spread_ref, w_ref, _ = refs[:7]
     refs = refs[7:]
     if not first:
@@ -409,7 +443,8 @@
 
 
 def grad_chunks(
-    chunk, items, places, arrived, gates, read_keys, entry, pre, spread, out_weight, earlier, final, after
+    chunk, items, places, arrived, gates, read_keys, entry, pre, spread, out_weight, earlier, final, after,
+    distant=False,
 ):
     count = len(arrived)
     inner = out_weight.shape[0]
@@ -420,14 +455,15 @@
     out_shape += [pltpu.VMEM((n // 2, inner), BF16)] * 2 if final else [pltpu.VMEM((n, inner), F32)]
     at = 1 + count + 7
     return call(
-        functools.partial(grad_kernel, items, chunk, first, final),
+        functools.partial(grad_kernel, items, chunk, first, final, distant),
         "grad_chunks",
         out_shape,
-        [SM] + [VM] * (count + 7 + (0 if first else 3)),
+        [SM] + [HB if distant else VM] * count + [VM] * (7 + (0 if first else 3)),
         (
             places, *arrived, gates, read_keys, entry, pre, spread, out_weight, after,
             *([] if first else (earlier[2], earlier[0], earlier[1])),
         ),
+        scratch=[pltpu.VMEM(arrived[0].shape, BF16), pltpu.SemaphoreType.DMA((1,))] if distant else (),
         aliases=None if first else {at + 1: 0, at + 2: 1},
     )
 
@@ -466,6 +502,7 @@
         [pltpu.HBM((tokens, inner), BF16)],
         [SM] + [VM] * 8,
         (places, part, write_keys, exit_w, states, blk, keep, other, spread),
+        flops=TAIL_COST,
         scratch=[
             pltpu.VMEM((n, inner), F32),
             pltpu.VMEM((tokens, inner), BF16),
@@ -510,11 +547,17 @@
 
 
 def enter_kernel(through, places, near_ref, facts_ref, one_ref, two_ref, _, *rest):
-    copies = start(rest[-1], *zip(rest[:through], rest[through + 3 :])) if through else []
+    copies = []
+    for i in range(through):
+        source, target = rest[i], rest[through + 3 + i]
+        step = source.shape[0] // PARTS
+        parts = [pl.ds(j * step, step) for j in range(PARTS)]
+        copies += start(rest[-1].at[i], *[(source.at[p], target.at[p]) for p in parts])
     mine_ref, hers_ref, out_ref = rest[through : through + 3]
     low = places[0] == 0
     one, one_decay, one_last, one_first = untagged(one_ref[...])
     two, _, two_last, _ = untagged(two_ref[...])
+    two = jnp.where(places[places.shape[0] - 2] > 0, two, 0.0)
     facts = facts_ref[...]
     at_near = one + jnp.where(one_first == two_last, one_decay, 0.0) * two
     near_live = (facts[3:4] == one_last).astype(F32)
@@ -530,8 +573,7 @@
         copy.wait()
 
 
-def pair_back_kernel(places, keep_ref, got_ref, facts_ref, _, *rest):
-    tagged_ref, near_ref = rest[len(rest) // 2 - 1 :][:2]
+def pair_back_kernel(places, keep_ref, got_ref, facts_ref, _, tagged_ref, near_ref):
     low = places[0] == 0
     facts = facts_ref[...]
     keep, got = keep_ref[...].astype(F32), got_ref[...].astype(F32)
@@ -544,26 +586,23 @@
     near_ref[...] = near.astype(BF16)
 
 
-def enter_back_kernel(places, near_ref, facts_ref, one_ref, two_ref, _, *rest):
-    mine_ref, hers_ref = rest[len(rest) // 2 - 1 :][:2]
+def enter_back_kernel(places, near_ref, facts_ref, one_ref, two_ref, _, mine_ref, hers_ref):
     low = places[0] == 0
     one, one_decay, one_last, one_first = untagged(one_ref[...])
     two, _, two_last, _ = untagged(two_ref[...])
+    two = jnp.where(places[places.shape[0] - 1] > 0, two, 0.0)
     at_near = one + jnp.where(one_first == two_last, one_decay, 0.0) * two
     at_far = near_ref[...].astype(F32) + facts_ref[1:2, :] * at_near
     mine_ref[...] = jnp.where(low, at_far, at_near).astype(BF16)
     hers_ref[...] = jnp.where(low, at_near, at_far).astype(BF16)
 
 
-def small(kernel, name, shapes, args, after, through=(), kept=()):
+def small(kernel, name, shapes, args, after, through=()):
     out_shape = [pltpu.VMEM(dims, kind) for dims, kind in shapes]
-    out_shape += [pltpu.VMEM(a.shape, a.dtype) for a in (*through, *kept)]
-    count = 1 + len(args) + len(through)
+    out_shape += [pltpu.VMEM(a.shape, a.dtype) for a in through]
     return call(
-        kernel, name, out_shape, [SM] + [VM] * len(args) + [HB] * len(through) + [VM] * len(kept),
-        (*args, after, *through, *kept),
-        aliases={count + i: len(shapes) + i for i in range(len(kept))},
-        scratch=[pltpu.SemaphoreType.DMA((len(through),))] if through else (),
+        kernel, name, out_shape, [SM] + [VM] * len(args) + [HB] * len(through), (*args, after, *through),
+        scratch=[pltpu.SemaphoreType.DMA((len(through), PARTS))] if through else (),
     )
 
 
@@ -571,8 +610,8 @@
     half = tagged.shape[0] - TILE
     window = max(lax.axis_size("seq") // 4, 1)
     if window <= 2:
-        one = shifted(tagged, "seq", 2 * way)
-        return one, shifted(tagged, "seq", 4 * way) if window == 2 else jnp.zeros_like(one)
+        two = rotated(tagged, "seq", 4 * way) if window == 2 else jnp.zeros_like(tagged)
+        return shifted(tagged, "seq", 2 * way), two
     total, decay, _, first = untagged(tagged)
     came, _, came_last, _ = untagged(shifted(tagged, "seq", 2 * way))
     decay = jnp.where(first == came_last, decay, 0.0)
@@ -604,10 +643,12 @@
         source = (here - 2 * d) % members
         target = ((chip + d) % chips) * 2
         numbers += [source, source ^ 1, target + 1 - core, target + core]
-    places = jnp.stack([side] + numbers).astype(jnp.int32)
+    pair_at, pairs = lax.axis_index("seq") // 2, lax.axis_size("seq") // 2
+    places = jnp.stack([side] + numbers + [pair_at >= 2, pair_at + 2 < pairs]).astype(jnp.int32)
 
     remote = [rotated(grad_out, "head", 2 * d) for d in range(1, chips)]
     sibling = swapped(grad_out, "head")
+    mate_weight = swapped(out_weight, "head")
 
     spread = (
         jnp.arange(LANES)[:, None] == (jnp.arange(inner) // width)[None, :]
@@ -626,23 +667,25 @@
     )
     one, two = between_pairs(pair, 1)
 
-    def grads(items, arrived, earlier, final, after):
+    def grads(items, arrived, earlier, final, after, distant=False):
         return grad_chunks(
-            chunk, items, places, arrived, gates, c, entry, pre, spread, weight, earlier, final, after
+            chunk, items, places, arrived, gates, c, entry, pre, spread, weight, earlier, final, after,
+            distant,
         )
 
     back = grads((1, 2), [own_grad, sibling], None, chips == 1, pair)
-    part = inside(places, back[0], b, c, crow, skip, heads, back[1], which=(0, 1))[0]
+    part, mate_weight = inside(
+        places, back[0], b, c, crow, skip, heads, back[1], (mate_weight,), which=(0, 1)
+    )
     enter_keep, hers, facts, *remote = small(
         functools.partial(enter_kernel, len(remote)), "enter", [(half, BF16), (half, BF16), (facts_shape, F32)],
         (places, near, facts, one, two), part, remote,
     )
     enter_other = swapped(hers, "seq")
 
-    def tail(items, *after):
-        return forward_tail(
-            chunk, items, places, mixed, gates, c, entry, local, enter_keep, enter_other, pre, spread,
-            weight, after,
+    def gated(items, *after):
+        return gated_chunks(
+            chunk, items, places, mixed, gates, c, entry, local, enter_keep, enter_other, pre, spread, after
         )
 
     for d in range(chips - 1):
@@ -651,29 +694,28 @@
         back = grads((4 + 4 * d,), [relayed], back, d == chips - 2, back[1])
     mix, states, back_keep, back_send = back
     got = swapped(back_send, "seq")
-    after, given, stayed = back_send, [], []
+    after, landed = back_send, []
     for d in range(chips - 1):
-        *give, after = tail((5 + 4 * d, 6 + 4 * d), after)
-        given += give
-        stayed.append(after)
-    pair, near, *given = small(
+        give, stay = gated((5 + 4 * d, 6 + 4 * d), after)
+        (after,) = project(stay, weight, None, F32, (give,), flops=FAR_COST)
+        for total in project(swapped(give, "head"), mate_weight, after, BF16, count=HALVES):
+            landed.append(rotated(total, "head", 2 * (d + 1)))
+            after = total
+    pair, near = small(
         pair_back_kernel, "pair_back", [(tagged, BF16), (half, BF16)],
-        (places, back_keep, got, facts), after, kept=given,
+        (places, back_keep, got, facts), after,
     )
     one, two = between_pairs(pair, -1)
-    landed, pieces = [], len(given) // max(chips - 1, 1)
-    for d in range(chips - 1):
-        got = [swapped(piece, "head") for piece in given[d * pieces : (d + 1) * pieces]]
-        after = chunk_sum(stayed[d], got)
-        landed.append(rotated(after, "head", 2 * (d + 1)))
-    *give, stay = tail((2, 1), pair, after)
-    part = inside(places, mix, b, c, crow, skip, heads, stay, which=(1, chips), earlier=part)[0]
-    arrive_keep, hers, *give = small(
+    give, stay = gated((2, 1), pair)
+    (own,) = project(stay, weight, None, F32, (give,), flops=NEAR_COST)
+    (own,) = project(swapped(give, "head"), mate_weight, own, F32)
+    part = inside(places, mix, b, c, crow, skip, heads, own, which=(1, chips), earlier=part)[0]
+    arrive_keep, hers = small(
         enter_back_kernel, "enter_back", [(half, BF16), (half, BF16)],
-        (places, near, facts, one, two), part, kept=give,
+        (places, near, facts, one, two), part,
     )
     arrive_other = swapped(hers, "seq")
-    out = chunk_sum(stay, [swapped(piece, "head") for piece in give], landed, True)
+    out = chunk_sum(own, landed)
     grad_inputs = back_tail(
         places, part, b, exit_w, states, blk, arrive_keep, arrive_other, spread
     )

time: 88.8 us -> 82.6 us (0.930)
  waiting for transfers between devices: 14.7 us -> 9.47 us
    ppermute x2 -> x4, starting transfers between devices: 3.17 us -> 10.6 us  [rotated(): lax.ppermute(block, axis, [(i, (i + distance) % size) for i in range(size)])]
    ppermute x4 -> x2, starting transfers between devices: 10.8 us -> 5.01 us  [shifted(): return lax.ppermute(block, axis, route)]
    ppermute x4 -> x2, waiting for transfers between devices: 3.54 us -> 0.01 us  [shifted(): return lax.ppermute(block, axis, route)]
    ppermute x16 -> x9, waiting for transfers between devices: 7.05 us -> 4.26 us  [swapped(): lax.ppermute(block, axis, [(i, i ^ 1) for i in range(lax.axis_size(axis))])]
    ppermute x16 -> x9, starting transfers between devices: 7.59 us -> 6.16 us  [swapped(): lax.ppermute(block, axis, [(i, i ^ 1) for i in range(lax.axis_size(axis))])]
    ppermute x2 -> x4, waiting for transfers between devices: 4.15 us -> 5.21 us  [rotated(): lax.ppermute(block, axis, [(i, (i + distance) % size) for i in range(size)])]
    pallas_call x16 -> x19, Pallas kernels: 50.1 us -> 49.7 us  [call(): pl.pallas_call(kernel, in_specs=in_specs, out_specs=[VM if o.memory_space...]
  transfers between devices with their start and end apart: 22 -> 15, of which waited for: 8 -> 5; matrix products, arithmetic and copies ran while one was open for 0% -> 0% of each run, Pallas kernels for 52% -> 57%
where the time goes in v4:
time: 82.6 us; the launch traced here: 82.4 us
  Pallas kernels  49.7 us (60%)
  starting transfers between devices  21.8 us (26%)
  waiting for transfers between devices  9.47 us (11%)
  between operations  1.07 us (1%)
    pallas_call x19, Pallas kernels, call(): pl.pallas_call(kernel, in_specs=in_specs, out_specs=[VM if o.memory_space...  49.7 us
    ppermute x4, starting transfers between devices, rotated(): lax.ppermute(block, axis, [(i, (i + distance) % size) for i in range(size)])  10.6 us
    ppermute x9, starting transfers between devices, swapped(): lax.ppermute(block, axis, [(i, i ^ 1) for i in range(lax.axis_size(axis))])  6.16 us
    ppermute x4, waiting for transfers between devices, rotated(): lax.ppermute(block, axis, [(i, (i + distance) % size) for i in range(size)])  5.21 us
    ppermute x2, starting transfers between devices, shifted(): return lax.ppermute(block, axis, route)  5.01 us
    ppermute x9, waiting for transfers between devices, swapped(): lax.ppermute(block, axis, [(i, i ^ 1) for i in range(lax.axis_size(axis))])  4.26 us
  transfers between devices with their start and end apart: 15, of which 5 were waited for; matrix products, arithmetic and copies ran while one was open for 0% of the time, Pallas kernels for 57%

profile of v4, /device:TPU:0, one launch (start us, length us, event | category | flops | bytes accessed | tf_op | source)
XLA Modules:
  0.0 82.4 jit_solution(1301572306630037163)
XLA Ops:
  1.2 2.9 %collective-permute-start.5 = (bf16[256,2560]{1,0:T(8,128)(2,1)}, bf16[256,2560]{1,0:T(8,128)(2,1)}, u32[]{:S(2)}, u32[]{:S(2)}) collective-permute-start(bf16[256,2560]{1,0:T(8,128)(2,1)} %rest_2_.1), channel_id=1, source_target_pairs={{0,2},{1,3},{2,0},{3,1},{4,6},{5,7},{6,4},{7,5},{8,10},{9,11},{10,... | collective-permute-start | bytes 3932168 | tf_op jit(solution)/shard_map/ppermute | solution.py:526
  4.3 4.3 %local_states.1 = (f32[4,24,256]{2,1,0:T(8,128)S(1)}, bf16[1024,128]{1,0:T(8,128)(2,1)S(1)}, bf16[1024,128]{1,0:T(8,128)(2,1)S(1)}, bf16[4,128,1280]{2,1,0:T(8,1...) custom-call(s32[9]{0:T(128)S(1)} %stack.47.places, ...), custom_call_target="tpu_custom_call" | custom-call | flops 1 | bytes 1 | tf_op jit(solution)/shard_map/local_states/pallas_call | solution.py:38
  8.6 1.6 %collective-permute-start = (bf16[80,1280]{1,0:T(8,128)(2,1)S(1)}, bf16[80,1280]{1,0:T(8,128)(2,1)S(1)}, u32[]{:S(2)}, u32[]{:S(2)}) collective-permute-start(bf16[80,1280]{1,0:T(8,128)(2,1)S(1)} %get-tuple-element.47._), channel_id=1, source_target_pairs={{0,4},{4,0},{8,12},{12,8},{16,20},{20,16},{24,28},{28,24},{1,5},{5... | collective-permute-start | bytes 614408 | tf_op jit(solution)/shard_map/ppermute | solution.py:521
  10.4 7.0 %inside_forward.1 = (bf16[1024,1280]{1,0:T(8,128)(2,1)S(1)}, bf16[1024,1280]{1,0:T(8,128)(2,1)S(1)}, bf16[1280,2560]{1,0:T(8,128)(2,1)S(1)}, bf16[256,2560]{1,0:T(8,128)(2,1)S(1)}) custom-call(s32[9]{0:T(128)S(1)} %stack.47.places, bf16[1024,1280]{1,0:T(8,128)(2,1)} %x_ref.1, bf16[1024,128]{1,0:T(8,128)(2,1)S(1)} %get-tuple-element.44.b_ref, ...), custom_call_target="tpu_custom_call" | custom-call | flops 1 | bytes 1 | tf_op jit(solution)/shard_map/inside_forward/pallas_call | solution.py:38
  18.1 3.5 %collective-permute-start.1 = (bf16[80,1280]{1,0:T(8,128)(2,1)S(1)}, bf16[80,1280]{1,0:T(8,128)(2,1)S(1)}, u32[]{:S(2)}, u32[]{:S(2)}) collective-permute-start(bf16[80,1280]{1,0:T(8,128)(2,1)S(1)} %get-tuple-element.56.refs_8_), channel_id=1, source_target_pairs={{0,8},{4,12},{8,16},{12,20},{16,24},{20,28},{1,9},{5,13},{9,17},{1... | collective-permute-start | bytes 614408 | tf_op jit(solution)/shard_map/ppermute | solution.py:517
  21.6 2.6 %collective-permute-start.2 = (bf16[80,1280]{1,0:T(8,128)(2,1)S(1)}, bf16[80,1280]{1,0:T(8,128)(2,1)S(1)}, u32[]{:S(2)}, u32[]{:S(2)}) collective-permute-start(bf16[80,1280]{1,0:T(8,128)(2,1)S(1)} %get-tuple-element.56.refs_8_), channel_id=1, source_target_pairs={{0,16},{4,20},{8,24},{12,28},{16,0},{20,4},{24,8},{28,12},{1,17},{... | collective-permute-start | bytes 614408 | tf_op jit(solution)/shard_map/ppermute | solution.py:526
  24.3 6.1 %grad_chunks.3 = (bf16[1024,1280]{1,0:T(8,128)(2,1)S(1)}, bf16[4,128,1280]{2,1,0:T(8,128)(2,1)S(1)}, f32[128,1280]{1,0:T(8,128)S(1)}) custom-call(s32[9]{0:T(128)S(1)} %stack.47.places, bf16[256,2560]{1,0:T(8,128)(2,1)S(1)} %get-tuple-element.57.refs_0_, bf16[256,2560]{1,0:T(8,128)(2,1)} %collective-permute-done.3.refs_1_, ...), custom_call_target="tpu_custom_call" | custom-call | flops 1 | bytes 1 | tf_op jit(solution)/shard_map/grad_chunks/pallas_call | solution.py:38
  30.4 3.6 %inside_backward.2 = (bf16[1024,1280]{1,0:T(8,128)(2,1)S(1)}, bf16[1280,2560]{1,0:T(8,128)(2,1)S(1)}) custom-call(s32[9]{0:T(128)S(1)} %stack.47.places, bf16[1024,1280]{1,0:T(8,128)(2,1)S(1)} %get-tuple-element.60.x_ref.refs_9_, bf16[1024,128]{1,0:T(8,128)(2,1)S(1)} %get-tuple-element.44.b_ref, ...), custom_call_target="tpu_custom_call" | custom-call | flops 1 | bytes 1 | tf_op jit(solution)/shard_map/inside_backward/pallas_call | solution.py:38
  34.0 1.8 %enter.1 = (bf16[64,1280]{1,0:T(8,128)(2,1)S(1)}, bf16[64,1280]{1,0:T(8,128)(2,1)S(1)}, f32[8,1280]{1,0:T(8,128)S(1)}, bf16[256,2560]{1,0:T(8,128)(2,1)S(1)}) custom-call(s32[9]{0:T(128)S(1)} %stack.47.places, bf16[64,1280]{1,0:T(8,128)(2,1)S(1)} %get-tuple-element.54.near_ref, f32[8,1280]{1,0:T(8,128)S(1)} %get-tuple-element.55.facts_ref, ...), custom_call_target="tpu_custom_call" | custom-call | flops 1 | bytes 1 | tf_op jit(solution)/shard_map/enter/pallas_call | solution.py:38
  37.3 2.9 %grad_chunks.4 = (bf16[1024,1280]{1,0:T(8,128)(2,1)S(1)}, bf16[4,128,1280]{2,1,0:T(8,128)(2,1)S(1)}, f32[128,1280]{1,0:T(8,128)S(1)}) custom-call(s32[9]{0:T(128)S(1)} %stack.47.places, bf16[256,2560]{1,0:T(8,128)(2,1)S(1)} %get-tuple-element.65.refs_0_, ...), custom_call_target="tpu_custom_call", output_to_operand_aliasing={{0}: (10, {}), {1}: (11, {})} | custom-call | flops 1 | bytes 1 | tf_op jit(solution)/shard_map/grad_chunks/pallas_call | solution.py:38
  40.2 2.9 %grad_chunks.5 = (bf16[1024,1280]{1,0:T(8,128)(2,1)S(1)}, bf16[4,128,1280]{2,1,0:T(8,128)(2,1)S(1)}, bf16[64,1280]{1,0:T(8,128)(2,1)S(1)}, bf16[64,1280]{1,0:T(8,128)(2,1)S(1)}) custom-call(s32[9]{0:T(128)S(1)} %stack.47.places, bf16[256,2560]{1,0:T(8,128)(2,1)S(1)} %collective-permute-done.7.refs_0_, ...), custom_call_target="tpu_custom_call", output_to_operand_aliasing={{0}: (10, {}), {1}: (11, {})} | custom-call | flops 1 | bytes 1 | tf_op jit(solution)/shard_map/grad_chunks/pallas_call | solution.py:38
  44.0 1.9 %gated_chunks.2 = (bf16[256,1280]{1,0:T(8,128)(2,1)S(1)}, bf16[256,1280]{1,0:T(8,128)(2,1)S(1)}) custom-call(s32[9]{0:T(128)S(1)} %stack.47.places, bf16[1024,1280]{1,0:T(8,128)(2,1)S(1)} %get-tuple-element.48._.mixed_ref, bf16[1024,1280]{1,0:T(8,128)(2,1)S(1)} %get-tuple-element.49.refs_2_.refs_1_.gates_ref, ...), custom_call_target="tpu_custom_call" | custom-call | flops 1 | bytes 1 | tf_op jit(solution)/shard_map/gated_chunks/pallas_call | solution.py:38
  45.9 1.8 %project.4.rest_0_ = f32[256,2560]{1,0:T(8,128)S(1)} custom-call(bf16[256,1280]{1,0:T(8,128)(2,1)S(1)} %get-tuple-element.75.gated_ref, bf16[1280,2560]{1,0:T(8,128)(2,1)S(1)} %get-tuple-element.59.refs_7_.refs_6_.w_ref, bf16[256,1280]{1,0:T(8,128)(2,1)S(1)} %get-tuple-element.73.rest_0_), custom_call_target="tpu_custom_call" | custom-call | flops 23060000768 | bytes 1 | tf_op jit(solution)/shard_map/project/pallas_call | solution.py:38
  48.0 1.9 %project.5._ = bf16[256,2560]{1,0:T(8,128)(2,1)S(1)} custom-call(bf16[256,1280]{1,0:T(8,128)(2,1)S(1)} %collective-permute-done.9.gated_ref, bf16[1280,2560]{1,0:T(8,128)(2,1)S(1)} %get-tuple-element.74.w_ref, f32[256,2560]{1,0:T(8,128)S(1)} %project.4.rest_0_), custom_call_target="tpu_custom_call" | custom-call | flops 1 | bytes 1 | tf_op jit(solution)/shard_map/project/pallas_call | solution.py:38
  51.9 1.5 %collective-permute-start.12 = (bf16[80,1280]{1,0:T(8,128)(2,1)S(1)}, bf16[80,1280]{1,0:T(8,128)(2,1)S(1)}, u32[]{:S(2)}, u32[]{:S(2)}) collective-permute-start(bf16[80,1280]{1,0:T(8,128)(2,1)S(1)} %get-tuple-element.76.rest_0_), channel_id=1, source_target_pairs={{8,0},{12,4},{16,8},{20,12},{24,16},{28,20},{9,1},{13,5},{17,9},{2... | collective-permute-start | bytes 614408 | tf_op jit(solution)/shard_map/ppermute | solution.py:517
  53.4 3.7 %collective-permute-start.13 = (bf16[80,1280]{1,0:T(8,128)(2,1)S(1)}, bf16[80,1280]{1,0:T(8,128)(2,1)S(1)}, u32[]{:S(2)}, u32[]{:S(2)}) collective-permute-start(bf16[80,1280]{1,0:T(8,128)(2,1)S(1)} %get-tuple-element.76.rest_0_), channel_id=1, source_target_pairs={{0,16},{4,20},{8,24},{12,28},{16,0},{20,4},{24,8},{28,12},{1,17},{... | collective-permute-start | bytes 614408 | tf_op jit(solution)/shard_map/ppermute | solution.py:526
  57.2 1.9 %gated_chunks.3 = (bf16[256,1280]{1,0:T(8,128)(2,1)S(1)}, bf16[256,1280]{1,0:T(8,128)(2,1)S(1)}) custom-call(s32[9]{0:T(128)S(1)} %stack.47.places, bf16[1024,1280]{1,0:T(8,128)(2,1)S(1)} %get-tuple-element.48._.mixed_ref, bf16[1024,1280]{1,0:T(8,128)(2,1)S(1)} %get-tuple-element.49.refs_2_.refs_1_.gates_ref, ...), custom_call_target="tpu_custom_call" | custom-call | flops 1 | bytes 1 | tf_op jit(solution)/shard_map/gated_chunks/pallas_call | solution.py:38
  59.1 1.8 %project.6.rest_0_ = f32[256,2560]{1,0:T(8,128)S(1)} custom-call(bf16[256,1280]{1,0:T(8,128)(2,1)S(1)} %get-tuple-element.78.gated_ref, bf16[1280,2560]{1,0:T(8,128)(2,1)S(1)} %get-tuple-element.59.refs_7_.refs_6_.w_ref, bf16[256,1280]{1,0:T(8,128)(2,1)S(1)} %get-tuple-element.77.rest_0_), custom_call_target="tpu_custom_call" | custom-call | flops 9223999488 | bytes 1 | tf_op jit(solution)/shard_map/project/pallas_call | solution.py:38
  61.2 1.9 %project.7.own_ref._ = f32[256,2560]{1,0:T(8,128)S(1)} custom-call(bf16[256,1280]{1,0:T(8,128)(2,1)S(1)} %collective-permute-done.10.gated_ref, bf16[1280,2560]{1,0:T(8,128)(2,1)S(1)} %get-tuple-element.74.w_ref, f32[256,2560]{1,0:T(8,128)S(1)} %project.6.rest_0_), custom_call_target="tpu_custom_call" | custom-call | flops 1 | bytes 1 | tf_op jit(solution)/shard_map/project/pallas_call | solution.py:38
  63.1 3.4 %inside_backward.3._.part_ref = bf16[1024,1280]{1,0:T(8,128)(2,1)S(1)} custom-call(s32[9]{0:T(128)S(1)} %stack.47.places, bf16[1024,1280]{1,0:T(8,128)(2,1)S(1)} %get-tuple-element.79.x_ref, bf16[1024,128]{1,0:T(8,128)(2,1)S(1)} %get-tuple-element.44.b_ref, ...), custom_call_target="tpu_custom_call", output_to_operand_aliasing={{}: (7, {})} | custom-call | flops 1 | bytes 1 | tf_op jit(solution)/shard_map/inside_backward/pallas_call | solution.py:38
  66.5 4.1 %collective-permute-done.13.two_ref = bf16[80,1280]{1,0:T(8,128)(2,1)S(1)} collective-permute-done((bf16[80,1280]{1,0:T(8,128)(2,1)S(1)}, bf16[80,1280]{1,0:T(8,128)(2,1)S(1)}, u32[]{:S(2)}, u32[]{:S(2)}) %collective-permute-start.13) | collective-permute-done | bytes 204832 | tf_op jit(solution)/shard_map/ppermute | solution.py:526
  71.3 1.6 %collective-permute-start.14 = (bf16[64,1280]{1,0:T(8,128)(2,1)S(1)}, bf16[64,1280]{1,0:T(8,128)(2,1)S(1)}, u32[]{:S(2)}, u32[]{:S(2)}) collective-permute-start(bf16[64,1280]{1,0:T(8,128)(2,1)S(1)} %get-tuple-element.85), channel_id=1, source_target_pairs={{0,4},{4,0},{8,12},{12,8},{16,20},{20,16},{24,28},{28,24},{1,5},{5... | collective-permute-start | bytes 491528 | tf_op jit(solution)/shard_map/ppermute | solution.py:521
  72.9 3.8 %collective-permute-done.14.other_ref = bf16[64,1280]{1,0:T(8,128)(2,1)S(1)} collective-permute-done((bf16[64,1280]{1,0:T(8,128)(2,1)S(1)}, bf16[64,1280]{1,0:T(8,128)(2,1)S(1)}, u32[]{:S(2)}, u32[]{:S(2)}) %collective-permute-start.14) | collective-permute-done | bytes 163872 | tf_op jit(solution)/shard_map/ppermute | solution.py:521
  76.7 3.2 %back_tail.1 = bf16[1024,1280]{1,0:T(8,128)(2,1)} custom-call(s32[9]{0:T(128)S(1)} %stack.47.places, bf16[1024,1280]{1,0:T(8,128)(2,1)S(1)} %inside_backward.3._.part_ref, bf16[1024,128]{1,0:T(8,128)(2,1)S(1)} %get-tuple-element.44.b_ref, bf16[1024,128]{1,0:T(8,128)(2,1)S(1)} %get-tuple-element.80.exit_ref, ...), custom_call_target="tpu_custom_call" | custom-call | flops 1730000000 | bytes 1 | tf_op jit(solution)/shard_map/back_tail/pallas_call | solution.py:38
  (33 shorter events, 9.6 us)
Async XLA Ops:
  0.6 9.6 %copy-start = (f32[20]{0:T(128)S(1)}, f32[20]{0:T(128)}, u32[]{:S(2)}) copy-start(f32[20]{0:T(128)} %param.14) | copy-start | bytes 244
  0.6 29.7 %collective-permute-start.4 = (bf16[1280,2560]{1,0:T(8,128)(2,1)}, bf16[1280,2560]{1,0:T(8,128)(2,1)}, u32[]{:S(2)}, u32[]{:S(2)}) collective-permute-start(bf16[1280,2560]{1,0:T(8,128)(2,1)} %rest_1_.1), channel_id=1, source_target_pairs={{0,1},{1,0},{2,3},{3,2},{4,5},{5,4},{6,7},{7,6},{8,9},{9,8},{10,11... | collective-permute-start | bytes 19660808 | tf_op jit(solution)/shard_map/ppermute | solution.py:521
  1.2 23.1 %collective-permute-start.3 = (bf16[256,2560]{1,0:T(8,128)(2,1)}, bf16[256,2560]{1,0:T(8,128)(2,1)}, u32[]{:S(2)}, u32[]{:S(2)}) collective-permute-start(bf16[256,2560]{1,0:T(8,128)(2,1)} %rest_2_.1), channel_id=1, source_target_pairs={{0,1},{1,0},{2,3},{3,2},{4,5},{5,4},{6,7},{7,6},{8,9},{9,8},{10,11... | collective-permute-start | bytes 3932168 | tf_op jit(solution)/shard_map/ppermute | solution.py:521
  1.2 32.7 %collective-permute-start.5 = (bf16[256,2560]{1,0:T(8,128)(2,1)}, bf16[256,2560]{1,0:T(8,128)(2,1)}, u32[]{:S(2)}, u32[]{:S(2)}) collective-permute-start(bf16[256,2560]{1,0:T(8,128)(2,1)} %rest_2_.1), channel_id=1, source_target_pairs={{0,2},{1,3},{2,0},{3,1},{4,6},{5,7},{6,4},{7,5},{8,10},{9,11},{10,... | collective-permute-start | bytes 3932168 | tf_op jit(solution)/shard_map/ppermute | solution.py:526
  8.6 8.8 %collective-permute-start = (bf16[80,1280]{1,0:T(8,128)(2,1)S(1)}, bf16[80,1280]{1,0:T(8,128)(2,1)S(1)}, u32[]{:S(2)}, u32[]{:S(2)}) collective-permute-start(bf16[80,1280]{1,0:T(8,128)(2,1)S(1)} %get-tuple-element.47._), channel_id=1, source_target_pairs={{0,4},{4,0},{8,12},{12,8},{16,20},{20,16},{24,28},{28,24},{1,5},{5... | collective-permute-start | bytes 614408 | tf_op jit(solution)/shard_map/ppermute | solution.py:521
  18.1 15.8 %collective-permute-start.1 = (bf16[80,1280]{1,0:T(8,128)(2,1)S(1)}, bf16[80,1280]{1,0:T(8,128)(2,1)S(1)}, u32[]{:S(2)}, u32[]{:S(2)}) collective-permute-start(bf16[80,1280]{1,0:T(8,128)(2,1)S(1)} %get-tuple-element.56.refs_8_), channel_id=1, source_target_pairs={{0,8},{4,12},{8,16},{12,20},{16,24},{20,28},{1,9},{5,13},{9,17},{1... | collective-permute-start | bytes 614408 | tf_op jit(solution)/shard_map/ppermute | solution.py:517
  21.6 12.3 %collective-permute-start.2 = (bf16[80,1280]{1,0:T(8,128)(2,1)S(1)}, bf16[80,1280]{1,0:T(8,128)(2,1)S(1)}, u32[]{:S(2)}, u32[]{:S(2)}) collective-permute-start(bf16[80,1280]{1,0:T(8,128)(2,1)S(1)} %get-tuple-element.56.refs_8_), channel_id=1, source_target_pairs={{0,16},{4,20},{8,24},{12,28},{16,0},{20,4},{24,8},{28,12},{1,17},{... | collective-permute-start | bytes 614408 | tf_op jit(solution)/shard_map/ppermute | solution.py:526
  35.8 4.4 %collective-permute-start.7 = (bf16[256,2560]{1,0:T(8,128)(2,1)S(1)}, bf16[256,2560]{1,0:T(8,128)(2,1)S(1)}, u32[]{:S(2)}, u32[]{:S(2)}) collective-permute-start(bf16[256,2560]{1,0:T(8,128)(2,1)S(1)} %get-tuple-element.65.refs_0_), channel_id=1, source_target_pairs={{0,1},{1,0},{2,3},{3,2},{4,5},{5,4},{6,7},{7,6},{8,9},{9,8},{10,11... | collective-permute-start | bytes 3932168 | tf_op jit(solution)/shard_map/ppermute | solution.py:521
  35.9 8.1 %collective-permute-start.6 = (bf16[64,1280]{1,0:T(8,128)(2,1)S(1)}, bf16[64,1280]{1,0:T(8,128)(2,1)S(1)}, u32[]{:S(2)}, u32[]{:S(2)}) collective-permute-start(bf16[64,1280]{1,0:T(8,128)(2,1)S(1)} %get-tuple-element.64.refs_7_), channel_id=1, source_target_pairs={{0,4},{4,0},{8,12},{12,8},{16,20},{20,16},{24,28},{28,24},{1,5},{5... | collective-permute-start | bytes 491528 | tf_op jit(solution)/shard_map/ppermute | solution.py:521
  43.2 8.1 %collective-permute-start.8 = (bf16[64,1280]{1,0:T(8,128)(2,1)S(1)}, bf16[64,1280]{1,0:T(8,128)(2,1)S(1)}, u32[]{:S(2)}, u32[]{:S(2)}) collective-permute-start(bf16[64,1280]{1,0:T(8,128)(2,1)S(1)} %get-tuple-element.71.rest_0_), channel_id=1, source_target_pairs={{0,4},{4,0},{8,12},{12,8},{16,20},{20,16},{24,28},{28,24},{1,5},{5... | collective-permute-start | bytes 491528 | tf_op jit(solution)/shard_map/ppermute | solution.py:521
  45.9 2.2 %collective-permute-start.9 = (bf16[256,1280]{1,0:T(8,128)(2,1)S(1)}, bf16[256,1280]{1,0:T(8,128)(2,1)S(1)}, u32[]{:S(2)}, u32[]{:S(2)}) collective-permute-start(bf16[256,1280]{1,0:T(8,128)(2,1)S(1)} %get-tuple-element.73.rest_0_), channel_id=1, source_target_pairs={{0,1},{1,0},{2,3},{3,2},{4,5},{5,4},{6,7},{7,6},{8,9},{9,8},{10,11... | collective-permute-start | bytes 1966088 | tf_op jit(solution)/shard_map/ppermute | solution.py:521
  49.9 31.0 %collective-permute-start.11 = (bf16[256,2560]{1,0:T(8,128)(2,1)S(1)}, bf16[256,2560]{1,0:T(8,128)(2,1)S(1)}, u32[]{:S(2)}, u32[]{:S(2)}) collective-permute-start(bf16[256,2560]{1,0:T(8,128)(2,1)S(1)} %project.5._), channel_id=1, source_target_pairs={{0,2},{1,3},{2,0},{3,1},{4,6},{5,7},{6,4},{7,5},{8,10},{9,11},{10,... | collective-permute-start | bytes 3932168 | tf_op jit(solution)/shard_map/ppermute | solution.py:526
  51.9 14.6 %collective-permute-start.12 = (bf16[80,1280]{1,0:T(8,128)(2,1)S(1)}, bf16[80,1280]{1,0:T(8,128)(2,1)S(1)}, u32[]{:S(2)}, u32[]{:S(2)}) collective-permute-start(bf16[80,1280]{1,0:T(8,128)(2,1)S(1)} %get-tuple-element.76.rest_0_), channel_id=1, source_target_pairs={{8,0},{12,4},{16,8},{20,12},{24,16},{28,20},{9,1},{13,5},{17,9},{2... | collective-permute-start | bytes 614408 | tf_op jit(solution)/shard_map/ppermute | solution.py:517
  53.4 17.1 %collective-permute-start.13 = (bf16[80,1280]{1,0:T(8,128)(2,1)S(1)}, bf16[80,1280]{1,0:T(8,128)(2,1)S(1)}, u32[]{:S(2)}, u32[]{:S(2)}) collective-permute-start(bf16[80,1280]{1,0:T(8,128)(2,1)S(1)} %get-tuple-element.76.rest_0_), channel_id=1, source_target_pairs={{0,16},{4,20},{8,24},{12,28},{16,0},{20,4},{24,8},{28,12},{1,17},{... | collective-permute-start | bytes 614408 | tf_op jit(solution)/shard_map/ppermute | solution.py:526
  59.1 2.2 %collective-permute-start.10 = (bf16[256,1280]{1,0:T(8,128)(2,1)S(1)}, bf16[256,1280]{1,0:T(8,128)(2,1)S(1)}, u32[]{:S(2)}, u32[]{:S(2)}) collective-permute-start(bf16[256,1280]{1,0:T(8,128)(2,1)S(1)} %get-tuple-element.77.rest_0_), channel_id=1, source_target_pairs={{0,1},{1,0},{2,3},{3,2},{4,5},{5,4},{6,7},{7,6},{8,9},{9,8},{10,11... | collective-permute-start | bytes 1966088 | tf_op jit(solution)/shard_map/ppermute | solution.py:521
  71.3 5.4 %collective-permute-start.14 = (bf16[64,1280]{1,0:T(8,128)(2,1)S(1)}, bf16[64,1280]{1,0:T(8,128)(2,1)S(1)}, u32[]{:S(2)}, u32[]{:S(2)}) collective-permute-start(bf16[64,1280]{1,0:T(8,128)(2,1)S(1)} %get-tuple-element.85), channel_id=1, source_target_pairs={{0,4},{4,0},{8,12},{12,8},{16,20},{20,16},{24,28},{28,24},{1,5},{5... | collective-permute-start | bytes 491528 | tf_op jit(solution)/shard_map/ppermute | solution.py:521

commit v5 on v4

--- a/solution.py
+++ b/solution.py
@@ -12,7 +12,6 @@
 LANES = 128
 TILE = 16
 PARTS = 4
-HALVES = 1
 TAIL_COST, FAR_COST, NEAR_COST = 1.73e9, 2.306e10, 9.224e9
 LOG2E = math.log2(math.e)
 F32 = jnp.float32
@@ -382,14 +381,12 @@
 def sum_kernel(own_ref, *rest):
     landed_refs, (out_hbm, out_ref, sems) = rest[:-3], rest[-3:]
     outgoing = []
-    width = landed_refs[0].shape[1] if landed_refs else own_ref.shape[1]
-    for i in range(own_ref.shape[1] // width):
-        at = pl.ds(i * width, width)
+    for j, at in enumerate(tiling(own_ref.shape[1])):
         total = own_ref[:, at]
-        for ref in landed_refs[i :: own_ref.shape[1] // width]:
-            total = total + ref[...].astype(F32)
+        for ref in landed_refs:
+            total = total + ref[:, at].astype(F32)
         out_ref[:, at] = total.astype(BF16)
-        outgoing += start(sems.at[i], (out_ref.at[:, at], out_hbm.at[:, at]))
+        outgoing += start(sems.at[j], (out_ref.at[:, at], out_hbm.at[:, at]))
     for copy in outgoing:
         copy.wait()
 
@@ -403,7 +400,7 @@
         (own, *landed),
         scratch=[
             pltpu.VMEM(own.shape, BF16),
-            pltpu.SemaphoreType.DMA((HALVES, 1)),
+            pltpu.SemaphoreType.DMA((len(tiling(own.shape[1])), 1)),
         ],
     )[0]
 
@@ -698,7 +695,7 @@
     for d in range(chips - 1):
         give, stay = gated((5 + 4 * d, 6 + 4 * d), after)
         (after,) = project(stay, weight, None, F32, (give,), flops=FAR_COST)
-        for total in project(swapped(give, "head"), mate_weight, after, BF16, count=HALVES):
+        for total in project(swapped(give, "head"), mate_weight, after, BF16):
             landed.append(rotated(total, "head", 2 * (d + 1)))
             after = total
     pair, near = small(

time: 82.6 us -> 82.5 us (level)
  no operation moved by 1% of the time
where the time goes in v5:
time: 82.5 us; the launch traced here: 82.3 us
  Pallas kernels  49.6 us (60%)
  starting transfers between devices  21.8 us (26%)
  waiting for transfers between devices  9.47 us (11%)
  between operations  1.07 us (1%)
    pallas_call x19, Pallas kernels, call(): pl.pallas_call(kernel, in_specs=in_specs, out_specs=[VM if o.memory_space...  49.6 us
    ppermute x4, starting transfers between devices, rotated(): lax.ppermute(block, axis, [(i, (i + distance) % size) for i in range(size)])  10.6 us
    ppermute x9, starting transfers between devices, swapped(): lax.ppermute(block, axis, [(i, i ^ 1) for i in range(lax.axis_size(axis))])  6.16 us
    ppermute x4, waiting for transfers between devices, rotated(): lax.ppermute(block, axis, [(i, (i + distance) % size) for i in range(size)])  5.21 us
    ppermute x2, starting transfers between devices, shifted(): return lax.ppermute(block, axis, route)  5.01 us
    ppermute x9, waiting for transfers between devices, swapped(): lax.ppermute(block, axis, [(i, i ^ 1) for i in range(lax.axis_size(axis))])  4.26 us
  transfers between devices with their start and end apart: 15, of which 5 were waited for; matrix products, arithmetic and copies ran while one was open for 0% of the time, Pallas kernels for 57%

profile of v5, /device:TPU:0, one launch (start us, length us, event | category | flops | bytes accessed | tf_op | source)
XLA Modules:
  0.0 82.3 jit_solution(10842093783746464071)
XLA Ops:
  1.2 2.9 %collective-permute-start.5 = (bf16[256,2560]{1,0:T(8,128)(2,1)}, bf16[256,2560]{1,0:T(8,128)(2,1)}, u32[]{:S(2)}, u32[]{:S(2)}) collective-permute-start(bf16[256,2560]{1,0:T(8,128)(2,1)} %rest_2_.1), channel_id=1, source_target_pairs={{0,2},{1,3},{2,0},{3,1},{4,6},{5,7},{6,4},{7,5},{8,10},{9,11},{10,... | collective-permute-start | bytes 3932168 | tf_op jit(solution)/shard_map/ppermute | solution.py:523
  4.3 4.3 %local_states.1 = (f32[4,24,256]{2,1,0:T(8,128)S(1)}, bf16[1024,128]{1,0:T(8,128)(2,1)S(1)}, bf16[1024,128]{1,0:T(8,128)(2,1)S(1)}, bf16[4,128,1280]{2,1,0:T(8,1...) custom-call(s32[9]{0:T(128)S(1)} %stack.47.places, ...), custom_call_target="tpu_custom_call" | custom-call | flops 1 | bytes 1 | tf_op jit(solution)/shard_map/local_states/pallas_call | solution.py:37
  8.6 1.6 %collective-permute-start = (bf16[80,1280]{1,0:T(8,128)(2,1)S(1)}, bf16[80,1280]{1,0:T(8,128)(2,1)S(1)}, u32[]{:S(2)}, u32[]{:S(2)}) collective-permute-start(bf16[80,1280]{1,0:T(8,128)(2,1)S(1)} %get-tuple-element.47._), channel_id=1, source_target_pairs={{0,4},{4,0},{8,12},{12,8},{16,20},{20,16},{24,28},{28,24},{1,5},{5... | collective-permute-start | bytes 614408 | tf_op jit(solution)/shard_map/ppermute | solution.py:518
  10.4 7.0 %inside_forward.1 = (bf16[1024,1280]{1,0:T(8,128)(2,1)S(1)}, bf16[1024,1280]{1,0:T(8,128)(2,1)S(1)}, bf16[1280,2560]{1,0:T(8,128)(2,1)S(1)}, bf16[256,2560]{1,0:T(8,128)(2,1)S(1)}) custom-call(s32[9]{0:T(128)S(1)} %stack.47.places, bf16[1024,1280]{1,0:T(8,128)(2,1)} %x_ref.1, bf16[1024,128]{1,0:T(8,128)(2,1)S(1)} %get-tuple-element.44.b_ref, ...), custom_call_target="tpu_custom_call" | custom-call | flops 1 | bytes 1 | tf_op jit(solution)/shard_map/inside_forward/pallas_call | solution.py:37
  18.1 3.5 %collective-permute-start.1 = (bf16[80,1280]{1,0:T(8,128)(2,1)S(1)}, bf16[80,1280]{1,0:T(8,128)(2,1)S(1)}, u32[]{:S(2)}, u32[]{:S(2)}) collective-permute-start(bf16[80,1280]{1,0:T(8,128)(2,1)S(1)} %get-tuple-element.56.refs_8_), channel_id=1, source_target_pairs={{0,8},{4,12},{8,16},{12,20},{16,24},{20,28},{1,9},{5,13},{9,17},{1... | collective-permute-start | bytes 614408 | tf_op jit(solution)/shard_map/ppermute | solution.py:514
  21.6 2.6 %collective-permute-start.2 = (bf16[80,1280]{1,0:T(8,128)(2,1)S(1)}, bf16[80,1280]{1,0:T(8,128)(2,1)S(1)}, u32[]{:S(2)}, u32[]{:S(2)}) collective-permute-start(bf16[80,1280]{1,0:T(8,128)(2,1)S(1)} %get-tuple-element.56.refs_8_), channel_id=1, source_target_pairs={{0,16},{4,20},{8,24},{12,28},{16,0},{20,4},{24,8},{28,12},{1,17},{... | collective-permute-start | bytes 614408 | tf_op jit(solution)/shard_map/ppermute | solution.py:523
  24.3 6.1 %grad_chunks.3 = (bf16[1024,1280]{1,0:T(8,128)(2,1)S(1)}, bf16[4,128,1280]{2,1,0:T(8,128)(2,1)S(1)}, f32[128,1280]{1,0:T(8,128)S(1)}) custom-call(s32[9]{0:T(128)S(1)} %stack.47.places, bf16[256,2560]{1,0:T(8,128)(2,1)S(1)} %get-tuple-element.57.refs_0_, bf16[256,2560]{1,0:T(8,128)(2,1)} %collective-permute-done.3.refs_1_, ...), custom_call_target="tpu_custom_call" | custom-call | flops 1 | bytes 1 | tf_op jit(solution)/shard_map/grad_chunks/pallas_call | solution.py:37
  30.4 3.6 %inside_backward.2 = (bf16[1024,1280]{1,0:T(8,128)(2,1)S(1)}, bf16[1280,2560]{1,0:T(8,128)(2,1)S(1)}) custom-call(s32[9]{0:T(128)S(1)} %stack.47.places, bf16[1024,1280]{1,0:T(8,128)(2,1)S(1)} %get-tuple-element.60.x_ref.refs_9_, bf16[1024,128]{1,0:T(8,128)(2,1)S(1)} %get-tuple-element.44.b_ref, ...), custom_call_target="tpu_custom_call" | custom-call | flops 1 | bytes 1 | tf_op jit(solution)/shard_map/inside_backward/pallas_call | solution.py:37
  34.0 1.8 %enter.1 = (bf16[64,1280]{1,0:T(8,128)(2,1)S(1)}, bf16[64,1280]{1,0:T(8,128)(2,1)S(1)}, f32[8,1280]{1,0:T(8,128)S(1)}, bf16[256,2560]{1,0:T(8,128)(2,1)S(1)}) custom-call(s32[9]{0:T(128)S(1)} %stack.47.places, bf16[64,1280]{1,0:T(8,128)(2,1)S(1)} %get-tuple-element.54.near_ref, f32[8,1280]{1,0:T(8,128)S(1)} %get-tuple-element.55.facts_ref, ...), custom_call_target="tpu_custom_call" | custom-call | flops 1 | bytes 1 | tf_op jit(solution)/shard_map/enter/pallas_call | solution.py:37
  37.3 2.9 %grad_chunks.4 = (bf16[1024,1280]{1,0:T(8,128)(2,1)S(1)}, bf16[4,128,1280]{2,1,0:T(8,128)(2,1)S(1)}, f32[128,1280]{1,0:T(8,128)S(1)}) custom-call(s32[9]{0:T(128)S(1)} %stack.47.places, bf16[256,2560]{1,0:T(8,128)(2,1)S(1)} %get-tuple-element.65.refs_0_, ...), custom_call_target="tpu_custom_call", output_to_operand_aliasing={{0}: (10, {}), {1}: (11, {})} | custom-call | flops 1 | bytes 1 | tf_op jit(solution)/shard_map/grad_chunks/pallas_call | solution.py:37
  40.2 2.9 %grad_chunks.5 = (bf16[1024,1280]{1,0:T(8,128)(2,1)S(1)}, bf16[4,128,1280]{2,1,0:T(8,128)(2,1)S(1)}, bf16[64,1280]{1,0:T(8,128)(2,1)S(1)}, bf16[64,1280]{1,0:T(8,128)(2,1)S(1)}) custom-call(s32[9]{0:T(128)S(1)} %stack.47.places, bf16[256,2560]{1,0:T(8,128)(2,1)S(1)} %collective-permute-done.7.refs_0_, ...), custom_call_target="tpu_custom_call", output_to_operand_aliasing={{0}: (10, {}), {1}: (11, {})} | custom-call | flops 1 | bytes 1 | tf_op jit(solution)/shard_map/grad_chunks/pallas_call | solution.py:37
  44.0 1.9 %gated_chunks.2 = (bf16[256,1280]{1,0:T(8,128)(2,1)S(1)}, bf16[256,1280]{1,0:T(8,128)(2,1)S(1)}) custom-call(s32[9]{0:T(128)S(1)} %stack.47.places, bf16[1024,1280]{1,0:T(8,128)(2,1)S(1)} %get-tuple-element.48._.mixed_ref, bf16[1024,1280]{1,0:T(8,128)(2,1)S(1)} %get-tuple-element.49.refs_2_.refs_1_.gates_ref, ...), custom_call_target="tpu_custom_call" | custom-call | flops 1 | bytes 1 | tf_op jit(solution)/shard_map/gated_chunks/pallas_call | solution.py:37
  45.9 1.8 %project.4.rest_0_ = f32[256,2560]{1,0:T(8,128)S(1)} custom-call(bf16[256,1280]{1,0:T(8,128)(2,1)S(1)} %get-tuple-element.75.gated_ref, bf16[1280,2560]{1,0:T(8,128)(2,1)S(1)} %get-tuple-element.59.refs_7_.refs_6_.w_ref, bf16[256,1280]{1,0:T(8,128)(2,1)S(1)} %get-tuple-element.73.rest_0_), custom_call_target="tpu_custom_call" | custom-call | flops 23060000768 | bytes 1 | tf_op jit(solution)/shard_map/project/pallas_call | solution.py:37
  48.0 1.9 %project.5._ = bf16[256,2560]{1,0:T(8,128)(2,1)S(1)} custom-call(bf16[256,1280]{1,0:T(8,128)(2,1)S(1)} %collective-permute-done.9.gated_ref, bf16[1280,2560]{1,0:T(8,128)(2,1)S(1)} %get-tuple-element.74.w_ref, f32[256,2560]{1,0:T(8,128)S(1)} %project.4.rest_0_), custom_call_target="tpu_custom_call" | custom-call | flops 1 | bytes 1 | tf_op jit(solution)/shard_map/project/pallas_call | solution.py:37
  51.9 1.5 %collective-permute-start.12 = (bf16[80,1280]{1,0:T(8,128)(2,1)S(1)}, bf16[80,1280]{1,0:T(8,128)(2,1)S(1)}, u32[]{:S(2)}, u32[]{:S(2)}) collective-permute-start(bf16[80,1280]{1,0:T(8,128)(2,1)S(1)} %get-tuple-element.76.rest_0_), channel_id=1, source_target_pairs={{8,0},{12,4},{16,8},{20,12},{24,16},{28,20},{9,1},{13,5},{17,9},{2... | collective-permute-start | bytes 614408 | tf_op jit(solution)/shard_map/ppermute | solution.py:514
  53.4 3.7 %collective-permute-start.13 = (bf16[80,1280]{1,0:T(8,128)(2,1)S(1)}, bf16[80,1280]{1,0:T(8,128)(2,1)S(1)}, u32[]{:S(2)}, u32[]{:S(2)}) collective-permute-start(bf16[80,1280]{1,0:T(8,128)(2,1)S(1)} %get-tuple-element.76.rest_0_), channel_id=1, source_target_pairs={{0,16},{4,20},{8,24},{12,28},{16,0},{20,4},{24,8},{28,12},{1,17},{... | collective-permute-start | bytes 614408 | tf_op jit(solution)/shard_map/ppermute | solution.py:523
  57.2 1.9 %gated_chunks.3 = (bf16[256,1280]{1,0:T(8,128)(2,1)S(1)}, bf16[256,1280]{1,0:T(8,128)(2,1)S(1)}) custom-call(s32[9]{0:T(128)S(1)} %stack.47.places, bf16[1024,1280]{1,0:T(8,128)(2,1)S(1)} %get-tuple-element.48._.mixed_ref, bf16[1024,1280]{1,0:T(8,128)(2,1)S(1)} %get-tuple-element.49.refs_2_.refs_1_.gates_ref, ...), custom_call_target="tpu_custom_call" | custom-call | flops 1 | bytes 1 | tf_op jit(solution)/shard_map/gated_chunks/pallas_call | solution.py:37
  59.1 1.8 %project.6.rest_0_ = f32[256,2560]{1,0:T(8,128)S(1)} custom-call(bf16[256,1280]{1,0:T(8,128)(2,1)S(1)} %get-tuple-element.78.gated_ref, bf16[1280,2560]{1,0:T(8,128)(2,1)S(1)} %get-tuple-element.59.refs_7_.refs_6_.w_ref, bf16[256,1280]{1,0:T(8,128)(2,1)S(1)} %get-tuple-element.77.rest_0_), custom_call_target="tpu_custom_call" | custom-call | flops 9223999488 | bytes 1 | tf_op jit(solution)/shard_map/project/pallas_call | solution.py:37
  61.2 1.9 %project.7.own_ref._ = f32[256,2560]{1,0:T(8,128)S(1)} custom-call(bf16[256,1280]{1,0:T(8,128)(2,1)S(1)} %collective-permute-done.10.gated_ref, bf16[1280,2560]{1,0:T(8,128)(2,1)S(1)} %get-tuple-element.74.w_ref, f32[256,2560]{1,0:T(8,128)S(1)} %project.6.rest_0_), custom_call_target="tpu_custom_call" | custom-call | flops 1 | bytes 1 | tf_op jit(solution)/shard_map/project/pallas_call | solution.py:37
  63.1 3.4 %inside_backward.3._.part_ref = bf16[1024,1280]{1,0:T(8,128)(2,1)S(1)} custom-call(s32[9]{0:T(128)S(1)} %stack.47.places, bf16[1024,1280]{1,0:T(8,128)(2,1)S(1)} %get-tuple-element.79.x_ref, bf16[1024,128]{1,0:T(8,128)(2,1)S(1)} %get-tuple-element.44.b_ref, ...), custom_call_target="tpu_custom_call", output_to_operand_aliasing={{}: (7, {})} | custom-call | flops 1 | bytes 1 | tf_op jit(solution)/shard_map/inside_backward/pallas_call | solution.py:37
  66.5 4.1 %collective-permute-done.13.two_ref = bf16[80,1280]{1,0:T(8,128)(2,1)S(1)} collective-permute-done((bf16[80,1280]{1,0:T(8,128)(2,1)S(1)}, bf16[80,1280]{1,0:T(8,128)(2,1)S(1)}, u32[]{:S(2)}, u32[]{:S(2)}) %collective-permute-start.13) | collective-permute-done | bytes 204832 | tf_op jit(solution)/shard_map/ppermute | solution.py:523
  71.3 1.6 %collective-permute-start.14 = (bf16[64,1280]{1,0:T(8,128)(2,1)S(1)}, bf16[64,1280]{1,0:T(8,128)(2,1)S(1)}, u32[]{:S(2)}, u32[]{:S(2)}) collective-permute-start(bf16[64,1280]{1,0:T(8,128)(2,1)S(1)} %get-tuple-element.85), channel_id=1, source_target_pairs={{0,4},{4,0},{8,12},{12,8},{16,20},{20,16},{24,28},{28,24},{1,5},{5... | collective-permute-start | bytes 491528 | tf_op jit(solution)/shard_map/ppermute | solution.py:518
  72.9 3.8 %collective-permute-done.14.other_ref = bf16[64,1280]{1,0:T(8,128)(2,1)S(1)} collective-permute-done((bf16[64,1280]{1,0:T(8,128)(2,1)S(1)}, bf16[64,1280]{1,0:T(8,128)(2,1)S(1)}, u32[]{:S(2)}, u32[]{:S(2)}) %collective-permute-start.14) | collective-permute-done | bytes 163872 | tf_op jit(solution)/shard_map/ppermute | solution.py:518
  76.7 3.2 %back_tail.1 = bf16[1024,1280]{1,0:T(8,128)(2,1)} custom-call(s32[9]{0:T(128)S(1)} %stack.47.places, bf16[1024,1280]{1,0:T(8,128)(2,1)S(1)} %inside_backward.3._.part_ref, bf16[1024,128]{1,0:T(8,128)(2,1)S(1)} %get-tuple-element.44.b_ref, bf16[1024,128]{1,0:T(8,128)(2,1)S(1)} %get-tuple-element.80.exit_ref, ...), custom_call_target="tpu_custom_call" | custom-call | flops 1730000000 | bytes 1 | tf_op jit(solution)/shard_map/back_tail/pallas_call | solution.py:37
  (33 shorter events, 9.4 us)
Async XLA Ops:
  0.6 9.6 %copy-start = (f32[20]{0:T(128)S(1)}, f32[20]{0:T(128)}, u32[]{:S(2)}) copy-start(f32[20]{0:T(128)} %param.14) | copy-start | bytes 244
  0.6 29.7 %collective-permute-start.4 = (bf16[1280,2560]{1,0:T(8,128)(2,1)}, bf16[1280,2560]{1,0:T(8,128)(2,1)}, u32[]{:S(2)}, u32[]{:S(2)}) collective-permute-start(bf16[1280,2560]{1,0:T(8,128)(2,1)} %rest_1_.1), channel_id=1, source_target_pairs={{0,1},{1,0},{2,3},{3,2},{4,5},{5,4},{6,7},{7,6},{8,9},{9,8},{10,11... | collective-permute-start | bytes 19660808 | tf_op jit(solution)/shard_map/ppermute | solution.py:518
  1.2 23.1 %collective-permute-start.3 = (bf16[256,2560]{1,0:T(8,128)(2,1)}, bf16[256,2560]{1,0:T(8,128)(2,1)}, u32[]{:S(2)}, u32[]{:S(2)}) collective-permute-start(bf16[256,2560]{1,0:T(8,128)(2,1)} %rest_2_.1), channel_id=1, source_target_pairs={{0,1},{1,0},{2,3},{3,2},{4,5},{5,4},{6,7},{7,6},{8,9},{9,8},{10,11... | collective-permute-start | bytes 3932168 | tf_op jit(solution)/shard_map/ppermute | solution.py:518
  1.2 32.7 %collective-permute-start.5 = (bf16[256,2560]{1,0:T(8,128)(2,1)}, bf16[256,2560]{1,0:T(8,128)(2,1)}, u32[]{:S(2)}, u32[]{:S(2)}) collective-permute-start(bf16[256,2560]{1,0:T(8,128)(2,1)} %rest_2_.1), channel_id=1, source_target_pairs={{0,2},{1,3},{2,0},{3,1},{4,6},{5,7},{6,4},{7,5},{8,10},{9,11},{10,... | collective-permute-start | bytes 3932168 | tf_op jit(solution)/shard_map/ppermute | solution.py:523
  8.6 8.8 %collective-permute-start = (bf16[80,1280]{1,0:T(8,128)(2,1)S(1)}, bf16[80,1280]{1,0:T(8,128)(2,1)S(1)}, u32[]{:S(2)}, u32[]{:S(2)}) collective-permute-start(bf16[80,1280]{1,0:T(8,128)(2,1)S(1)} %get-tuple-element.47._), channel_id=1, source_target_pairs={{0,4},{4,0},{8,12},{12,8},{16,20},{20,16},{24,28},{28,24},{1,5},{5... | collective-permute-start | bytes 614408 | tf_op jit(solution)/shard_map/ppermute | solution.py:518
  18.1 15.8 %collective-permute-start.1 = (bf16[80,1280]{1,0:T(8,128)(2,1)S(1)}, bf16[80,1280]{1,0:T(8,128)(2,1)S(1)}, u32[]{:S(2)}, u32[]{:S(2)}) collective-permute-start(bf16[80,1280]{1,0:T(8,128)(2,1)S(1)} %get-tuple-element.56.refs_8_), channel_id=1, source_target_pairs={{0,8},{4,12},{8,16},{12,20},{16,24},{20,28},{1,9},{5,13},{9,17},{1... | collective-permute-start | bytes 614408 | tf_op jit(solution)/shard_map/ppermute | solution.py:514
  21.6 12.3 %collective-permute-start.2 = (bf16[80,1280]{1,0:T(8,128)(2,1)S(1)}, bf16[80,1280]{1,0:T(8,128)(2,1)S(1)}, u32[]{:S(2)}, u32[]{:S(2)}) collective-permute-start(bf16[80,1280]{1,0:T(8,128)(2,1)S(1)} %get-tuple-element.56.refs_8_), channel_id=1, source_target_pairs={{0,16},{4,20},{8,24},{12,28},{16,0},{20,4},{24,8},{28,12},{1,17},{... | collective-permute-start | bytes 614408 | tf_op jit(solution)/shard_map/ppermute | solution.py:523
  35.8 4.4 %collective-permute-start.7 = (bf16[256,2560]{1,0:T(8,128)(2,1)S(1)}, bf16[256,2560]{1,0:T(8,128)(2,1)S(1)}, u32[]{:S(2)}, u32[]{:S(2)}) collective-permute-start(bf16[256,2560]{1,0:T(8,128)(2,1)S(1)} %get-tuple-element.65.refs_0_), channel_id=1, source_target_pairs={{0,1},{1,0},{2,3},{3,2},{4,5},{5,4},{6,7},{7,6},{8,9},{9,8},{10,11... | collective-permute-start | bytes 3932168 | tf_op jit(solution)/shard_map/ppermute | solution.py:518
  35.9 8.1 %collective-permute-start.6 = (bf16[64,1280]{1,0:T(8,128)(2,1)S(1)}, bf16[64,1280]{1,0:T(8,128)(2,1)S(1)}, u32[]{:S(2)}, u32[]{:S(2)}) collective-permute-start(bf16[64,1280]{1,0:T(8,128)(2,1)S(1)} %get-tuple-element.64.refs_7_), channel_id=1, source_target_pairs={{0,4},{4,0},{8,12},{12,8},{16,20},{20,16},{24,28},{28,24},{1,5},{5... | collective-permute-start | bytes 491528 | tf_op jit(solution)/shard_map/ppermute | solution.py:518
  43.2 8.1 %collective-permute-start.8 = (bf16[64,1280]{1,0:T(8,128)(2,1)S(1)}, bf16[64,1280]{1,0:T(8,128)(2,1)S(1)}, u32[]{:S(2)}, u32[]{:S(2)}) collective-permute-start(bf16[64,1280]{1,0:T(8,128)(2,1)S(1)} %get-tuple-element.71.rest_0_), channel_id=1, source_target_pairs={{0,4},{4,0},{8,12},{12,8},{16,20},{20,16},{24,28},{28,24},{1,5},{5... | collective-permute-start | bytes 491528 | tf_op jit(solution)/shard_map/ppermute | solution.py:518
  45.9 2.2 %collective-permute-start.9 = (bf16[256,1280]{1,0:T(8,128)(2,1)S(1)}, bf16[256,1280]{1,0:T(8,128)(2,1)S(1)}, u32[]{:S(2)}, u32[]{:S(2)}) collective-permute-start(bf16[256,1280]{1,0:T(8,128)(2,1)S(1)} %get-tuple-element.73.rest_0_), channel_id=1, source_target_pairs={{0,1},{1,0},{2,3},{3,2},{4,5},{5,4},{6,7},{7,6},{8,9},{9,8},{10,11... | collective-permute-start | bytes 1966088 | tf_op jit(solution)/shard_map/ppermute | solution.py:518
  49.9 31.0 %collective-permute-start.11 = (bf16[256,2560]{1,0:T(8,128)(2,1)S(1)}, bf16[256,2560]{1,0:T(8,128)(2,1)S(1)}, u32[]{:S(2)}, u32[]{:S(2)}) collective-permute-start(bf16[256,2560]{1,0:T(8,128)(2,1)S(1)} %project.5._), channel_id=1, source_target_pairs={{0,2},{1,3},{2,0},{3,1},{4,6},{5,7},{6,4},{7,5},{8,10},{9,11},{10,... | collective-permute-start | bytes 3932168 | tf_op jit(solution)/shard_map/ppermute | solution.py:523
  51.9 14.6 %collective-permute-start.12 = (bf16[80,1280]{1,0:T(8,128)(2,1)S(1)}, bf16[80,1280]{1,0:T(8,128)(2,1)S(1)}, u32[]{:S(2)}, u32[]{:S(2)}) collective-permute-start(bf16[80,1280]{1,0:T(8,128)(2,1)S(1)} %get-tuple-element.76.rest_0_), channel_id=1, source_target_pairs={{8,0},{12,4},{16,8},{20,12},{24,16},{28,20},{9,1},{13,5},{17,9},{2... | collective-permute-start | bytes 614408 | tf_op jit(solution)/shard_map/ppermute | solution.py:514
  53.4 17.1 %collective-permute-start.13 = (bf16[80,1280]{1,0:T(8,128)(2,1)S(1)}, bf16[80,1280]{1,0:T(8,128)(2,1)S(1)}, u32[]{:S(2)}, u32[]{:S(2)}) collective-permute-start(bf16[80,1280]{1,0:T(8,128)(2,1)S(1)} %get-tuple-element.76.rest_0_), channel_id=1, source_target_pairs={{0,16},{4,20},{8,24},{12,28},{16,0},{20,4},{24,8},{28,12},{1,17},{... | collective-permute-start | bytes 614408 | tf_op jit(solution)/shard_map/ppermute | solution.py:523
  59.1 2.2 %collective-permute-start.10 = (bf16[256,1280]{1,0:T(8,128)(2,1)S(1)}, bf16[256,1280]{1,0:T(8,128)(2,1)S(1)}, u32[]{:S(2)}, u32[]{:S(2)}) collective-permute-start(bf16[256,1280]{1,0:T(8,128)(2,1)S(1)} %get-tuple-element.77.rest_0_), channel_id=1, source_target_pairs={{0,1},{1,0},{2,3},{3,2},{4,5},{5,4},{6,7},{7,6},{8,9},{9,8},{10,11... | collective-permute-start | bytes 1966088 | tf_op jit(solution)/shard_map/ppermute | solution.py:518
  71.3 5.4 %collective-permute-start.14 = (bf16[64,1280]{1,0:T(8,128)(2,1)S(1)}, bf16[64,1280]{1,0:T(8,128)(2,1)S(1)}, u32[]{:S(2)}, u32[]{:S(2)}) collective-permute-start(bf16[64,1280]{1,0:T(8,128)(2,1)S(1)} %get-tuple-element.85), channel_id=1, source_target_pairs={{0,4},{4,0},{8,12},{12,8},{16,20},{20,16},{24,28},{28,24},{1,5},{5... | collective-permute-start | bytes 491528 | tf_op jit(solution)/shard_map/ppermute | solution.py:518

commit v6 on v4

--- a/solution.py
+++ b/solution.py
@@ -646,9 +646,9 @@
     pair_at, pairs = lax.axis_index("seq") // 2, lax.axis_size("seq") // 2
     places = jnp.stack([side] + numbers + [pair_at >= 2, pair_at + 2 < pairs]).astype(jnp.int32)
 
-    remote = [rotated(grad_out, "head", 2 * d) for d in range(1, chips)]
     sibling = swapped(grad_out, "head")
     mate_weight = swapped(out_weight, "head")
+    remote = [rotated(grad_out, "head", 2 * d) for d in range(1, chips)]
 
     spread = (
         jnp.arange(LANES)[:, None] == (jnp.arange(inner) // width)[None, :]

time: 82.6 us -> 82.6 us (level)
  no operation moved by 1% of the time
where the time goes in v6:
time: 82.6 us; the launch traced here: 82.4 us
  Pallas kernels  49.7 us (60%)
  starting transfers between devices  21.8 us (26%)
  waiting for transfers between devices  9.47 us (11%)
  between operations  1.07 us (1%)
    pallas_call x19, Pallas kernels, call(): pl.pallas_call(kernel, in_specs=in_specs, out_specs=[VM if o.memory_space...  49.7 us
    ppermute x4, starting transfers between devices, rotated(): lax.ppermute(block, axis, [(i, (i + distance) % size) for i in range(size)])  10.6 us
    ppermute x9, starting transfers between devices, swapped(): lax.ppermute(block, axis, [(i, i ^ 1) for i in range(lax.axis_size(axis))])  6.16 us
    ppermute x4, waiting for transfers between devices, rotated(): lax.ppermute(block, axis, [(i, (i + distance) % size) for i in range(size)])  5.21 us
    ppermute x2, starting transfers between devices, shifted(): return lax.ppermute(block, axis, route)  5.01 us
    ppermute x9, waiting for transfers between devices, swapped(): lax.ppermute(block, axis, [(i, i ^ 1) for i in range(lax.axis_size(axis))])  4.26 us
  transfers between devices with their start and end apart: 15, of which 5 were waited for; matrix products, arithmetic and copies ran while one was open for 0% of the time, Pallas kernels for 57%

profile of v6, /device:TPU:0, one launch (start us, length us, event | category | flops | bytes accessed | tf_op | source)
XLA Modules:
  0.0 82.4 jit_solution(1301572306630037163)
XLA Ops:
  1.2 2.9 %collective-permute-start.5 = (bf16[256,2560]{1,0:T(8,128)(2,1)}, bf16[256,2560]{1,0:T(8,128)(2,1)}, u32[]{:S(2)}, u32[]{:S(2)}) collective-permute-start(bf16[256,2560]{1,0:T(8,128)(2,1)} %rest_2_.1), channel_id=1, source_target_pairs={{0,2},{1,3},{2,0},{3,1},{4,6},{5,7},{6,4},{7,5},{8,10},{9,11},{10,... | collective-permute-start | bytes 3932168 | tf_op jit(solution)/shard_map/ppermute | solution.py:526
  4.3 4.3 %local_states.1 = (f32[4,24,256]{2,1,0:T(8,128)S(1)}, bf16[1024,128]{1,0:T(8,128)(2,1)S(1)}, bf16[1024,128]{1,0:T(8,128)(2,1)S(1)}, bf16[4,128,1280]{2,1,0:T(8,1...) custom-call(s32[9]{0:T(128)S(1)} %stack.47.places, ...), custom_call_target="tpu_custom_call" | custom-call | flops 1 | bytes 1 | tf_op jit(solution)/shard_map/local_states/pallas_call | solution.py:38
  8.6 1.6 %collective-permute-start = (bf16[80,1280]{1,0:T(8,128)(2,1)S(1)}, bf16[80,1280]{1,0:T(8,128)(2,1)S(1)}, u32[]{:S(2)}, u32[]{:S(2)}) collective-permute-start(bf16[80,1280]{1,0:T(8,128)(2,1)S(1)} %get-tuple-element.47._), channel_id=1, source_target_pairs={{0,4},{4,0},{8,12},{12,8},{16,20},{20,16},{24,28},{28,24},{1,5},{5... | collective-permute-start | bytes 614408 | tf_op jit(solution)/shard_map/ppermute | solution.py:521
  10.4 7.0 %inside_forward.1 = (bf16[1024,1280]{1,0:T(8,128)(2,1)S(1)}, bf16[1024,1280]{1,0:T(8,128)(2,1)S(1)}, bf16[1280,2560]{1,0:T(8,128)(2,1)S(1)}, bf16[256,2560]{1,0:T(8,128)(2,1)S(1)}) custom-call(s32[9]{0:T(128)S(1)} %stack.47.places, bf16[1024,1280]{1,0:T(8,128)(2,1)} %x_ref.1, bf16[1024,128]{1,0:T(8,128)(2,1)S(1)} %get-tuple-element.44.b_ref, ...), custom_call_target="tpu_custom_call" | custom-call | flops 1 | bytes 1 | tf_op jit(solution)/shard_map/inside_forward/pallas_call | solution.py:38
  18.1 3.5 %collective-permute-start.1 = (bf16[80,1280]{1,0:T(8,128)(2,1)S(1)}, bf16[80,1280]{1,0:T(8,128)(2,1)S(1)}, u32[]{:S(2)}, u32[]{:S(2)}) collective-permute-start(bf16[80,1280]{1,0:T(8,128)(2,1)S(1)} %get-tuple-element.56.refs_8_), channel_id=1, source_target_pairs={{0,8},{4,12},{8,16},{12,20},{16,24},{20,28},{1,9},{5,13},{9,17},{1... | collective-permute-start | bytes 614408 | tf_op jit(solution)/shard_map/ppermute | solution.py:517
  21.6 2.6 %collective-permute-start.2 = (bf16[80,1280]{1,0:T(8,128)(2,1)S(1)}, bf16[80,1280]{1,0:T(8,128)(2,1)S(1)}, u32[]{:S(2)}, u32[]{:S(2)}) collective-permute-start(bf16[80,1280]{1,0:T(8,128)(2,1)S(1)} %get-tuple-element.56.refs_8_), channel_id=1, source_target_pairs={{0,16},{4,20},{8,24},{12,28},{16,0},{20,4},{24,8},{28,12},{1,17},{... | collective-permute-start | bytes 614408 | tf_op jit(solution)/shard_map/ppermute | solution.py:526
  24.3 6.1 %grad_chunks.3 = (bf16[1024,1280]{1,0:T(8,128)(2,1)S(1)}, bf16[4,128,1280]{2,1,0:T(8,128)(2,1)S(1)}, f32[128,1280]{1,0:T(8,128)S(1)}) custom-call(s32[9]{0:T(128)S(1)} %stack.47.places, bf16[256,2560]{1,0:T(8,128)(2,1)S(1)} %get-tuple-element.57.refs_0_, bf16[256,2560]{1,0:T(8,128)(2,1)} %collective-permute-done.3.refs_1_, ...), custom_call_target="tpu_custom_call" | custom-call | flops 1 | bytes 1 | tf_op jit(solution)/shard_map/grad_chunks/pallas_call | solution.py:38
  30.4 3.6 %inside_backward.2 = (bf16[1024,1280]{1,0:T(8,128)(2,1)S(1)}, bf16[1280,2560]{1,0:T(8,128)(2,1)S(1)}) custom-call(s32[9]{0:T(128)S(1)} %stack.47.places, bf16[1024,1280]{1,0:T(8,128)(2,1)S(1)} %get-tuple-element.60.x_ref.refs_9_, bf16[1024,128]{1,0:T(8,128)(2,1)S(1)} %get-tuple-element.44.b_ref, ...), custom_call_target="tpu_custom_call" | custom-call | flops 1 | bytes 1 | tf_op jit(solution)/shard_map/inside_backward/pallas_call | solution.py:38
  34.0 1.8 %enter.1 = (bf16[64,1280]{1,0:T(8,128)(2,1)S(1)}, bf16[64,1280]{1,0:T(8,128)(2,1)S(1)}, f32[8,1280]{1,0:T(8,128)S(1)}, bf16[256,2560]{1,0:T(8,128)(2,1)S(1)}) custom-call(s32[9]{0:T(128)S(1)} %stack.47.places, bf16[64,1280]{1,0:T(8,128)(2,1)S(1)} %get-tuple-element.54.near_ref, f32[8,1280]{1,0:T(8,128)S(1)} %get-tuple-element.55.facts_ref, ...), custom_call_target="tpu_custom_call" | custom-call | flops 1 | bytes 1 | tf_op jit(solution)/shard_map/enter/pallas_call | solution.py:38
  37.3 2.9 %grad_chunks.4 = (bf16[1024,1280]{1,0:T(8,128)(2,1)S(1)}, bf16[4,128,1280]{2,1,0:T(8,128)(2,1)S(1)}, f32[128,1280]{1,0:T(8,128)S(1)}) custom-call(s32[9]{0:T(128)S(1)} %stack.47.places, bf16[256,2560]{1,0:T(8,128)(2,1)S(1)} %get-tuple-element.65.refs_0_, ...), custom_call_target="tpu_custom_call", output_to_operand_aliasing={{0}: (10, {}), {1}: (11, {})} | custom-call | flops 1 | bytes 1 | tf_op jit(solution)/shard_map/grad_chunks/pallas_call | solution.py:38
  40.2 2.9 %grad_chunks.5 = (bf16[1024,1280]{1,0:T(8,128)(2,1)S(1)}, bf16[4,128,1280]{2,1,0:T(8,128)(2,1)S(1)}, bf16[64,1280]{1,0:T(8,128)(2,1)S(1)}, bf16[64,1280]{1,0:T(8,128)(2,1)S(1)}) custom-call(s32[9]{0:T(128)S(1)} %stack.47.places, bf16[256,2560]{1,0:T(8,128)(2,1)S(1)} %collective-permute-done.7.refs_0_, ...), custom_call_target="tpu_custom_call", output_to_operand_aliasing={{0}: (10, {}), {1}: (11, {})} | custom-call | flops 1 | bytes 1 | tf_op jit(solution)/shard_map/grad_chunks/pallas_call | solution.py:38
  44.0 1.9 %gated_chunks.2 = (bf16[256,1280]{1,0:T(8,128)(2,1)S(1)}, bf16[256,1280]{1,0:T(8,128)(2,1)S(1)}) custom-call(s32[9]{0:T(128)S(1)} %stack.47.places, bf16[1024,1280]{1,0:T(8,128)(2,1)S(1)} %get-tuple-element.48._.mixed_ref, bf16[1024,1280]{1,0:T(8,128)(2,1)S(1)} %get-tuple-element.49.refs_2_.refs_1_.gates_ref, ...), custom_call_target="tpu_custom_call" | custom-call | flops 1 | bytes 1 | tf_op jit(solution)/shard_map/gated_chunks/pallas_call | solution.py:38
  45.9 1.8 %project.4.rest_0_ = f32[256,2560]{1,0:T(8,128)S(1)} custom-call(bf16[256,1280]{1,0:T(8,128)(2,1)S(1)} %get-tuple-element.75.gated_ref, bf16[1280,2560]{1,0:T(8,128)(2,1)S(1)} %get-tuple-element.59.refs_7_.refs_6_.w_ref, bf16[256,1280]{1,0:T(8,128)(2,1)S(1)} %get-tuple-element.73.rest_0_), custom_call_target="tpu_custom_call" | custom-call | flops 23060000768 | bytes 1 | tf_op jit(solution)/shard_map/project/pallas_call | solution.py:38
  48.0 1.9 %project.5._ = bf16[256,2560]{1,0:T(8,128)(2,1)S(1)} custom-call(bf16[256,1280]{1,0:T(8,128)(2,1)S(1)} %collective-permute-done.9.gated_ref, bf16[1280,2560]{1,0:T(8,128)(2,1)S(1)} %get-tuple-element.74.w_ref, f32[256,2560]{1,0:T(8,128)S(1)} %project.4.rest_0_), custom_call_target="tpu_custom_call" | custom-call | flops 1 | bytes 1 | tf_op jit(solution)/shard_map/project/pallas_call | solution.py:38
  51.9 1.5 %collective-permute-start.12 = (bf16[80,1280]{1,0:T(8,128)(2,1)S(1)}, bf16[80,1280]{1,0:T(8,128)(2,1)S(1)}, u32[]{:S(2)}, u32[]{:S(2)}) collective-permute-start(bf16[80,1280]{1,0:T(8,128)(2,1)S(1)} %get-tuple-element.76.rest_0_), channel_id=1, source_target_pairs={{8,0},{12,4},{16,8},{20,12},{24,16},{28,20},{9,1},{13,5},{17,9},{2... | collective-permute-start | bytes 614408 | tf_op jit(solution)/shard_map/ppermute | solution.py:517
  53.4 3.7 %collective-permute-start.13 = (bf16[80,1280]{1,0:T(8,128)(2,1)S(1)}, bf16[80,1280]{1,0:T(8,128)(2,1)S(1)}, u32[]{:S(2)}, u32[]{:S(2)}) collective-permute-start(bf16[80,1280]{1,0:T(8,128)(2,1)S(1)} %get-tuple-element.76.rest_0_), channel_id=1, source_target_pairs={{0,16},{4,20},{8,24},{12,28},{16,0},{20,4},{24,8},{28,12},{1,17},{... | collective-permute-start | bytes 614408 | tf_op jit(solution)/shard_map/ppermute | solution.py:526
  57.2 1.9 %gated_chunks.3 = (bf16[256,1280]{1,0:T(8,128)(2,1)S(1)}, bf16[256,1280]{1,0:T(8,128)(2,1)S(1)}) custom-call(s32[9]{0:T(128)S(1)} %stack.47.places, bf16[1024,1280]{1,0:T(8,128)(2,1)S(1)} %get-tuple-element.48._.mixed_ref, bf16[1024,1280]{1,0:T(8,128)(2,1)S(1)} %get-tuple-element.49.refs_2_.refs_1_.gates_ref, ...), custom_call_target="tpu_custom_call" | custom-call | flops 1 | bytes 1 | tf_op jit(solution)/shard_map/gated_chunks/pallas_call | solution.py:38
  59.1 1.8 %project.6.rest_0_ = f32[256,2560]{1,0:T(8,128)S(1)} custom-call(bf16[256,1280]{1,0:T(8,128)(2,1)S(1)} %get-tuple-element.78.gated_ref, bf16[1280,2560]{1,0:T(8,128)(2,1)S(1)} %get-tuple-element.59.refs_7_.refs_6_.w_ref, bf16[256,1280]{1,0:T(8,128)(2,1)S(1)} %get-tuple-element.77.rest_0_), custom_call_target="tpu_custom_call" | custom-call | flops 9223999488 | bytes 1 | tf_op jit(solution)/shard_map/project/pallas_call | solution.py:38
  61.2 1.9 %project.7.own_ref._ = f32[256,2560]{1,0:T(8,128)S(1)} custom-call(bf16[256,1280]{1,0:T(8,128)(2,1)S(1)} %collective-permute-done.10.gated_ref, bf16[1280,2560]{1,0:T(8,128)(2,1)S(1)} %get-tuple-element.74.w_ref, f32[256,2560]{1,0:T(8,128)S(1)} %project.6.rest_0_), custom_call_target="tpu_custom_call" | custom-call | flops 1 | bytes 1 | tf_op jit(solution)/shard_map/project/pallas_call | solution.py:38
  63.1 3.4 %inside_backward.3._.part_ref = bf16[1024,1280]{1,0:T(8,128)(2,1)S(1)} custom-call(s32[9]{0:T(128)S(1)} %stack.47.places, bf16[1024,1280]{1,0:T(8,128)(2,1)S(1)} %get-tuple-element.79.x_ref, bf16[1024,128]{1,0:T(8,128)(2,1)S(1)} %get-tuple-element.44.b_ref, ...), custom_call_target="tpu_custom_call", output_to_operand_aliasing={{}: (7, {})} | custom-call | flops 1 | bytes 1 | tf_op jit(solution)/shard_map/inside_backward/pallas_call | solution.py:38
  66.5 4.1 %collective-permute-done.13.two_ref = bf16[80,1280]{1,0:T(8,128)(2,1)S(1)} collective-permute-done((bf16[80,1280]{1,0:T(8,128)(2,1)S(1)}, bf16[80,1280]{1,0:T(8,128)(2,1)S(1)}, u32[]{:S(2)}, u32[]{:S(2)}) %collective-permute-start.13) | collective-permute-done | bytes 204832 | tf_op jit(solution)/shard_map/ppermute | solution.py:526
  71.3 1.6 %collective-permute-start.14 = (bf16[64,1280]{1,0:T(8,128)(2,1)S(1)}, bf16[64,1280]{1,0:T(8,128)(2,1)S(1)}, u32[]{:S(2)}, u32[]{:S(2)}) collective-permute-start(bf16[64,1280]{1,0:T(8,128)(2,1)S(1)} %get-tuple-element.85), channel_id=1, source_target_pairs={{0,4},{4,0},{8,12},{12,8},{16,20},{20,16},{24,28},{28,24},{1,5},{5... | collective-permute-start | bytes 491528 | tf_op jit(solution)/shard_map/ppermute | solution.py:521
  72.9 3.8 %collective-permute-done.14.other_ref = bf16[64,1280]{1,0:T(8,128)(2,1)S(1)} collective-permute-done((bf16[64,1280]{1,0:T(8,128)(2,1)S(1)}, bf16[64,1280]{1,0:T(8,128)(2,1)S(1)}, u32[]{:S(2)}, u32[]{:S(2)}) %collective-permute-start.14) | collective-permute-done | bytes 163872 | tf_op jit(solution)/shard_map/ppermute | solution.py:521
  76.7 3.2 %back_tail.1 = bf16[1024,1280]{1,0:T(8,128)(2,1)} custom-call(s32[9]{0:T(128)S(1)} %stack.47.places, bf16[1024,1280]{1,0:T(8,128)(2,1)S(1)} %inside_backward.3._.part_ref, bf16[1024,128]{1,0:T(8,128)(2,1)S(1)} %get-tuple-element.44.b_ref, bf16[1024,128]{1,0:T(8,128)(2,1)S(1)} %get-tuple-element.80.exit_ref, ...), custom_call_target="tpu_custom_call" | custom-call | flops 1730000000 | bytes 1 | tf_op jit(solution)/shard_map/back_tail/pallas_call | solution.py:38
  (33 shorter events, 9.6 us)
Async XLA Ops:
  0.6 9.6 %copy-start = (f32[20]{0:T(128)S(1)}, f32[20]{0:T(128)}, u32[]{:S(2)}) copy-start(f32[20]{0:T(128)} %param.14) | copy-start | bytes 244
  0.6 29.7 %collective-permute-start.4 = (bf16[1280,2560]{1,0:T(8,128)(2,1)}, bf16[1280,2560]{1,0:T(8,128)(2,1)}, u32[]{:S(2)}, u32[]{:S(2)}) collective-permute-start(bf16[1280,2560]{1,0:T(8,128)(2,1)} %rest_1_.1), channel_id=1, source_target_pairs={{0,1},{1,0},{2,3},{3,2},{4,5},{5,4},{6,7},{7,6},{8,9},{9,8},{10,11... | collective-permute-start | bytes 19660808 | tf_op jit(solution)/shard_map/ppermute | solution.py:521
  1.2 23.1 %collective-permute-start.3 = (bf16[256,2560]{1,0:T(8,128)(2,1)}, bf16[256,2560]{1,0:T(8,128)(2,1)}, u32[]{:S(2)}, u32[]{:S(2)}) collective-permute-start(bf16[256,2560]{1,0:T(8,128)(2,1)} %rest_2_.1), channel_id=1, source_target_pairs={{0,1},{1,0},{2,3},{3,2},{4,5},{5,4},{6,7},{7,6},{8,9},{9,8},{10,11... | collective-permute-start | bytes 3932168 | tf_op jit(solution)/shard_map/ppermute | solution.py:521
  1.2 32.7 %collective-permute-start.5 = (bf16[256,2560]{1,0:T(8,128)(2,1)}, bf16[256,2560]{1,0:T(8,128)(2,1)}, u32[]{:S(2)}, u32[]{:S(2)}) collective-permute-start(bf16[256,2560]{1,0:T(8,128)(2,1)} %rest_2_.1), channel_id=1, source_target_pairs={{0,2},{1,3},{2,0},{3,1},{4,6},{5,7},{6,4},{7,5},{8,10},{9,11},{10,... | collective-permute-start | bytes 3932168 | tf_op jit(solution)/shard_map/ppermute | solution.py:526
  8.6 8.8 %collective-permute-start = (bf16[80,1280]{1,0:T(8,128)(2,1)S(1)}, bf16[80,1280]{1,0:T(8,128)(2,1)S(1)}, u32[]{:S(2)}, u32[]{:S(2)}) collective-permute-start(bf16[80,1280]{1,0:T(8,128)(2,1)S(1)} %get-tuple-element.47._), channel_id=1, source_target_pairs={{0,4},{4,0},{8,12},{12,8},{16,20},{20,16},{24,28},{28,24},{1,5},{5... | collective-permute-start | bytes 614408 | tf_op jit(solution)/shard_map/ppermute | solution.py:521
  18.1 15.8 %collective-permute-start.1 = (bf16[80,1280]{1,0:T(8,128)(2,1)S(1)}, bf16[80,1280]{1,0:T(8,128)(2,1)S(1)}, u32[]{:S(2)}, u32[]{:S(2)}) collective-permute-start(bf16[80,1280]{1,0:T(8,128)(2,1)S(1)} %get-tuple-element.56.refs_8_), channel_id=1, source_target_pairs={{0,8},{4,12},{8,16},{12,20},{16,24},{20,28},{1,9},{5,13},{9,17},{1... | collective-permute-start | bytes 614408 | tf_op jit(solution)/shard_map/ppermute | solution.py:517
  21.6 12.3 %collective-permute-start.2 = (bf16[80,1280]{1,0:T(8,128)(2,1)S(1)}, bf16[80,1280]{1,0:T(8,128)(2,1)S(1)}, u32[]{:S(2)}, u32[]{:S(2)}) collective-permute-start(bf16[80,1280]{1,0:T(8,128)(2,1)S(1)} %get-tuple-element.56.refs_8_), channel_id=1, source_target_pairs={{0,16},{4,20},{8,24},{12,28},{16,0},{20,4},{24,8},{28,12},{1,17},{... | collective-permute-start | bytes 614408 | tf_op jit(solution)/shard_map/ppermute | solution.py:526
  35.8 4.4 %collective-permute-start.7 = (bf16[256,2560]{1,0:T(8,128)(2,1)S(1)}, bf16[256,2560]{1,0:T(8,128)(2,1)S(1)}, u32[]{:S(2)}, u32[]{:S(2)}) collective-permute-start(bf16[256,2560]{1,0:T(8,128)(2,1)S(1)} %get-tuple-element.65.refs_0_), channel_id=1, source_target_pairs={{0,1},{1,0},{2,3},{3,2},{4,5},{5,4},{6,7},{7,6},{8,9},{9,8},{10,11... | collective-permute-start | bytes 3932168 | tf_op jit(solution)/shard_map/ppermute | solution.py:521
  35.9 8.1 %collective-permute-start.6 = (bf16[64,1280]{1,0:T(8,128)(2,1)S(1)}, bf16[64,1280]{1,0:T(8,128)(2,1)S(1)}, u32[]{:S(2)}, u32[]{:S(2)}) collective-permute-start(bf16[64,1280]{1,0:T(8,128)(2,1)S(1)} %get-tuple-element.64.refs_7_), channel_id=1, source_target_pairs={{0,4},{4,0},{8,12},{12,8},{16,20},{20,16},{24,28},{28,24},{1,5},{5... | collective-permute-start | bytes 491528 | tf_op jit(solution)/shard_map/ppermute | solution.py:521
  43.2 8.1 %collective-permute-start.8 = (bf16[64,1280]{1,0:T(8,128)(2,1)S(1)}, bf16[64,1280]{1,0:T(8,128)(2,1)S(1)}, u32[]{:S(2)}, u32[]{:S(2)}) collective-permute-start(bf16[64,1280]{1,0:T(8,128)(2,1)S(1)} %get-tuple-element.71.rest_0_), channel_id=1, source_target_pairs={{0,4},{4,0},{8,12},{12,8},{16,20},{20,16},{24,28},{28,24},{1,5},{5... | collective-permute-start | bytes 491528 | tf_op jit(solution)/shard_map/ppermute | solution.py:521
  45.9 2.2 %collective-permute-start.9 = (bf16[256,1280]{1,0:T(8,128)(2,1)S(1)}, bf16[256,1280]{1,0:T(8,128)(2,1)S(1)}, u32[]{:S(2)}, u32[]{:S(2)}) collective-permute-start(bf16[256,1280]{1,0:T(8,128)(2,1)S(1)} %get-tuple-element.73.rest_0_), channel_id=1, source_target_pairs={{0,1},{1,0},{2,3},{3,2},{4,5},{5,4},{6,7},{7,6},{8,9},{9,8},{10,11... | collective-permute-start | bytes 1966088 | tf_op jit(solution)/shard_map/ppermute | solution.py:521
  49.9 31.0 %collective-permute-start.11 = (bf16[256,2560]{1,0:T(8,128)(2,1)S(1)}, bf16[256,2560]{1,0:T(8,128)(2,1)S(1)}, u32[]{:S(2)}, u32[]{:S(2)}) collective-permute-start(bf16[256,2560]{1,0:T(8,128)(2,1)S(1)} %project.5._), channel_id=1, source_target_pairs={{0,2},{1,3},{2,0},{3,1},{4,6},{5,7},{6,4},{7,5},{8,10},{9,11},{10,... | collective-permute-start | bytes 3932168 | tf_op jit(solution)/shard_map/ppermute | solution.py:526
  51.9 14.6 %collective-permute-start.12 = (bf16[80,1280]{1,0:T(8,128)(2,1)S(1)}, bf16[80,1280]{1,0:T(8,128)(2,1)S(1)}, u32[]{:S(2)}, u32[]{:S(2)}) collective-permute-start(bf16[80,1280]{1,0:T(8,128)(2,1)S(1)} %get-tuple-element.76.rest_0_), channel_id=1, source_target_pairs={{8,0},{12,4},{16,8},{20,12},{24,16},{28,20},{9,1},{13,5},{17,9},{2... | collective-permute-start | bytes 614408 | tf_op jit(solution)/shard_map/ppermute | solution.py:517
  53.4 17.1 %collective-permute-start.13 = (bf16[80,1280]{1,0:T(8,128)(2,1)S(1)}, bf16[80,1280]{1,0:T(8,128)(2,1)S(1)}, u32[]{:S(2)}, u32[]{:S(2)}) collective-permute-start(bf16[80,1280]{1,0:T(8,128)(2,1)S(1)} %get-tuple-element.76.rest_0_), channel_id=1, source_target_pairs={{0,16},{4,20},{8,24},{12,28},{16,0},{20,4},{24,8},{28,12},{1,17},{... | collective-permute-start | bytes 614408 | tf_op jit(solution)/shard_map/ppermute | solution.py:526
  59.1 2.2 %collective-permute-start.10 = (bf16[256,1280]{1,0:T(8,128)(2,1)S(1)}, bf16[256,1280]{1,0:T(8,128)(2,1)S(1)}, u32[]{:S(2)}, u32[]{:S(2)}) collective-permute-start(bf16[256,1280]{1,0:T(8,128)(2,1)S(1)} %get-tuple-element.77.rest_0_), channel_id=1, source_target_pairs={{0,1},{1,0},{2,3},{3,2},{4,5},{5,4},{6,7},{7,6},{8,9},{9,8},{10,11... | collective-permute-start | bytes 1966088 | tf_op jit(solution)/shard_map/ppermute | solution.py:521
  71.3 5.4 %collective-permute-start.14 = (bf16[64,1280]{1,0:T(8,128)(2,1)S(1)}, bf16[64,1280]{1,0:T(8,128)(2,1)S(1)}, u32[]{:S(2)}, u32[]{:S(2)}) collective-permute-start(bf16[64,1280]{1,0:T(8,128)(2,1)S(1)} %get-tuple-element.85), channel_id=1, source_target_pairs={{0,4},{4,0},{8,12},{12,8},{16,20},{20,16},{24,28},{28,24},{1,5},{5... | collective-permute-start | bytes 491528 | tf_op jit(solution)/shard_map/ppermute | solution.py:521
